TPU v7x, 32 devices: a whole 2x2x4 slice. The times are simulated.
32 devices in a mesh: ens: 2 (over x), lon: 16 (over z, y, core).
Axes of the slice: x: 2, y: 2, z: 4, core: 2. Of those that a mesh axis runs over, the one named last changes fastest.
Arguments:
- tracers: float32 [2, 50, 32, 2048], P(None, 'ens', None, 'lon'), parts along dimension 1, may hold values from -6 to 6
- east_flow: float32 [50, 32, 2048], P('ens', None, 'lon'), parts along dimension 0, may hold values from -0.3 to 0.3
- north_flow: float32 [50, 32, 2048], P('ens', None, 'lon'), parts along dimension 0, may hold values from -0.3 to 0.3
- mixing: float32 [48, 32, 2048], P('ens', None, 'lon'), parts along dimension 0, may hold values from 0.05 to 5
- depth_levels: int32 [32, 2048], P(None, 'lon'), may hold values from 0 to 25
- atm_flux: float32 [4, 128, 128], P('ens', 'lon'), parts along dimension 0, may hold values from -6 to 6
- source_blocks: int32 [16, 16, 2], P('lon'), may hold values from 0 to 7
- target_rows: int32 [16, 16, 2], P(None, 'lon'), may hold values from 0 to 31
- regrid_weights: float32 [16, 16, 2, 128, 128], P('lon'), may hold values from -0.5 to 0.5
Outputs:
- tracers_out: float32 [2, 50, 32, 2048], P(None, 'ens', None, 'lon'), parts along dimension 1
There are 2 independent parts, one for each index of `ens`. A program takes and returns all parts, laid end to end along the dimension named above; an argument that names none is the same for every part. Nothing has to cross between parts.
All inputs are finite; a program needn't handle non-finite values.
Results may differ from a plain program's by a relative error of at most 0.0001.
Values sent between devices are 32-bit elements; how exact they have to be, the bound alone decides.
No kernel may reach another device: no remote copies, remote signals or barrier semaphores. Data moves between devices by JAX's collectives and lax.ppermute only.
A program may use at most 64 MiB of HBM per device.

v0:
```python
import jax
import jax.numpy as jnp
from jax import lax
from jax.sharding import PartitionSpec as P

SUB = 4


DIFFUSION = 0.12
FLUX_GAIN = 0.5


def partner(value, axis, stride):
    return lax.ppermute(value, axis, [(i, i ^ 1 << stride) for i in range(lax.axis_size(axis))])


def padded(block, sides, width):
    for axis, dim in sides:
        count = lax.axis_size(axis)
        forward = [(i, i + 1) for i in range(count - 1)]
        forward.append((count - 1, 0))
        backward = [(target, source) for source, target in forward]
        low = lax.ppermute(
            lax.slice_in_dim(block, block.shape[dim] - width, None, axis=dim), axis, forward
        )
        high = lax.ppermute(lax.slice_in_dim(block, 0, width, axis=dim), axis, backward)
        block = jnp.concatenate([low, block, high], axis=dim)
    return block


def face_flux(velocity, inside, beyond, wet_inside, wet_beyond):
    return (
        wet_inside
        * wet_beyond
        * (velocity * (0.5 * (inside + beyond)) - DIFFUSION * (beyond - inside))
    )


def solve_columns(rhs, links):
    depth = rhs.shape[1]
    nothing = jnp.zeros_like(links[0])
    above = [nothing] + [links[level] for level in range(depth - 1)]
    below = [links[level] for level in range(depth - 1)] + [nothing]
    ratios = []
    partial_value = []
    for level in range(depth):
        if level == 0:
            pivot_value = 1.0 + above[level] + below[level]
            ratios.append(-below[level] / pivot_value)
            partial_value.append(rhs[:, level] / pivot_value)
        else:
            pivot_value = 1.0 + above[level] + below[level] + above[level] * ratios[level - 1]
            ratios.append(-below[level] / pivot_value)
            partial_value.append(
                (rhs[:, level] + above[level] * partial_value[level - 1]) / pivot_value
            )
    levels_out = [None] * depth
    levels_out[depth - 1] = partial_value[depth - 1]
    for level in range(depth - 2, -1, -1):
        levels_out[level] = partial_value[level] - ratios[level] * levels_out[level + 1]
    return jnp.stack(levels_out, axis=1)


def partner_block(piece):
    bit_count = lax.axis_size("lon").bit_length() - 1
    bit_order = list(range(bit_count))
    moved = piece
    for bit_number in bit_order:
        moved = partner(moved, "lon", bit_number)
    return moved


def on_device(
    tracers,
    east_flow,
    north_flow,
    mixing,
    depth_levels,
    atm_flux,
    source_blocks,
    target_rows,
    regrid_weights,
):
    depth = tracers.shape[1]
    lat_rows = tracers.shape[2]
    levels = jnp.arange(depth, dtype=jnp.int32)[:, None, None]
    wet_mask = (levels < depth_levels[None]).astype(jnp.float32)
    chosen = source_blocks[0]
    block_index = jnp.arange(atm_flux.shape[1], dtype=jnp.int32)
    source_hot = (chosen[:, :, None] == block_index).astype(jnp.float32)
    picked = jnp.einsum("esb,nba->esna", source_hot, atm_flux, precision=lax.Precision.HIGHEST)
    pieces = jnp.einsum(
        "esna,esao->esno", picked, regrid_weights[0], precision=lax.Precision.HIGHEST
    )
    received = lax.all_to_all(pieces, "lon", split_axis=0, concat_axis=0, tiled=True)
    static_parts = jnp.stack([wet_mask, east_flow], axis=0)
    static_wide = padded(static_parts, (("lon", 3),), 1)
    wet_wide = static_wide[0]
    flow_wide = static_wide[1]
    wet_fold = partner_block(wet_mask[None, :, -1, :])[0][..., ::-1]
    north_wet = jnp.concatenate([wet_mask[:, 1:, :], wet_fold[:, None, :]], axis=1)
    tracer = tracers
    for substep in range(SUB):
        tracer_wide = padded(tracer, (("lon", 3),), 1)
        face_all = face_flux(
            flow_wide[..., :-1],
            tracer_wide[..., :-1],
            tracer_wide[..., 1:],
            wet_wide[..., :-1],
            wet_wide[..., 1:],
        )
        east_flux = face_all[..., 1:]
        west_flux = face_all[..., :-1]
        tracer_fold = partner_block(tracer[:, :, -1, :])[..., ::-1]
        north_cells = jnp.concatenate([tracer[:, :, 1:, :], tracer_fold[:, :, None, :]], axis=2)
        north_flux = face_flux(north_flow, tracer, north_cells, wet_mask, north_wet)
        south_flux = jnp.concatenate(
            [jnp.zeros_like(north_flux[:, :, :1]), north_flux[:, :, :-1]], axis=2
        )
        tracer = tracer - (east_flux - west_flux + north_flux - south_flux)
    targets = target_rows[:, 0, :]
    rows_index = jnp.arange(lat_rows, dtype=jnp.int32)
    one_hot = (targets[:, :, None] == rows_index).astype(jnp.float32)
    surface = jnp.einsum("scj,scno->njo", one_hot, received, precision=lax.Precision.HIGHEST)
    rhs = tracer.at[:, 0].add(FLUX_GAIN * surface * wet_mask[0])
    links = mixing * wet_mask[1:]
    return solve_columns(rhs, links)


def solution(mesh):
    return jax.shard_map(
        on_device,
        mesh=mesh,
        in_specs=(
            P(None, "ens", None, "lon"),
            P("ens", None, "lon"),
            P("ens", None, "lon"),
            P("ens", None, "lon"),
            P(None, "lon"),
            P("ens", "lon", None),
            P("lon", None, None),
            P(None, "lon", None),
            P("lon", None, None, None, None),
        ),
        out_specs=P(None, "ens", None, "lon"),
        check_vma=False,
    )
```

profile of v0, /device:TPU:0, one launch (start us, length us, event | category | flops | bytes accessed | tf_op | source)
XLA Modules:
  0.0 164.4 jit_solution(7536638618499926165)
XLA Ops:
  1.7 2.6 %slice_maximum_fusion = (f32[2,25,32,1]{3,2,1,0:T(8,128)}, f32[2,25,32,1]{3,2,1,0:T(8,128)}) fusion(f32[1,25,32,128]{3,2,1,0:T(8,128)} %bitcast.197, f32[1,25,32,128]{3,2,1,0:T(8,128)S(1)} %fusion.19), kind=kLoop, calls=%fused_computation.41 | loop fusion | flops 3200 | bytes 832000 | tf_op jit(solution)/shard_map/stack | solution.py:96
  4.3 2.1 %copy.59 = f32[2,25,32,1]{2,0,3,1:T(2,128)} copy(f32[2,25,32,1]{3,2,1,0:T(8,128)} %get-tuple-element.84) | data formatting | bytes 12800 | tf_op jit(solution)/shard_map/slice | solution.py:24
  6.9 2.1 %copy.60 = f32[2,25,32,1]{2,0,3,1:T(2,128)} copy(f32[2,25,32,1]{3,2,1,0:T(8,128)} %get-tuple-element.85) | data formatting | bytes 12800 | tf_op jit(solution)/shard_map/slice | solution.py:26
  9.0 5.0 %collective-permute-start.1 = (f32[2,25,32,1]{2,0,3,1:T(2,128)}, f32[2,25,32,1]{2,0,3,1:T(2,128)}, u32[]{:S(2)}, u32[]{:S(2)}) collective-permute-start(f32[2,25,32,1]{2,0,3,1:T(2,128)} %copy.60), channel_id=1, source_target_pairs={{1,0},{2,1},{3,2},{4,3},{5,4},{6,5},{7,6},{8,7},{9,8},{10,9},{11,1... | collective-permute-start | bytes 19208 | tf_op jit(solution)/shard_map/ppermute | solution.py:26
  14.0 1.4 fusion.94
  15.4 2.1 %copy.97 = f32[2,25,32,1]{2,0,3,1:T(2,128)} copy(f32[2,25,32,1]{3,2,1,0:T(8,128)} %get-tuple-element.86) | data formatting | bytes 12800
  17.6 2.1 %copy.98 = f32[2,25,32,1]{2,0,3,1:T(2,128)} copy(f32[2,25,32,1]{3,2,1,0:T(8,128)} %get-tuple-element.87) | data formatting | bytes 12800
  19.7 4.4 %collective-permute-start.3 = (f32[2,25,32,1]{2,0,3,1:T(2,128)}, f32[2,25,32,1]{2,0,3,1:T(2,128)}, u32[]{:S(2)}, u32[]{:S(2)}) collective-permute-start(f32[2,25,32,1]{2,0,3,1:T(2,128)} %copy.98), channel_id=1, source_target_pairs={{1,0},{2,1},{3,2},{4,3},{5,4},{6,5},{7,6},{8,7},{9,8},{10,9},{11,1... | collective-permute-start | bytes 19208 | tf_op jit(solution)/shard_map/ppermute | solution.py:26
  25.1 1.9 %fusion = f32[16,2,2,128]{3,2,1,0:T(2,128)S(1)} fusion(f32[1,16,2,128,128]{4,3,2,1,0:T(8,128)S(1)} %copy-done, f32[16,2,2,128]{3,0,2,1:T(8,128)S(1)} %fusion.49), kind=kOutput, calls=%fused_computation | convolution fusion | flops 12582912 | bytes 2162688 | tf_op jit(solution)/shard_map/esna,esao->esno/dot_general | solution.py:92
  27.6 4.2 %all-to-all-start = ((f32[16,2,2,128]{3,1,2,0:T(2,128)}), f32[16,2,2,128]{3,1,2,0:T(2,128)}, u32[]{:S(2)}, u32[]{:S(2)}) async-start(f32[16,2,2,128]{3,1,2,0:T(2,128)} %copy.91), calls=%async_computation | async-start | bytes 65536 | tf_op jit(solution)/shard_map/all_to_all | solution.py:95
  31.7 1.1 slice_multiply_fusion.2
  40.9 2.0 %copy.61 = f32[2,25,32,1]{3,2,1,0:T(8,128)} copy(f32[2,25,32,1]{2,0,3,1:T(2,128)} %collective-permute-done) | data formatting | bytes 12800 | tf_op jit(solution)/shard_map/ppermute | solution.py:23
  42.9 2.0 %copy.62 = f32[2,25,32,1]{3,2,1,0:T(8,128)} copy(f32[2,25,32,1]{2,0,3,1:T(2,128)} %collective-permute-done.1) | data formatting | bytes 12800 | tf_op jit(solution)/shard_map/ppermute | solution.py:26
  44.9 2.2 %pad_maximum_fusion = f32[2,25,32,130]{3,2,1,0:T(8,128)S(1)} fusion(f32[2,25,32,1]{3,2,1,0:T(8,128)} %copy.62, f32[1,25,32,128]{3,2,1,0:T(8,128)} %bitcast.198, f32[1,25,32,128]{3,2,1,0:T(8,128)S(1)} %copy-done.12, f32[2,25,32,1]{3,2,1,0:T(8,128)} %copy.61), kind=kLoop, calls=%fused_computation.2 | loop fusion | flops 624000 | bytes 1664000 | tf_op jit(solution)/shard_map/concatenate | solution.py:27
  47.1 1.6 collective-permute-start.5
  48.9 2.2 %collective-permute-done.5 = f32[1,25,128]{2,0,1:T(1,128)S(1)} collective-permute-done((f32[1,25,128]{2,0,1:T(1,128)}, f32[1,25,128]{2,0,1:T(1,128)S(1)}, u32[]{:S(2)}, u32[]{:S(2)}) %collective-permute-start.5) | collective-permute-done | bytes 12832 | tf_op jit(solution)/shard_map/ppermute | solution.py:14
  51.1 1.5 collective-permute-start.6
  52.7 1.5 collective-permute-start.9
  54.1 1.5 slice_multiply_fusion
  55.6 2.0 %copy.64 = f32[2,25,32,1]{3,2,0,1:T(8,128)} copy(f32[2,25,32,1]{2,0,3,1:T(2,128)} %collective-permute-done.2) | data formatting | bytes 12800 | tf_op jit(solution)/shard_map/ppermute | solution.py:23
  57.7 2.0 %copy.68 = f32[2,25,32,1]{3,2,0,1:T(8,128)} copy(f32[2,25,32,1]{2,0,3,1:T(2,128)} %collective-permute-done.3) | data formatting | bytes 12800 | tf_op jit(solution)/shard_map/ppermute | solution.py:26
  59.7 2.4 %collective-permute-start.7 = (f32[1,25,128]{2,0,1:T(1,128)S(1)}, f32[1,25,128]{2,0,1:T(1,128)S(1)}, u32[]{:S(2)}, u32[]{:S(2)}) collective-permute-start(f32[1,25,128]{2,0,1:T(1,128)S(1)} %collective-permute-done.6), channel_id=1, source_target_pairs={{0,8},{1,9},{2,10},{3,11},{4,12},{5,13},{6,14},{7,15},{8,0},{9,1},... | collective-permute-start | bytes 38408 | tf_op jit(solution)/shard_map/ppermute | solution.py:14
  62.6 3.6 %subtract_multiply_fusion.3 = f32[2,25,32,129]{3,2,0,1:T(8,128)} fusion(f32[2,25,32,1]{3,2,0,1:T(8,128)} %copy.68, f32[2,25,32,1]{3,2,0,1:T(8,128)} %copy.64, f32[25,32,129]{2,1,0:T(8,128)} %get-tuple-element.128, f32[25,32,129]{2,1,0:T(8,128)} %get-tuple-element.129, f32[2,25,32,128]{3,2,1,0:T(8,128)S(1)} %copy-done.3), kind=kLoop, calls=%fused_computation.14 | loop fusion | flops 1651200 | bytes 2483200 | tf_op jit(solution)/shard_map/mul | solution.py:33
  66.9 2.0 %maximum_select_fusion = (f32[25,32,128]{2,1,0:T(8,128)S(1)}, f32[25,32,128]{2,1,0:T(8,128)}) fusion(f32[25,1,128]{2,1,0:T(1,128)S(1)} %copy.69, f32[25,31,128]{2,1,0:T(8,128)} %slice.435, s32[32,128]{1,0:T(8,128)S(1)} %copy-done.13, f32[25,32,128]{2,1,0:T(8,128)} %param.13), kind=kLoop, calls=%fused_computation.50 | loop fusion | flops 409600 | bytes 1654784 | tf_op jit(solution)/shard_map/mul | solution.py:33
  68.9 2.6 %collective-permute-done.11 = f32[2,25,128]{2,0,1:T(2,128)} collective-permute-done((f32[2,25,128]{2,0,1:T(2,128)}, f32[2,25,128]{2,0,1:T(2,128)}, u32[]{:S(2)}, u32[]{:S(2)}) %collective-permute-start.11) | collective-permute-done | bytes 25632 | tf_op jit(solution)/shard_map/ppermute | solution.py:14
  72.4 1.7 %subtract_multiply_fusion.7 = f32[2,25,32,128]{3,2,0,1:T(8,128)S(1)} fusion(f32[2,25,1,128]{3,2,0,1:T(1,128)S(1)} %bitcast.200, f32[2,25,31,128]{3,2,0,1:T(8,128)} %copy.116, f32[25,32,128]{2,1,0:T(8,128)} %get-tuple-element.127, f32[25,32,128]{2,1,0:T(8,128)S(1)} %get-tuple-element.126, f32[2,25,32,128]{3,2,1,0:T(8,128)S(1)} %copy-done.3), kind=kLoop, calls=%fused_computation.49 | loop fusion | flops 1433600 | bytes 3276800 | tf_op jit(solution)/shard_map/mul | solution.py:33
  75.1 1.4 fusion.74
  77.1 1.4 fusion.93
  78.5 2.1 %copy.75 = f32[2,25,32,1]{2,0,3,1:T(2,128)} copy(f32[2,25,32,1]{3,2,0,1:T(8,128)} %get-tuple-element.82) | data formatting | bytes 12800 | tf_op jit(solution)/shard_map/slice | solution.py:24
  80.7 2.1 %copy.77 = f32[2,25,32,1]{2,0,3,1:T(2,128)} copy(f32[2,25,32,1]{3,2,0,1:T(8,128)} %get-tuple-element.83) | data formatting | bytes 12800 | tf_op jit(solution)/shard_map/slice | solution.py:26
  82.8 4.4 %collective-permute-start.13 = (f32[2,25,32,1]{2,0,3,1:T(2,128)}, f32[2,25,32,1]{2,0,3,1:T(2,128)}, u32[]{:S(2)}, u32[]{:S(2)}) collective-permute-start(f32[2,25,32,1]{2,0,3,1:T(2,128)} %copy.77), channel_id=1, source_target_pairs={{1,0},{2,1},{3,2},{4,3},{5,4},{6,5},{7,6},{8,7},{9,8},{10,9},{11,1... | collective-permute-start | bytes 19208 | tf_op jit(solution)/shard_map/ppermute | solution.py:26
  87.2 1.4 fusion.76
  88.6 1.0 slice.443
  89.6 2.0 %copy.76 = f32[2,25,32,1]{3,2,0,1:T(8,128)} copy(f32[2,25,32,1]{2,0,3,1:T(2,128)} %collective-permute-done.12) | data formatting | bytes 12800 | tf_op jit(solution)/shard_map/ppermute | solution.py:23
  91.7 2.0 %copy.78 = f32[2,25,32,1]{3,2,0,1:T(8,128)} copy(f32[2,25,32,1]{2,0,3,1:T(2,128)} %collective-permute-done.13) | data formatting | bytes 12800 | tf_op jit(solution)/shard_map/ppermute | solution.py:26
  94.1 3.6 %subtract_multiply_fusion.2 = f32[2,25,32,129]{3,2,0,1:T(8,128)} fusion(f32[2,25,32,1]{3,2,0,1:T(8,128)} %copy.78, f32[2,25,32,128]{3,2,0,1:T(8,128)S(1)} %fusion.17, f32[2,25,32,1]{3,2,0,1:T(8,128)} %copy.76, f32[25,32,129]{2,1,0:T(8,128)} %get-tuple-element.128, f32[25,32,129]{2,1,0:T(8,128)} %get-tuple-element.129), kind=kLoop, calls=%fused_computation.13 | loop fusion | flops 1651200 | bytes 2483200 | tf_op jit(solution)/shard_map/mul | solution.py:33
  97.7 1.0 collective-permute-done.17
  99.6 1.7 %subtract_multiply_fusion.6 = f32[2,25,32,128]{3,2,0,1:T(8,128)S(1)} fusion(f32[2,25,32,128]{3,2,0,1:T(8,128)S(1)} %fusion.17, f32[2,25,1,128]{3,2,0,1:T(1,128)S(1)} %bitcast.201, f32[2,25,31,128]{3,2,0,1:T(8,128)} %slice.443, f32[25,32,128]{2,1,0:T(8,128)} %get-tuple-element.127, f32[25,32,128]{2,1,0:T(8,128)S(1)} %get-tuple-element.126), kind=kLoop, calls=%fused_computation.48 | loop fusion | flops 1433600 | bytes 3276800 | tf_op jit(solution)/shard_map/mul | solution.py:33
  101.4 1.6 fusion.14
  103.1 1.6 add_bitcast_fusion
  105.3 1.4 fusion.92
  106.8 2.1 %copy.80 = f32[2,25,32,1]{2,0,3,1:T(2,128)} copy(f32[2,25,32,1]{3,2,0,1:T(8,128)} %get-tuple-element.80) | data formatting | bytes 12800 | tf_op jit(solution)/shard_map/slice | solution.py:24
  108.9 2.1 %copy.82 = f32[2,25,32,1]{2,0,3,1:T(2,128)} copy(f32[2,25,32,1]{3,2,0,1:T(8,128)} %get-tuple-element.81) | data formatting | bytes 12800 | tf_op jit(solution)/shard_map/slice | solution.py:26
  111.0 4.4 %collective-permute-start.19 = (f32[2,25,32,1]{2,0,3,1:T(2,128)}, f32[2,25,32,1]{2,0,3,1:T(2,128)}, u32[]{:S(2)}, u32[]{:S(2)}) collective-permute-start(f32[2,25,32,1]{2,0,3,1:T(2,128)} %copy.82), channel_id=1, source_target_pairs={{1,0},{2,1},{3,2},{4,3},{5,4},{6,5},{7,6},{8,7},{9,8},{10,9},{11,1... | collective-permute-start | bytes 19208 | tf_op jit(solution)/shard_map/ppermute | solution.py:26
  115.4 1.6 fusion.77
  117.0 1.0 slice.450
  118.1 2.0 %copy.81 = f32[2,25,32,1]{3,2,0,1:T(8,128)} copy(f32[2,25,32,1]{2,0,3,1:T(2,128)} %collective-permute-done.18) | data formatting | bytes 12800 | tf_op jit(solution)/shard_map/ppermute | solution.py:23
  120.1 2.0 %copy.83 = f32[2,25,32,1]{3,2,0,1:T(8,128)} copy(f32[2,25,32,1]{2,0,3,1:T(2,128)} %collective-permute-done.19) | data formatting | bytes 12800 | tf_op jit(solution)/shard_map/ppermute | solution.py:26
  122.1 1.2 collective-permute-start.23
  123.3 3.6 %subtract_multiply_fusion.1 = f32[2,25,32,129]{3,2,0,1:T(8,128)} fusion(f32[2,25,32,1]{3,2,0,1:T(8,128)} %copy.83, f32[2,25,32,128]{3,2,0,1:T(8,128)S(1)} %fusion.14, f32[2,25,32,1]{3,2,0,1:T(8,128)} %copy.81, f32[25,32,129]{2,1,0:T(8,128)} %get-tuple-element.128, f32[25,32,129]{2,1,0:T(8,128)} %get-tuple-element.129), kind=kLoop, calls=%fused_computation.12 | loop fusion | flops 1651200 | bytes 2483200 | tf_op jit(solution)/shard_map/mul | solution.py:33
  128.0 1.7 %subtract_multiply_fusion.5 = f32[2,25,32,128]{3,2,0,1:T(8,128)S(1)} fusion(f32[2,25,32,128]{3,2,0,1:T(8,128)S(1)} %fusion.14, f32[2,25,1,128]{3,2,0,1:T(1,128)S(1)} %bitcast.202, f32[2,25,31,128]{3,2,0,1:T(8,128)} %slice.450, f32[25,32,128]{2,1,0:T(8,128)} %get-tuple-element.127, f32[25,32,128]{2,1,0:T(8,128)S(1)} %get-tuple-element.126), kind=kLoop, calls=%fused_computation.47 | loop fusion | flops 1433600 | bytes 3276800 | tf_op jit(solution)/shard_map/mul | solution.py:33
  129.8 1.6 fusion.11
  131.6 1.6 slice_bitcast_fusion.25
  134.2 1.4 fusion.91
  135.6 1.5 copy.85
  137.4 2.1 %copy.87 = f32[2,25,32,1]{2,0,3,1:T(2,128)} copy(f32[2,25,32,1]{3,2,0,1:T(8,128)} %get-tuple-element.79) | data formatting | bytes 12800 | tf_op jit(solution)/shard_map/slice | solution.py:26
  139.5 4.3 %collective-permute-start.25 = (f32[2,25,32,1]{2,0,3,1:T(2,128)}, f32[2,25,32,1]{2,0,3,1:T(2,128)}, u32[]{:S(2)}, u32[]{:S(2)}) collective-permute-start(f32[2,25,32,1]{2,0,3,1:T(2,128)} %copy.87), channel_id=1, source_target_pairs={{1,0},{2,1},{3,2},{4,3},{5,4},{6,5},{7,6},{8,7},{9,8},{10,9},{11,1... | collective-permute-start | bytes 19208 | tf_op jit(solution)/shard_map/ppermute | solution.py:26
  143.7 1.3 fusion.46
  146.0 2.0 %copy.86 = f32[2,25,32,1]{3,2,0,1:T(8,128)} copy(f32[2,25,32,1]{2,0,3,1:T(2,128)} %collective-permute-done.24) | data formatting | bytes 12800 | tf_op jit(solution)/shard_map/ppermute | solution.py:23
  148.1 2.0 %copy.88 = f32[2,25,32,1]{3,2,0,1:T(8,128)} copy(f32[2,25,32,1]{2,0,3,1:T(2,128)} %collective-permute-done.25) | data formatting | bytes 12800 | tf_op jit(solution)/shard_map/ppermute | solution.py:26
  150.9 3.6 %subtract_multiply_fusion = f32[2,25,32,129]{3,2,0,1:T(8,128)} fusion(f32[2,25,32,1]{3,2,0,1:T(8,128)} %copy.88, f32[2,25,32,128]{3,2,0,1:T(8,128)S(1)} %fusion.11, f32[2,25,32,1]{3,2,0,1:T(8,128)} %copy.86, f32[25,32,129]{2,1,0:T(8,128)} %get-tuple-element.128, f32[25,32,129]{2,1,0:T(8,128)} %get-tuple-element.129), kind=kLoop, calls=%fused_computation.11 | loop fusion | flops 1651200 | bytes 2483200 | tf_op jit(solution)/shard_map/mul | solution.py:33
  156.0 1.7 %subtract_multiply_fusion.4 = f32[2,25,32,128]{3,2,0,1:T(8,128)S(1)} fusion(f32[2,25,32,128]{3,2,0,1:T(8,128)S(1)} %fusion.11, f32[2,25,1,128]{3,2,0,1:T(1,128)S(1)} %bitcast.199, f32[2,25,31,128]{3,2,0,1:T(8,128)} %slice.457, f32[25,32,128]{2,1,0:T(8,128)} %get-tuple-element.127, f32[25,32,128]{2,1,0:T(8,128)S(1)} %get-tuple-element.126), kind=kLoop, calls=%fused_computation.46 | loop fusion | flops 1433600 | bytes 3276800 | tf_op jit(solution)/shard_map/mul | solution.py:33
  158.1 1.3 fusion.8
  159.6 1.9 %constant_dynamic-update-slice_fusion.24 = (f32[2,25,32,128]{3,2,0,1:T(8,128)S(1)}, f32[2,1,32,128]{3,2,0,1:T(8,128)S(1)}, f32[2,1,32,128]{3,2,0,1:T(8,128)S(1)}...) fusion(f32[32,128]{1,0:T(8,128)} %get-tuple-element.124, ...), kind=kOutput, calls=%fused_computation.81 | convolution fusion | flops 4154367 | bytes 2850944 | tf_op jit(solution)/shard_map/scj,scno->njo/dot_general | solution.py:124
  (221 shorter events, 26.4 us)
Async XLA Ops:
  0.0 25.1 %copy-start = (f32[1,16,2,128,128]{4,3,2,1,0:T(8,128)S(1)}, f32[1,16,2,128,128]{4,3,2,1,0:T(8,128)}, u32[]{:S(2)}) copy-start(f32[1,16,2,128,128]{4,3,2,1,0:T(8,128)} %param.19) | copy-start | bytes 6291460
  1.7 12.3 %copy-start.3 = (f32[2,25,32,128]{3,2,1,0:T(8,128)S(1)}, f32[2,25,32,128]{3,2,1,0:T(8,128)}, u32[]{:S(2)}) copy-start(f32[2,25,32,128]{3,2,1,0:T(8,128)} %param.11) | copy-start | bytes 2457604
  6.4 34.1 %collective-permute-start = (f32[2,25,32,1]{2,0,3,1:T(2,128)}, f32[2,25,32,1]{2,0,3,1:T(2,128)}, u32[]{:S(2)}, u32[]{:S(2)}) collective-permute-start(f32[2,25,32,1]{2,0,3,1:T(2,128)} %copy.59), channel_id=1, source_target_pairs={{0,1},{1,2},{2,3},{3,4},{4,5},{5,6},{6,7},{7,8},{8,9},{9,10},{10,1... | collective-permute-start | bytes 19208 | tf_op jit(solution)/shard_map/ppermute | solution.py:23
  9.0 33.9 %collective-permute-start.1 = (f32[2,25,32,1]{2,0,3,1:T(2,128)}, f32[2,25,32,1]{2,0,3,1:T(2,128)}, u32[]{:S(2)}, u32[]{:S(2)}) collective-permute-start(f32[2,25,32,1]{2,0,3,1:T(2,128)} %copy.60), channel_id=1, source_target_pairs={{1,0},{2,1},{3,2},{4,3},{5,4},{6,5},{7,6},{8,7},{9,8},{10,9},{11,1... | collective-permute-start | bytes 19208 | tf_op jit(solution)/shard_map/ppermute | solution.py:26
  15.4 8.7 %copy-start.13 = (s32[32,128]{1,0:T(8,128)S(1)}, s32[32,128]{1,0:T(8,128)}, u32[]{:S(2)}) copy-start(s32[32,128]{1,0:T(8,128)} %param.15) | copy-start | bytes 49156
  15.4 9.4 %copy-start.55 = (f32[2,8,128]{2,1,0:T(8,128)S(1)}, f32[2,8,128]{2,1,0:T(8,128)}, u32[]{:S(2)}) copy-start(f32[2,8,128]{2,1,0:T(8,128)} %param.16) | copy-start | bytes 24580
  15.4 9.4 %copy-start.56 = (s32[1,16,2]{1,2,0:T(2,128)S(1)}, s32[1,16,2]{1,2,0:T(2,128)}, u32[]{:S(2)}) copy-start(s32[1,16,2]{1,2,0:T(2,128)} %param.17) | copy-start | bytes 388
  17.6 38.0 %collective-permute-start.2 = (f32[2,25,32,1]{2,0,3,1:T(2,128)}, f32[2,25,32,1]{2,0,3,1:T(2,128)}, u32[]{:S(2)}, u32[]{:S(2)}) collective-permute-start(f32[2,25,32,1]{2,0,3,1:T(2,128)} %copy.97), channel_id=1, source_target_pairs={{0,1},{1,2},{2,3},{3,4},{4,5},{5,6},{6,7},{7,8},{8,9},{9,10},{10,1... | collective-permute-start | bytes 19208 | tf_op jit(solution)/shard_map/ppermute | solution.py:23
  19.7 38.0 %collective-permute-start.3 = (f32[2,25,32,1]{2,0,3,1:T(2,128)}, f32[2,25,32,1]{2,0,3,1:T(2,128)}, u32[]{:S(2)}, u32[]{:S(2)}) collective-permute-start(f32[2,25,32,1]{2,0,3,1:T(2,128)} %copy.98), channel_id=1, source_target_pairs={{1,0},{2,1},{3,2},{4,3},{5,4},{6,5},{7,6},{8,7},{9,8},{10,9},{11,1... | collective-permute-start | bytes 19208 | tf_op jit(solution)/shard_map/ppermute | solution.py:26
  24.2 13.8 %copy-start.10 = (f32[25,32,128]{2,1,0:T(8,128)}, f32[25,32,128]{2,1,0:T(8,128)S(1)}, u32[]{:S(2)}) copy-start(f32[25,32,128]{2,1,0:T(8,128)S(1)} %fusion.18) | copy-start | bytes 1228804
  24.9 22.3 %collective-permute-start.4 = (f32[1,25,128]{2,0,1:T(1,128)}, f32[1,25,128]{2,0,1:T(1,128)}, u32[]{:S(2)}, u32[]{:S(2)}) collective-permute-start(f32[1,25,128]{2,0,1:T(1,128)} %slice_bitcast_fusion.26), channel_id=1, source_target_pairs={{0,1},{1,0},{2,3},{3,2},{4,5},{5,4},{6,7},{7,6},{8,9},{9,8},{10,11... | collective-permute-start | bytes 38408 | tf_op jit(solution)/shard_map/ppermute | solution.py:14
  27.6 131.8 %all-to-all-start = ((f32[16,2,2,128]{3,1,2,0:T(2,128)}), f32[16,2,2,128]{3,1,2,0:T(2,128)}, u32[]{:S(2)}, u32[]{:S(2)}) async-start(f32[16,2,2,128]{3,1,2,0:T(2,128)} %copy.91), calls=%async_computation | async-start | bytes 65536 | tf_op jit(solution)/shard_map/all_to_all | solution.py:95
  32.8 3.9 %copy-start.9 = (f32[24,32,128]{2,1,0:T(8,128)}, f32[24,32,128]{2,1,0:T(8,128)S(1)}, u32[]{:S(2)}) copy-start(f32[24,32,128]{2,1,0:T(8,128)S(1)} %slice_multiply_fusion.2) | copy-start | bytes 1179652
  34.2 4.7 %copy-start.14 = (f32[1,32,128]{2,1,0:T(8,128)}, f32[1,32,128]{2,1,0:T(8,128)S(1)}, u32[]{:S(2)}) copy-start(f32[1,32,128]{2,1,0:T(8,128)S(1)} %get-tuple-element.50) | copy-start | bytes 49156
  34.2 81.2 %copy-start.16 = (f32[1,32,128]{2,1,0:T(8,128)}, f32[1,32,128]{2,1,0:T(8,128)S(1)}, u32[]{:S(2)}) copy-start(f32[1,32,128]{2,1,0:T(8,128)S(1)} %get-tuple-element.51) | copy-start | bytes 49156
  38.9 6.0 %copy-start.12 = (f32[1,25,32,128]{3,2,1,0:T(8,128)S(1)}, f32[1,25,32,128]{3,2,1,0:T(8,128)}, u32[]{:S(2)}) copy-start(f32[1,25,32,128]{3,2,1,0:T(8,128)} %copy-done.11) | copy-start | bytes 1228804
  40.5 12.2 %collective-permute-start.8 = (f32[2,25,128]{2,0,1:T(2,128)}, f32[2,25,128]{2,0,1:T(2,128)}, u32[]{:S(2)}, u32[]{:S(2)}) collective-permute-start(f32[2,25,128]{2,0,1:T(2,128)} %bitcast.187), channel_id=1, source_target_pairs={{0,1},{1,0},{2,3},{3,2},{4,5},{5,4},{6,7},{7,6},{8,9},{9,8},{10,11... | collective-permute-start | bytes 76808 | tf_op jit(solution)/shard_map/ppermute | solution.py:14
  47.1 4.0 %collective-permute-start.5 = (f32[1,25,128]{2,0,1:T(1,128)}, f32[1,25,128]{2,0,1:T(1,128)S(1)}, u32[]{:S(2)}, u32[]{:S(2)}) collective-permute-start(f32[1,25,128]{2,0,1:T(1,128)} %collective-permute-done.4), channel_id=1, source_target_pairs={{0,2},{1,3},{2,0},{3,1},{4,6},{5,7},{6,4},{7,5},{8,10},{9,11},{10,... | collective-permute-start | bytes 38408 | tf_op jit(solution)/shard_map/ppermute | solution.py:14
  51.1 8.6 %collective-permute-start.6 = (f32[1,25,128]{2,0,1:T(1,128)S(1)}, f32[1,25,128]{2,0,1:T(1,128)S(1)}, u32[]{:S(2)}, u32[]{:S(2)}) collective-permute-start(f32[1,25,128]{2,0,1:T(1,128)S(1)} %collective-permute-done.5), channel_id=1, source_target_pairs={{0,4},{1,5},{2,6},{3,7},{4,0},{5,1},{6,2},{7,3},{8,12},{9,13},{10,... | collective-permute-start | bytes 38408 | tf_op jit(solution)/shard_map/ppermute | solution.py:14
  52.7 9.4 %collective-permute-start.9 = (f32[2,25,128]{2,0,1:T(2,128)}, f32[2,25,128]{2,0,1:T(2,128)S(1)}, u32[]{:S(2)}, u32[]{:S(2)}) collective-permute-start(f32[2,25,128]{2,0,1:T(2,128)} %collective-permute-done.8), channel_id=1, source_target_pairs={{0,2},{1,3},{2,0},{3,1},{4,6},{5,7},{6,4},{7,5},{8,10},{9,11},{10,... | collective-permute-start | bytes 76808 | tf_op jit(solution)/shard_map/ppermute | solution.py:14
  59.7 6.6 %collective-permute-start.7 = (f32[1,25,128]{2,0,1:T(1,128)S(1)}, f32[1,25,128]{2,0,1:T(1,128)S(1)}, u32[]{:S(2)}, u32[]{:S(2)}) collective-permute-start(f32[1,25,128]{2,0,1:T(1,128)S(1)} %collective-permute-done.6), channel_id=1, source_target_pairs={{0,8},{1,9},{2,10},{3,11},{4,12},{5,13},{6,14},{7,15},{8,0},{9,1},... | collective-permute-start | bytes 38408 | tf_op jit(solution)/shard_map/ppermute | solution.py:14
  62.1 4.3 %collective-permute-start.10 = (f32[2,25,128]{2,0,1:T(2,128)S(1)}, f32[2,25,128]{2,0,1:T(2,128)}, u32[]{:S(2)}, u32[]{:S(2)}) collective-permute-start(f32[2,25,128]{2,0,1:T(2,128)S(1)} %collective-permute-done.9), channel_id=1, source_target_pairs={{0,4},{1,5},{2,6},{3,7},{4,0},{5,1},{6,2},{7,3},{8,12},{9,13},{10,... | collective-permute-start | bytes 76808 | tf_op jit(solution)/shard_map/ppermute | solution.py:14
  66.4 5.1 %collective-permute-start.11 = (f32[2,25,128]{2,0,1:T(2,128)}, f32[2,25,128]{2,0,1:T(2,128)}, u32[]{:S(2)}, u32[]{:S(2)}) collective-permute-start(f32[2,25,128]{2,0,1:T(2,128)} %collective-permute-done.10), channel_id=1, source_target_pairs={{0,8},{1,9},{2,10},{3,11},{4,12},{5,13},{6,14},{7,15},{8,0},{9,1},... | collective-permute-start | bytes 76808 | tf_op jit(solution)/shard_map/ppermute | solution.py:14
  72.3 1.7 %copy-start.4 = (f32[2,25,32,128]{3,2,1,0:T(8,128)S(1)}, f32[2,25,32,128]{3,2,1,0:T(8,128)}, u32[]{:S(2)}) copy-start(f32[2,25,32,128]{3,2,1,0:T(8,128)} %param.11) | copy-start | bytes 2457604
  72.4 2.0 %copy-start.5 = (f32[2,25,32,129]{3,2,0,1:T(8,128)S(1)}, f32[2,25,32,129]{3,2,0,1:T(8,128)}, u32[]{:S(2)}) copy-start(f32[2,25,32,129]{3,2,0,1:T(8,128)} %subtract_multiply_fusion.3) | copy-start | bytes 2476804
  74.8 24.8 %copy-start.2 = (f32[2,25,32,128]{3,2,0,1:T(8,128)}, f32[2,25,32,128]{3,2,0,1:T(8,128)S(1)}, u32[]{:S(2)}) copy-start(f32[2,25,32,128]{3,2,0,1:T(8,128)S(1)} %fusion.17) | copy-start | bytes 2457604
  74.9 1.6 collective-permute-start.14
  76.5 10.7 %copy-start.32 = (f32[1,32,128]{2,1,0:T(8,128)}, f32[1,32,128]{2,1,0:T(8,128)S(1)}, u32[]{:S(2)}) copy-start(f32[1,32,128]{2,1,0:T(8,128)S(1)} %get-tuple-element.68) | copy-start | bytes 49156
  76.5 10.7 %collective-permute-start.15 = (f32[2,25,128]{2,0,1:T(2,128)}, f32[2,25,128]{2,0,1:T(2,128)}, u32[]{:S(2)}, u32[]{:S(2)}) collective-permute-start(f32[2,25,128]{2,0,1:T(2,128)} %collective-permute-done.14), channel_id=1, source_target_pairs={{0,2},{1,3},{2,0},{3,1},{4,6},{5,7},{6,4},{7,5},{8,10},{9,11},{10,... | collective-permute-start | bytes 76808 | tf_op jit(solution)/shard_map/ppermute | solution.py:14
  80.7 9.0 %collective-permute-start.12 = (f32[2,25,32,1]{2,0,3,1:T(2,128)}, f32[2,25,32,1]{2,0,3,1:T(2,128)}, u32[]{:S(2)}, u32[]{:S(2)}) collective-permute-start(f32[2,25,32,1]{2,0,3,1:T(2,128)} %copy.75), channel_id=1, source_target_pairs={{0,1},{1,2},{2,3},{3,4},{4,5},{5,6},{6,7},{7,8},{8,9},{9,10},{10,1... | collective-permute-start | bytes 19208 | tf_op jit(solution)/shard_map/ppermute | solution.py:23
  82.8 8.8 %collective-permute-start.13 = (f32[2,25,32,1]{2,0,3,1:T(2,128)}, f32[2,25,32,1]{2,0,3,1:T(2,128)}, u32[]{:S(2)}, u32[]{:S(2)}) collective-permute-start(f32[2,25,32,1]{2,0,3,1:T(2,128)} %copy.77), channel_id=1, source_target_pairs={{1,0},{2,1},{3,2},{4,3},{5,4},{6,5},{7,6},{8,7},{9,8},{10,9},{11,1... | collective-permute-start | bytes 19208 | tf_op jit(solution)/shard_map/ppermute | solution.py:26
  87.2 6.5 %collective-permute-start.16 = (f32[2,25,128]{2,0,1:T(2,128)}, f32[2,25,128]{2,0,1:T(2,128)}, u32[]{:S(2)}, u32[]{:S(2)}) collective-permute-start(f32[2,25,128]{2,0,1:T(2,128)} %collective-permute-done.15), channel_id=1, source_target_pairs={{0,4},{1,5},{2,6},{3,7},{4,0},{5,1},{6,2},{7,3},{8,12},{9,13},{10,... | collective-permute-start | bytes 76808 | tf_op jit(solution)/shard_map/ppermute | solution.py:14
  93.7 5.1 %collective-permute-start.17 = (f32[2,25,128]{2,0,1:T(2,128)}, f32[2,25,128]{2,0,1:T(2,128)}, u32[]{:S(2)}, u32[]{:S(2)}) collective-permute-start(f32[2,25,128]{2,0,1:T(2,128)} %collective-permute-done.16), channel_id=1, source_target_pairs={{0,8},{1,9},{2,10},{3,11},{4,12},{5,13},{6,14},{7,15},{8,0},{9,1},... | collective-permute-start | bytes 76808 | tf_op jit(solution)/shard_map/ppermute | solution.py:14
  99.6 1.8 %copy-start.7 = (f32[2,25,32,129]{3,2,0,1:T(8,128)S(1)}, f32[2,25,32,129]{3,2,0,1:T(8,128)}, u32[]{:S(2)}) copy-start(f32[2,25,32,129]{3,2,0,1:T(8,128)} %subtract_multiply_fusion.2) | copy-start | bytes 2476804
  101.4 1.7 %copy-start.42 = (f32[1,32,128]{2,1,0:T(8,128)S(1)}, f32[1,32,128]{2,1,0:T(8,128)}, u32[]{:S(2)}) copy-start(f32[1,32,128]{2,1,0:T(8,128)} %get-tuple-element.45) | copy-start | bytes 49156
  101.4 1.7 %copy-start.50 = (f32[1,32,128]{2,1,0:T(8,128)S(1)}, f32[1,32,128]{2,1,0:T(8,128)}, u32[]{:S(2)}) copy-start(f32[1,32,128]{2,1,0:T(8,128)} %get-tuple-element.71) | copy-start | bytes 49156
  103.0 25.0 %copy-start.1 = (f32[2,25,32,128]{3,2,0,1:T(8,128)}, f32[2,25,32,128]{3,2,0,1:T(8,128)S(1)}, u32[]{:S(2)}) copy-start(f32[2,25,32,128]{3,2,0,1:T(8,128)S(1)} %fusion.14) | copy-start | bytes 2457604
  103.0 1.7 %collective-permute-start.20 = (f32[2,25,128]{2,0,1:T(2,128)S(1)}, f32[2,25,128]{2,0,1:T(2,128)}, u32[]{:S(2)}, u32[]{:S(2)}) collective-permute-start(f32[2,25,128]{2,0,1:T(2,128)S(1)} %bitcast.229), channel_id=1, source_target_pairs={{0,1},{1,0},{2,3},{3,2},{4,5},{5,4},{6,7},{7,6},{8,9},{9,8},{10,11... | collective-permute-start | bytes 76808 | tf_op jit(solution)/shard_map/ppermute | solution.py:14
  104.8 10.7 %collective-permute-start.21 = (f32[2,25,128]{2,0,1:T(2,128)}, f32[2,25,128]{2,0,1:T(2,128)}, u32[]{:S(2)}, u32[]{:S(2)}) collective-permute-start(f32[2,25,128]{2,0,1:T(2,128)} %collective-permute-done.20), channel_id=1, source_target_pairs={{0,2},{1,3},{2,0},{3,1},{4,6},{5,7},{6,4},{7,5},{8,10},{9,11},{10,... | collective-permute-start | bytes 76808 | tf_op jit(solution)/shard_map/ppermute | solution.py:14
  108.9 9.2 %collective-permute-start.18 = (f32[2,25,32,1]{2,0,3,1:T(2,128)}, f32[2,25,32,1]{2,0,3,1:T(2,128)}, u32[]{:S(2)}, u32[]{:S(2)}) collective-permute-start(f32[2,25,32,1]{2,0,3,1:T(2,128)} %copy.80), channel_id=1, source_target_pairs={{0,1},{1,2},{2,3},{3,4},{4,5},{5,6},{6,7},{7,8},{8,9},{9,10},{10,1... | collective-permute-start | bytes 19208 | tf_op jit(solution)/shard_map/ppermute | solution.py:23
  111.0 9.0 %collective-permute-start.19 = (f32[2,25,32,1]{2,0,3,1:T(2,128)}, f32[2,25,32,1]{2,0,3,1:T(2,128)}, u32[]{:S(2)}, u32[]{:S(2)}) collective-permute-start(f32[2,25,32,1]{2,0,3,1:T(2,128)} %copy.82), channel_id=1, source_target_pairs={{1,0},{2,1},{3,2},{4,3},{5,4},{6,5},{7,6},{8,7},{9,8},{10,9},{11,1... | collective-permute-start | bytes 19208 | tf_op jit(solution)/shard_map/ppermute | solution.py:26
  115.4 6.7 %collective-permute-start.22 = (f32[2,25,128]{2,0,1:T(2,128)}, f32[2,25,128]{2,0,1:T(2,128)}, u32[]{:S(2)}, u32[]{:S(2)}) collective-permute-start(f32[2,25,128]{2,0,1:T(2,128)} %collective-permute-done.21), channel_id=1, source_target_pairs={{0,4},{1,5},{2,6},{3,7},{4,0},{5,1},{6,2},{7,3},{8,12},{9,13},{10,... | collective-permute-start | bytes 76808 | tf_op jit(solution)/shard_map/ppermute | solution.py:14
  122.1 5.1 %collective-permute-start.23 = (f32[2,25,128]{2,0,1:T(2,128)}, f32[2,25,128]{2,0,1:T(2,128)}, u32[]{:S(2)}, u32[]{:S(2)}) collective-permute-start(f32[2,25,128]{2,0,1:T(2,128)} %collective-permute-done.22), channel_id=1, source_target_pairs={{0,8},{1,9},{2,10},{3,11},{4,12},{5,13},{6,14},{7,15},{8,0},{9,1},... | collective-permute-start | bytes 76808 | tf_op jit(solution)/shard_map/ppermute | solution.py:14
  128.0 1.8 %copy-start.8 = (f32[2,25,32,129]{3,2,0,1:T(8,128)S(1)}, f32[2,25,32,129]{3,2,0,1:T(8,128)}, u32[]{:S(2)}) copy-start(f32[2,25,32,129]{3,2,0,1:T(8,128)} %subtract_multiply_fusion.1) | copy-start | bytes 2476804
  129.8 1.8 %copy-start.24 = (f32[1,32,128]{2,1,0:T(8,128)S(1)}, f32[1,32,128]{2,1,0:T(8,128)}, u32[]{:S(2)}) copy-start(f32[1,32,128]{2,1,0:T(8,128)} %get-tuple-element.63) | copy-start | bytes 49156
  129.8 1.8 %copy-start.28 = (f32[1,32,128]{2,1,0:T(8,128)S(1)}, f32[1,32,128]{2,1,0:T(8,128)}, u32[]{:S(2)}) copy-start(f32[1,32,128]{2,1,0:T(8,128)} %get-tuple-element.66) | copy-start | bytes 49156
  129.8 1.8 %copy-start.34 = (f32[1,32,128]{2,1,0:T(8,128)S(1)}, f32[1,32,128]{2,1,0:T(8,128)}, u32[]{:S(2)}) copy-start(f32[1,32,128]{2,1,0:T(8,128)} %get-tuple-element.69) | copy-start | bytes 49156
  129.8 1.8 %copy-start.48 = (f32[1,32,128]{2,1,0:T(8,128)S(1)}, f32[1,32,128]{2,1,0:T(8,128)}, u32[]{:S(2)}) copy-start(f32[1,32,128]{2,1,0:T(8,128)} %get-tuple-element.60) | copy-start | bytes 49156
  131.5 1.7 %collective-permute-start.26 = (f32[2,25,128]{2,0,1:T(2,128)S(1)}, f32[2,25,128]{2,0,1:T(2,128)}, u32[]{:S(2)}, u32[]{:S(2)}) collective-permute-start(f32[2,25,128]{2,0,1:T(2,128)S(1)} %bitcast.228), channel_id=1, source_target_pairs={{0,1},{1,0},{2,3},{3,2},{4,5},{5,4},{6,7},{7,6},{8,9},{9,8},{10,11... | collective-permute-start | bytes 76808 | tf_op jit(solution)/shard_map/ppermute | solution.py:14
  133.2 10.5 %collective-permute-start.27 = (f32[2,25,128]{2,0,1:T(2,128)}, f32[2,25,128]{2,0,1:T(2,128)}, u32[]{:S(2)}, u32[]{:S(2)}) collective-permute-start(f32[2,25,128]{2,0,1:T(2,128)} %collective-permute-done.26), channel_id=1, source_target_pairs={{0,2},{1,3},{2,0},{3,1},{4,6},{5,7},{6,4},{7,5},{8,10},{9,11},{10,... | collective-permute-start | bytes 76808 | tf_op jit(solution)/shard_map/ppermute | solution.py:14
  137.1 8.9 %collective-permute-start.24 = (f32[2,25,32,1]{2,0,3,1:T(2,128)S(1)}, f32[2,25,32,1]{2,0,3,1:T(2,128)}, u32[]{:S(2)}, u32[]{:S(2)}) collective-permute-start(f32[2,25,32,1]{2,0,3,1:T(2,128)S(1)} %copy.85), channel_id=1, source_target_pairs={{0,1},{1,2},{2,3},{3,4},{4,5},{5,6},{6,7},{7,8},{8,9},{9,10},{10,1... | collective-permute-start | bytes 19208 | tf_op jit(solution)/shard_map/ppermute | solution.py:23
  139.5 8.6 %collective-permute-start.25 = (f32[2,25,32,1]{2,0,3,1:T(2,128)}, f32[2,25,32,1]{2,0,3,1:T(2,128)}, u32[]{:S(2)}, u32[]{:S(2)}) collective-permute-start(f32[2,25,32,1]{2,0,3,1:T(2,128)} %copy.87), channel_id=1, source_target_pairs={{1,0},{2,1},{3,2},{4,3},{5,4},{6,5},{7,6},{8,7},{9,8},{10,9},{11,1... | collective-permute-start | bytes 19208 | tf_op jit(solution)/shard_map/ppermute | solution.py:26
  143.7 6.4 %collective-permute-start.28 = (f32[2,25,128]{2,0,1:T(2,128)}, f32[2,25,128]{2,0,1:T(2,128)}, u32[]{:S(2)}, u32[]{:S(2)}) collective-permute-start(f32[2,25,128]{2,0,1:T(2,128)} %collective-permute-done.27), channel_id=1, source_target_pairs={{0,4},{1,5},{2,6},{3,7},{4,0},{5,1},{6,2},{7,3},{8,12},{9,13},{10,... | collective-permute-start | bytes 76808 | tf_op jit(solution)/shard_map/ppermute | solution.py:14
  150.1 5.1 %collective-permute-start.29 = (f32[2,25,128]{2,0,1:T(2,128)}, f32[2,25,128]{2,0,1:T(2,128)}, u32[]{:S(2)}, u32[]{:S(2)}) collective-permute-start(f32[2,25,128]{2,0,1:T(2,128)} %collective-permute-done.28), channel_id=1, source_target_pairs={{0,8},{1,9},{2,10},{3,11},{4,12},{5,13},{6,14},{7,15},{8,0},{9,1},... | collective-permute-start | bytes 76808 | tf_op jit(solution)/shard_map/ppermute | solution.py:14
  156.0 1.8 %copy-start.6 = (f32[2,25,32,129]{3,2,0,1:T(8,128)S(1)}, f32[2,25,32,129]{3,2,0,1:T(8,128)}, u32[]{:S(2)}) copy-start(f32[2,25,32,129]{3,2,0,1:T(8,128)} %subtract_multiply_fusion) | copy-start | bytes 2476804
  157.8 1.6 copy-start.21
  157.8 1.6 copy-start.23
  157.8 1.6 copy-start.25
  157.9 1.6 copy-start.27
  157.9 1.6 copy-start.29
  157.9 1.6 copy-start.30
  157.9 1.6 copy-start.31
  157.9 1.6 copy-start.33
  157.9 1.6 copy-start.35
  (25 other events, 34.5 us)
where the time goes:
time: 167 us; the launch traced here: 164 us
  local copies, waits for them, and re-layouts  60.4 us (36%)
  other arithmetic  51.6 us (31%)
  starting transfers between devices  40.7 us (24%)
  waiting for transfers between devices  6.68 us (4%)
  matrix products  3.94 us (2%)
    mul x9, other arithmetic, face_flux(): wet_inside * wet_beyond  23.3 us
    ppermute x5, starting transfers between devices, padded(): lax.ppermute(lax.slice_in_dim(block, 0, width, axis=dim), axis, backward)  22.5 us
    slice x8, local copies, waits for them, and re-layouts, padded(): lax.slice_in_dim(block, block.shape[dim] - width, None, axis=dim)  13.6 us
    ppermute x20, starting transfers between devices, partner(): lax.ppermute(value, axis, [(i, i ^ 1 << stride) for i in range(lax.axis_s...  13.3 us
    ppermute x5, local copies, waits for them, and re-layouts, padded(): lax.ppermute(lax.slice_in_dim(block, block.shape[dim] - width, None, axis...  10.1 us
    ppermute x5, local copies, waits for them, and re-layouts, padded(): lax.ppermute(lax.slice_in_dim(block, 0, width, axis=dim), axis, backward)  10 us
    mul x12, other arithmetic, solve_columns(): ratios[level] * levels_out[level + 1]  8.84 us
    slice x4, local copies, waits for them, and re-layouts, padded(): lax.slice_in_dim(block, 0, width, axis=dim)  8.42 us
  transfers between devices with their start and end apart: 31, of which 5 were waited for; matrix products, arithmetic and copies ran while one was open for 63% of the time, Pallas kernels for 0%

commit v1 on v0

v1 whole, which is shorter than its diff:
```python
import functools

import jax
import jax.numpy as jnp
from jax import lax
from jax.experimental import pallas as pl
from jax.experimental.pallas import tpu as pltpu
from jax.sharding import PartitionSpec as P

SUB = 4
DIFFUSION = 0.12
FLUX_GAIN = 0.5
GROUP = 5
F32 = jnp.float32
VMEM = pl.BlockSpec(memory_space=pltpu.VMEM)
SMEM = pl.BlockSpec(memory_space=pltpu.SMEM)
HBM = pl.BlockSpec(memory_space=pltpu.HBM)
VMEM_LIMIT = 16 * 1024 * 1024


def lane_index():
    return lax.broadcasted_iota(jnp.int32, (8, 128), 1)


def row_index():
    return lax.broadcasted_iota(jnp.int32, (8, 128), 0)


def lanes(tile, shift):
    shift = shift % 128
    return pltpu.roll(tile, shift, 1) if shift else tile


def rows(tile, shift):
    shift = shift % 8
    return pltpu.roll(tile, shift, 0) if shift else tile


def take(tile, index):
    return jnp.take_along_axis(tile, index, axis=1)


def spread_order():
    lane = lane_index()
    return 4 * (lane & 31) + (lane >> 5)


def gather_order():
    lane = lane_index()
    return 32 * (lane & 3) + (lane >> 2)


def call(body, out, in_specs, scratch=(), out_specs=None, cost=None, name=None):
    return pl.pallas_call(
        body,
        out_shape=out,
        in_specs=in_specs,
        out_specs=out_specs if out_specs is not None else [VMEM] * len(out),
        scratch_shapes=list(scratch),
        compiler_params=pltpu.CompilerParams(vmem_limit_bytes=VMEM_LIMIT),
        cost_estimate=cost,
        name=name,
    )


def cost(micros):
    return pl.CostEstimate(flops=0, bytes_accessed=int(micros * 3.0e6), transcendentals=0)


def shape(*dims):
    return pltpu.VMEM(dims, F32)


def in_hbm(*arrays):
    return [pltpu.with_memory_space_constraint(x, pltpu.HBM) for x in arrays]


def in_vmem(*arrays):
    return [pltpu.with_memory_space_constraint(x, pltpu.VMEM) for x in arrays]


def face(flow, mask):
    half = 0.5 * flow
    return mask * (half + DIFFUSION), mask * (half - DIFFUSION)


def stencil(east, north, west, south):
    a_e, b_e = east
    a_n, b_n = north
    a_w, b_w = west
    a_s, b_s = south
    return (((1.0 - a_e) + b_w) - a_n) + b_s, b_e, a_w, b_n, a_s


def advance(weights, cell, east, west, north, south):
    own, b_e, a_w, b_n, a_s = weights
    return (own * cell + (a_w * west - b_e * east)) + (a_s * south - b_n * north)


def north_of(tiles, beyond):
    row = row_index()
    turned = [rows(t, -1) for t in tiles]
    return [jnp.where(row == 7, n, t) for t, n in zip(turned, turned[1:] + [beyond])]


def south_of(tiles):
    row = row_index()
    turned = [rows(t, 1) for t in tiles]
    return [turned[0]] + [jnp.where(row == 0, p, t) for p, t in zip(turned, turned[1:])]


def northern_rows(t_hbm, e_hbm, n_hbm, d_hbm, t, e, n, d, sems):
    top = pl.ds(t_hbm.shape[2] - 8, 8)
    return [
        pltpu.make_async_copy(t_hbm.at[:, :, top], t, sems.at[0]),
        pltpu.make_async_copy(e_hbm.at[:, top], e, sems.at[1]),
        pltpu.make_async_copy(n_hbm.at[:, top], n, sems.at[2]),
        pltpu.make_async_copy(d_hbm.at[top], d, sems.at[3]),
    ]


def fold_kernel(depth, t_hbm, e_hbm, n_hbm, d_hbm, out, west, east, t, e, n, d, sems):
    copies = northern_rows(t_hbm, e_hbm, n_hbm, d_hbm, t, e, n, d, sems)
    for copy in copies:
        copy.start()
    for copy in copies:
        copy.wait()
    lane, row = lane_index(), row_index()
    turn = 127 - lane
    levels = d[...].astype(F32)
    wests = [jnp.zeros((8, 128), F32)] * 2
    easts = [jnp.zeros((8, 128), F32)] * 2
    for k in range(depth + 1):
        if k < depth:
            cells = jnp.where(row < 4, rows(t[0, k], 4), t[1, k])
            flows = jnp.where(row < 4, rows(n[k], 4), e[k])
            if k < 4:
                flows = jnp.where(row == 4, rows(levels, -k), flows)
            tiles = (cells, flows)
        else:
            tiles = (None, levels)
        for half, tile in enumerate(tiles):
            if tile is None:
                continue
            tile = take(tile, turn)
            if k < depth:
                out[k, 8 * half : 8 * half + 8] = tile
            tile = lanes(tile, 4 * k)
            easts[half] = jnp.where((lane >= 4 * k) & (lane < 4 * k + 4), tile, easts[half])
            last = (4 * k - 4) % 128
            wests[half] = jnp.where((lane >= last) & (lane < last + 4), tile, wests[half])
    order = spread_order()
    for half in range(2):
        west[8 * half : 8 * half + 8] = take(lanes(wests[half], 4), order)
        east[8 * half : 8 * half + 8] = take(easts[half], order)


def edge_columns(planes, levels_tile):
    lane = lane_index()
    zero = jnp.zeros((8, 128), F32)
    first, last = [zero, zero], [zero, zero]
    items = list(planes)
    if levels_tile is not None:
        items.append(levels_tile)
    for k, tile in enumerate(items):
        tile = lanes(tile, 4 * k)
        low = 4 * k
        inside = (lane >= low) & (lane < low + 8)
        if low + 8 > 128:
            inside = inside | (lane < low + 8 - 128)
        first[k % 2] = jnp.where(inside, tile, first[k % 2])
        high = (4 * k - 8) % 128
        inside = (lane >= high) & (lane < high + 8)
        if high + 8 > 128:
            inside = inside | (lane < high + 8 - 128)
        last[k % 2] = jnp.where(inside, tile, last[k % 2])
    even = ((lane >> 2) & 1) == 0
    order = spread_order()
    w1 = jnp.where(even, first[0], first[1])
    w2 = lanes(jnp.where(even, first[1], first[0]), -4)
    e1 = lanes(jnp.where(even, last[1], last[0]), 4)
    e2 = lanes(jnp.where(even, last[0], last[1]), 8)
    return [take(x, order) for x in (w1, w2, e2, e1)]


def columns_kernel(depth, t_hbm, e_hbm, n_hbm, d_hbm, blocks, to_core, to_odd, t, e, n, d, sems):
    copies = [
        pltpu.make_async_copy(d_hbm, d, sems.at[4]),
        pltpu.make_async_copy(t_hbm.at[0], t.at[0], sems.at[0]),
        pltpu.make_async_copy(t_hbm.at[1], t.at[1], sems.at[1]),
        pltpu.make_async_copy(e_hbm, e, sems.at[2]),
        pltpu.make_async_copy(n_hbm, n, sems.at[3]),
    ]
    for copy in copies:
        copy.start()
    even = lax.rem(lax.axis_index("lon"), 2) == 0
    count = t.shape[2] // 8
    copies[0].wait()
    for f, field in enumerate((t.at[0], t.at[1], e, n)):
        copies[f + 1].wait()
        for j in range(count):
            span = slice(8 * j, 8 * j + 8)
            planes = [field[k, span] for k in range(depth)]
            found = edge_columns(planes, d[span].astype(F32) if f == 0 else None)
            for b, tile in enumerate(found):
                blocks[b, f, span] = tile
            w1, e1 = found[0], found[3]
            to_core[f, span] = jnp.where(even, e1, w1)
            to_odd[f, span] = jnp.where(even, w1, e1)


def regrid_kernel(size, atm_hbm, w_hbm, src_hbm, out, wide, w, atm, src, sems, w_sems):
    first = [pltpu.make_async_copy(atm_hbm, atm, sems.at[0]), pltpu.make_async_copy(src_hbm, src, sems.at[1])]
    for copy in first:
        copy.start()
    parts = w_sems.shape[0]
    each = size // parts
    weights = [
        pltpu.make_async_copy(w_hbm.at[0, pl.ds(p * each, each)], w.at[pl.ds(p * each, each)], w_sems.at[p])
        for p in range(parts)
    ]
    for copy in weights:
        copy.start()
    for copy in first:
        copy.wait()
    flat = atm[...].reshape(atm.shape[0] * atm.shape[1], atm.shape[2])
    count = flat.shape[0]
    blocks = atm.shape[1]
    columns = jnp.transpose(jnp.concatenate([flat, jnp.zeros((128 - count, 128), F32)], axis=0))
    for c in range(count):
        wide[c] = jnp.broadcast_to(columns[:, c : c + 1], (128, 128))
    def owner(e, carry):
        for s in range(2):
            block = src[s, e]
            sums = [None, None]
            for i in range(16):
                span = slice(8 * i, 8 * i + 8)
                weight = w[e, s, span]
                for f in range(2):
                    term = weight * wide[f * blocks + block, span]
                    sums[f] = term if sums[f] is None else sums[f] + term
            for f in range(2):
                out[e, 2 * f + s : 2 * f + s + 1] = jnp.sum(sums[f], axis=0, keepdims=True)
        return carry

    for p in range(parts):
        weights[p].wait()
        lax.fori_loop(p * each, (p + 1) * each, owner, 0, unroll=2)


def inner_kernel(
    depth, t_hbm, e_hbm, n_hbm, d_hbm, mix_hbm, out, inverse, linked, surface_wet, t, e, n, d, mix, sems, other
):
    levels = pltpu.make_async_copy(d_hbm, d, other.at[0])
    mixing = pltpu.make_async_copy(mix_hbm, mix, other.at[1])

    def parts(g):
        part = pl.ds(g * GROUP, GROUP)
        return (
            pltpu.make_async_copy(t_hbm.at[:, part], t.at[:, part], sems.at[g]),
            pltpu.make_async_copy(e_hbm.at[part], e.at[part], sems.at[g]),
            pltpu.make_async_copy(n_hbm.at[part], n.at[part], sems.at[g]),
        )

    levels.start()
    for g in range(depth // GROUP):
        for copy in parts(g):
            copy.start()
        if g == 0:
            mixing.start()
    levels.wait()
    row = row_index()
    count = t.shape[2] // 8
    spans = [slice(8 * j, 8 * j + 8) for j in range(count)]
    deep = [d[s] for s in spans]

    def wet_at(k):
        return [jnp.where(x > k, 1.0, 0.0).astype(F32) for x in deep]

    def level(k):
        wet = wet_at(k)
        easts = [face(e[k, s], w * lanes(w, -1)) for s, w in zip(spans, wet)]
        norths = [face(n[k, s], w * v) for s, w, v in zip(spans, wet, north_of(wet, wet[0]))]
        wests = [(lanes(a, 1), lanes(b, 1)) for a, b in easts]
        a_s = south_of([a for a, _ in norths])
        b_s = south_of([b for _, b in norths])
        a_s[0] = jnp.where(row == 0, 0.0, a_s[0])
        b_s[0] = jnp.where(row == 0, 0.0, b_s[0])
        weights = [stencil(*faces) for faces in zip(easts, norths, wests, zip(a_s, b_s))]
        state = [[t[f, k, s] for s in spans] for f in range(2)]
        for _ in range(SUB):
            for f in range(2):
                cells = state[f]
                up, down = north_of(cells, cells[-1]), south_of(cells)
                state[f] = [
                    advance(w, c, lanes(c, -1), lanes(c, 1), u, v)
                    for w, c, u, v in zip(weights, cells, up, down)
                ]
        for f in range(2):
            for s, c in zip(spans, state[f]):
                out[f, k, s] = c

    def some(g, carry):
        for copy in parts(g):
            copy.wait()
        for i in range(GROUP):
            level(g * GROUP + i)
        return carry

    lax.fori_loop(0, depth // GROUP, some, 0)

    zero = jnp.zeros((8, 128), F32)
    mixing.wait()
    link_above = [zero] * count
    last_ratio = [zero] * count
    for s, wet in zip(spans, wet_at(0)):
        surface_wet[s] = wet
    for k in range(depth):
        wet = wet_at(k + 1)
        for j, s in enumerate(spans):
            link = mix[k, s] * wet[j] if k < depth - 1 else zero
            inv = 1.0 / (1.0 + link_above[j] + link + link_above[j] * last_ratio[j])
            inverse[k, s] = inv
            if k < depth - 1:
                linked[k, s] = link
            last_ratio[j] = -link * inv
            link_above[j] = link


def fold_weights(flows, wet, own_wet, toward_east, toward_west):
    row = row_index()
    result = []
    e_flow = [jnp.where(row < 4, rows(x, 4), x) for x in flows]
    n_flow = [jnp.where(row < 4, x, rows(x, 4)) for x in flows]
    easts = [face(x, w * v) for x, w, v in zip(e_flow, wet, toward_east(wet))]
    a_w = toward_west([a for a, _ in easts])
    b_w = toward_west([b for _, b in easts])
    for i in range(len(flows)):
        up = fold_north(wet[i], own_wet[i], own_wet[i])
        north = face(n_flow[i], wet[i] * up)
        south = (rows(north[0], 1), rows(north[1], 1))
        result.append(stencil(easts[i], north, (a_w[i], b_w[i]), south))
    return result


def fold_north(fold, first, second):
    row = row_index()
    return jnp.where((row & 3) == 3, jnp.where(row < 4, rows(first, 4), second), rows(fold, -1))


def strip_kernel(depth, t_hbm, e_hbm, n_hbm, d_hbm, fold, strip, t, e, n, d, sems):
    copies = northern_rows(t_hbm, e_hbm, n_hbm, d_hbm, t, e, n, d, sems)
    for copy in copies:
        copy.start()
    for copy in copies:
        copy.wait()
    row = row_index()
    deep = d[...]
    fold_deep = fold_levels(fold)

    def plus(tiles):
        return [lanes(x, 1) for x in tiles]

    def minus(tiles):
        return [lanes(x, -1) for x in tiles]

    def level(k):
        wet = jnp.where(deep > k, 1.0, 0.0).astype(F32)
        wet_fold = jnp.where(fold_deep > jnp.asarray(k).astype(F32), 1.0, 0.0).astype(F32)
        over = fold_weights([fold[k, 8:16]], [wet_fold], [wet], plus, minus)[0]
        east = face(e[k], wet * lanes(wet, -1))
        north = face(n[k], wet * jnp.where(row == 7, wet_fold, rows(wet, -1)))
        weights = stencil(
            east, north, (lanes(east[0], 1), lanes(east[1], 1)), (rows(north[0], 1), rows(north[1], 1))
        )
        one, two, cells = t[0, k], t[1, k], fold[k, 0:8]
        for step in range(SUB):
            up_one = jnp.where(row == 7, rows(cells, 4), rows(one, -1))
            up_two = jnp.where(row == 7, cells, rows(two, -1))
            if step < SUB - 1:
                up = fold_north(cells, one, two)
                cells = advance(over, cells, lanes(cells, 1), lanes(cells, -1), up, rows(cells, 1))
            one = advance(weights, one, lanes(one, -1), lanes(one, 1), up_one, rows(one, 1))
            two = advance(weights, two, lanes(two, -1), lanes(two, 1), up_two, rows(two, 1))
        strip[0, k] = one
        strip[1, k] = two

    def some(g, carry):
        for i in range(GROUP):
            level(g * GROUP + i)
        return carry

    lax.fori_loop(0, depth // GROUP, some, 0)


def fold_levels(fold):
    row = row_index()
    deep = jnp.zeros((8, 128), F32)
    for r in range(4):
        deep = jnp.where((row & 3) == r, jnp.broadcast_to(fold[r, 12:13], (8, 128)), deep)
    return deep


def fold_columns(depth, fold):
    return [
        edge_columns([fold[k, 8 * half : 8 * half + 8] for k in range(depth)], fold_levels(fold) if half else None)
        for half in range(2)
    ]


def corners_kernel(depth, size, fold, west, east, blocks, to_core, to_odd):
    me = lax.axis_index("lon")
    even = lax.rem(me, 2) == 0
    for half, found in enumerate(fold_columns(depth, fold)):
        span = slice(8 * half, 8 * half + 8)
        for b, tile in enumerate(found):
            blocks[b, span] = tile
        w1, e1 = found[0], found[3]
        to_core[span] = jnp.where(even, e1, w1)
        odd = jnp.where(even, w1, e1)
        odd = jnp.where(me == 0, west[span], odd)
        to_odd[span] = jnp.where(me == size - 1, east[span], odd)


def edge_side(depth, rows_count, cells, flows, fold_cells, fold_flows):
    lane, row = lane_index(), row_index()
    level = lane & 31
    count = rows_count // 8

    def plus(tiles):
        turned = [lanes(x, 32) for x in tiles]
        return [turned[0]] + [jnp.where(lane < 32, p, x) for p, x in zip(turned, turned[1:])]

    def minus(tiles):
        turned = [lanes(x, -32) for x in tiles]
        return [jnp.where(lane >= 96, q, x) for x, q in zip(turned, turned[1:])] + [turned[2]]

    at_levels = (lane & 96) + depth
    wet = [
        [
            jnp.where(take(cells[b][0][j], at_levels) > level.astype(F32), 1.0, 0.0).astype(F32)
            for j in range(count)
        ]
        for b in range(3)
    ]
    wet_fold = []
    for b in range(3):
        deep = take(fold_flows[b], at_levels)
        deep = jnp.where(row < 4, rows(deep, 4), deep)
        wet_fold.append(jnp.where(deep > level.astype(F32), 1.0, 0.0).astype(F32))
    over = fold_weights(fold_flows, wet_fold, [wet[b][-1] for b in range(3)], plus, minus)

    easts = [[None] * count for _ in range(3)]
    wests = [[None] * count for _ in range(3)]
    for j in range(count):
        beyond = minus([wet[b][j] for b in range(3)])
        found = [face(flows[b][0][j], wet[b][j] * beyond[b]) for b in range(3)]
        a_w, b_w = plus([a for a, _ in found]), plus([b for _, b in found])
        for b in range(3):
            easts[b][j] = found[b]
            wests[b][j] = (a_w[b], b_w[b])
    weights = []
    for b in range(3):
        up = north_of(wet[b], wet_fold[b])
        norths = [face(flows[b][1][j], wet[b][j] * up[j]) for j in range(count)]
        a_s, b_s = south_of([a for a, _ in norths]), south_of([c for _, c in norths])
        a_s[0] = jnp.where(row == 0, 0.0, a_s[0])
        b_s[0] = jnp.where(row == 0, 0.0, b_s[0])
        weights.append(
            [stencil(easts[b][j], norths[j], wests[b][j], (a_s[j], b_s[j])) for j in range(count)]
        )

    state = [[list(cells[b][f]) for f in range(2)] for b in range(3)]
    folded = list(fold_cells)
    for step in range(SUB):
        fold_east, fold_west = plus(folded), minus(folded)
        following = [[[None] * count for _ in range(2)] for _ in range(3)]
        for f in range(2):
            for j in range(count):
                line = [state[b][f][j] for b in range(3)]
                east, west = minus(line), plus(line)
                for b in range(3):
                    following[b][f][j] = (east[b], west[b])
        next_fold = []
        for b in range(3):
            up = fold_north(folded[b], state[b][0][-1], state[b][1][-1])
            next_fold.append(
                advance(over[b], folded[b], fold_east[b], fold_west[b], up, rows(folded[b], 1))
            )
        for b in range(3):
            beyond = (rows(folded[b], 4), folded[b])
            for f in range(2):
                tiles = state[b][f]
                up, down = north_of(tiles, beyond[f]), south_of(tiles)
                state[b][f] = [
                    advance(weights[b][j], tiles[j], *following[b][f][j], up[j], down[j]) for j in range(count)
                ]
        folded = next_fold
    return state[1]


def last_kernel(
    depth, strip, wet, inner, inverse, link, blocks, core, odd, fold, fold_core, fold_odd, pieces, target_hbm,
    out_hbm, merged, out, target, sems, other,
):
    targets = pltpu.make_async_copy(target_hbm, target, other.at[0])
    targets.start()
    lane, row = lane_index(), row_index()
    size = pieces.shape[0]
    rows_count = inner.shape[2]
    count = rows_count // 8
    spans = [slice(8 * j, 8 * j + 8) for j in range(count)]
    me = lax.axis_index("lon")
    even = lax.rem(me, 2) == 0

    def received(f, s, west):
        a, b = core[f, s], odd[f, s]
        return jnp.where(even, b, a) if west else jnp.where(even, a, b)

    def own(b, f, s):
        return blocks[b, f, s]

    sides = []
    for west in (True, False):
        near, far = (0, 1) if west else (3, 2)
        here = [[[own(b, f, s) for s in spans] for f in range(4)] for b in (near, far)]
        there = [[received(f, s, west) for s in spans] for f in range(4)]
        a, b = fold_core[...], fold_odd[...]
        letter = jnp.where(even, b, a) if west else jnp.where(even, a, b)
        line = [there, here[0], here[1]] if west else [here[1], here[0], there]
        cells_near = [fold[near, 0:8], fold[far, 0:8]]
        flows_near = [fold[near, 8:16], fold[far, 8:16]]
        if west:
            fold_cells = [letter[0:8]] + cells_near
            fold_flows = [letter[8:16]] + flows_near
        else:
            fold_cells = cells_near[::-1] + [letter[0:8]]
            fold_flows = flows_near[::-1] + [letter[8:16]]
        sides.append(
            edge_side(depth, rows_count, [x[0:2] for x in line], [x[2:4] for x in line], fold_cells, fold_flows)
        )

    order = gather_order()
    group_even = ((lane >> 2) & 1) == 0
    for f in range(2):
        for j, s in enumerate(spans):
            a = take(sides[0][f][j], order)
            b = lanes(take(sides[1][f][j], order), -4)
            merged[0, f, s] = jnp.where(group_even, a, b)
            merged[1, f, s] = jnp.where(group_even, b, a)

    surface = [[jnp.zeros((8, 128), F32) for _ in spans] for _ in range(2)]
    targets.wait()
    for a in range(size):
        for s in range(2):
            goal = target[s, a]
            hits = [row + 8 * j == goal for j in range(count)]
            for f in range(2):
                piece = jnp.broadcast_to(pieces[a, 2 * f + s : 2 * f + s + 1], (8, 128))
                surface[f] = [x + jnp.where(hit, piece, 0.0) for x, hit in zip(surface[f], hits)]

    outer = (lane < 4) | (lane >= 124)
    partial_value = [[None] * count for _ in range(2)]
    for k in range(depth):
        for f in range(2):
            for j, s in enumerate(spans):
                cell = inner[f, k, s]
                if j == count - 1:
                    cell = jnp.where(row >= 4, strip[f, k], cell)
                cell = jnp.where(outer, lanes(merged[k % 2, f, s], -4 * k), cell)
                if k == 0:
                    cell = cell + FLUX_GAIN * surface[f][j] * wet[s]
                else:
                    cell = cell + link[k - 1, s] * partial_value[f][j]
                value = cell * inverse[k, s]
                partial_value[f][j] = value
                out[f, k, s] = value
    copies = []
    for k in range(depth - 1, -1, -1):
        if k < depth - 1:
            for f in range(2):
                for j, s in enumerate(spans):
                    value = out[f, k, s] + link[k, s] * inverse[k, s] * partial_value[f][j]
                    partial_value[f][j] = value
                    out[f, k, s] = value
        if k % GROUP == 0:
            part = pl.ds(k, min(GROUP, depth - k))
            copy = pltpu.make_async_copy(out.at[:, part], out_hbm.at[:, part], sems.at[k // GROUP])
            copy.start()
            copies.append(copy)
    for copy in copies:
        copy.wait()


def on_device(
    tracers,
    east_flow,
    north_flow,
    mixing,
    depth_levels,
    atm_flux,
    source_blocks,
    target_rows,
    regrid_weights,
):
    size = lax.axis_size("lon")
    depth, lat = tracers.shape[1], tracers.shape[2]
    dma = pltpu.SemaphoreType.DMA
    band = [
        pltpu.VMEM((2, depth, 8, 128), F32),
        pltpu.VMEM((depth, 8, 128), F32),
        pltpu.VMEM((depth, 8, 128), F32),
        pltpu.VMEM((8, 128), jnp.int32),
    ]
    top, west_corner, east_corner = call(
        functools.partial(fold_kernel, depth),
        (shape(depth, 16, 128), shape(16, 128), shape(16, 128)),
        [HBM] * 4,
        [*band, dma((4,))],
        cost=cost(0.1),
        name="fold_rows",
    )(*in_hbm(tracers, east_flow, north_flow, depth_levels))
    fold = lax.ppermute(top, "lon", [(i, size - 1 - i) for i in range(size)])

    plane = shape(depth, lat, 128)
    block = [shape(2, depth, lat, 128), plane, plane, pltpu.VMEM((lat, 128), jnp.int32)]
    blocks, to_core, to_odd = call(
        functools.partial(columns_kernel, depth),
        (shape(4, 4, lat, 128), shape(4, lat, 128), shape(4, lat, 128)),
        [HBM] * 4,
        [*block, dma((5,))],
        cost=cost(0.1),
        name="edge_columns",
    )(*in_hbm(tracers, east_flow, north_flow, depth_levels))
    core = lax.ppermute(to_core, "lon", [(i, i ^ 1) for i in range(size)])
    odd = lax.ppermute(to_odd, "lon", [(i, (i + (1 if i % 2 else -1)) % size) for i in range(size)])

    (pieces,) = call(
        functools.partial(regrid_kernel, size),
        (shape(size, 4, 128),),
        [HBM, HBM, HBM],
        [
            pltpu.VMEM((2 * atm_flux.shape[1], 128, 128), F32),
            pltpu.VMEM((size, 2, 128, 128), F32),
            pltpu.VMEM(atm_flux.shape, F32),
            pltpu.SMEM((2, size), jnp.int32),
            dma((2,)),
            dma((4,)),
        ],
        cost=cost(0.1),
        name="regrid",
    )(*in_hbm(atm_flux, regrid_weights, jnp.transpose(source_blocks[0])))
    received = lax.all_to_all(pieces, "lon", split_axis=0, concat_axis=0, tiled=True)

    inner, inverse, link, wet = call(
        functools.partial(inner_kernel, depth),
        (shape(2, depth, lat, 128), plane, shape(depth - 1, lat, 128), shape(lat, 128)),
        [HBM] * 5,
        [*block, shape(depth - 1, lat, 128), dma((depth // GROUP + 1,)), dma((2,))],
        cost=cost(0.1),
        name="inner_cells",
    )(*in_hbm(tracers, east_flow, north_flow, depth_levels, mixing))

    fold_blocks, fold_core, fold_odd = call(
        functools.partial(corners_kernel, depth, size),
        (shape(4, 16, 128), shape(16, 128), shape(16, 128)),
        [VMEM] * 3,
        cost=cost(0.1),
        name="fold_corners",
    )(*in_vmem(fold, west_corner, east_corner))
    fold_core = lax.ppermute(fold_core, "lon", [(i, i ^ 1) for i in range(size)])
    near = [(i, i + (1 if i % 2 else -1)) for i in range(1, size - 1)]
    fold_odd = lax.ppermute(fold_odd, "lon", [(0, 0), *near, (size - 1, size - 1)])

    (strip,) = call(
        functools.partial(strip_kernel, depth),
        (shape(2, depth, 8, 128),),
        [HBM] * 4 + [VMEM],
        [*band, dma((4,))],
        cost=cost(0.1),
        name="top_strip",
    )(*in_hbm(tracers, east_flow, north_flow, depth_levels), *in_vmem(fold))

    (result,) = call(
        functools.partial(last_kernel, depth),
        (jax.ShapeDtypeStruct((2, depth, lat, 128), F32),),
        [VMEM] * 12 + [HBM],
        [
            pltpu.VMEM((2, 2, lat, 128), F32),
            pltpu.VMEM((2, depth, lat, 128), F32),
            pltpu.SMEM((2, size), jnp.int32),
            dma((-(-depth // GROUP),)),
            dma((1,)),
        ],
        out_specs=[HBM],
        cost=cost(0.1),
        name="edges_and_columns",
    )(
        *in_vmem(strip, wet, inner, inverse, link, blocks, core, odd, fold_blocks, fold_core, fold_odd, received),
        *in_hbm(jnp.transpose(target_rows[:, 0, :])),
    )
    return result


def solution(mesh):
    return jax.shard_map(
        on_device,
        mesh=mesh,
        in_specs=(
            P(None, "ens", None, "lon"),
            P("ens", None, "lon"),
            P("ens", None, "lon"),
            P("ens", None, "lon"),
            P(None, "lon"),
            P("ens", "lon", None),
            P("lon", None, None),
            P(None, "lon", None),
            P("lon", None, None, None, None),
        ),
        out_specs=P(None, "ens", None, "lon"),
        check_vma=False,
    )
```

time: 167 us -> 33.1 us (0.20)
  the two profiles are of different devices: /device:TPU:0 before, /device:TPU:1 now
where the time goes in v1:
time: 33.1 us; the launch traced here: 32.8 us
  Pallas kernels  17 us (51%)
  starting transfers between devices  15.7 us (47%)
    ppermute x1, starting transfers between devices, on_device(): fold = lax.ppermute(top, 'lon', [(i, size - 1 - i) for i in range(size)])  5.73 us
    all_to_all x1, starting transfers between devices, on_device(): lax.all_to_all(pieces, 'lon', split_axis=0, concat_axis=0, tiled=True)  5.63 us
    pallas_call x1, Pallas kernels, on_device(): call(functools.partial(inner_kernel, depth), (shape(2, depth, lat, 128),...  4.88 us
    ppermute x1, starting transfers between devices, on_device(): lax.ppermute(fold_odd, 'lon', [(0, 0), *near, (size - 1, size - 1)])  3.57 us
    pallas_call x1, Pallas kernels, on_device(): call(functools.partial(strip_kernel, depth), (shape(2, depth, 8, 128),),...  3.03 us
    pallas_call x1, Pallas kernels, on_device(): call(functools.partial(regrid_kernel, size), (shape(size, 4, 128),), [HBM...  2.67 us
    pallas_call x1, Pallas kernels, on_device(): call(functools.partial(columns_kernel, depth), (shape(4, 4, lat, 128), sh...  2.4 us
    pallas_call x1, Pallas kernels, on_device(): call(functools.partial(last_kernel, depth), (jax.ShapeDtypeStruct((2, dep...  2.35 us
  transfers between devices with their start and end apart: 6, of which 0 were waited for; matrix products, arithmetic and copies ran while one was open for 0% of the time, Pallas kernels for 40%

profile of v1, /device:TPU:1, one launch (start us, length us, event | category | flops | bytes accessed | tf_op | source)
XLA Modules:
  0.0 32.8 jit_solution(14823513263250980097)
XLA Ops:
  0.0 1.4 %fold_rows.1 = (f32[25,16,128]{2,1,0:T(8,128)S(1)}, f32[16,128]{1,0:T(8,128)S(1)}, f32[16,128]{1,0:T(8,128)S(1)}) custom-call(f32[2,25,32,128]{3,2,1,0:T(8,128)} %t_hbm.7, f32[25,32,128]{2,1,0:T(8,128)} %e_hbm.7, f32[25,32,128]{2,1,0:T(8,128)} %n_hbm.7, s32[32,128]{1,0:T(8,128)} %d_hbm.7), custom_call_target="tpu_custom_call" | custom-call | bytes 300000 | tf_op jit(solution)/shard_map/fold_rows/pallas_call | solution.py:615
  1.4 5.7 %collective-permute-start = (f32[25,16,128]{2,1,0:T(8,128)S(1)}, f32[25,16,128]{2,1,0:T(8,128)S(1)}, u32[]{:S(2)}, u32[]{:S(2)}) collective-permute-start(f32[25,16,128]{2,1,0:T(8,128)S(1)} %get-tuple-element.18), channel_id=1, source_target_pairs={{0,15},{1,14},{2,13},{3,12},{4,11},{5,10},{6,9},{7,8},{8,7},{9,6},... | collective-permute-start | bytes 614408 | tf_op jit(solution)/shard_map/ppermute | solution.py:623
  7.2 2.4 %edge_columns.1 = (f32[4,4,32,128]{3,2,1,0:T(8,128)S(1)}, f32[4,32,128]{2,1,0:T(8,128)S(1)}, f32[4,32,128]{2,1,0:T(8,128)S(1)}) custom-call(f32[2,25,32,128]{3,2,1,0:T(8,128)} %t_hbm.7, f32[25,32,128]{2,1,0:T(8,128)} %e_hbm.7, f32[25,32,128]{2,1,0:T(8,128)} %n_hbm.7, s32[32,128]{1,0:T(8,128)} %d_hbm.7), custom_call_target="tpu_custom_call" | custom-call | bytes 300000 | tf_op jit(solution)/shard_map/edge_columns/pallas_call | solution.py:627
  9.6 0.1 collective-permute-start.1
  9.6 0.6 %collective-permute-start.2 = (f32[4,32,128]{2,1,0:T(8,128)S(1)}, f32[4,32,128]{2,1,0:T(8,128)S(1)}, u32[]{:S(2)}, u32[]{:S(2)}) collective-permute-start(f32[4,32,128]{2,1,0:T(8,128)S(1)} %get-tuple-element.25), channel_id=1, source_target_pairs={{0,15},{1,2},{2,1},{3,4},{4,3},{5,6},{6,5},{7,8},{8,7},{9,10},{10,... | collective-permute-start | bytes 196616 | tf_op jit(solution)/shard_map/ppermute | solution.py:636
  10.3 2.7 %regrid.1 = f32[16,4,128]{2,1,0:T(4,128)} custom-call(f32[2,8,128]{2,1,0:T(8,128)} %atm_hbm.1, f32[1,16,2,128,128]{4,3,2,1,0:T(8,128)} %w_hbm.1, s32[2,16]{1,0:T(2,128)} %bitcast.6), custom_call_target="tpu_custom_call" | custom-call | bytes 300000 | tf_op jit(solution)/shard_map/regrid/pallas_call | solution.py:638
  12.9 5.6 %all-to-all-start = ((f32[16,4,128]{2,1,0:T(4,128)}), f32[16,4,128]{2,1,0:T(4,128)S(1)}, u32[]{:S(2)}, u32[]{:S(2)}) async-start(f32[16,4,128]{2,1,0:T(4,128)} %regrid.1), calls=%async_computation | async-start | bytes 65536 | tf_op jit(solution)/shard_map/all_to_all | solution.py:653
  18.6 0.0 collective-permute-done.fold
  18.6 0.3 fold_corners.1
  18.8 0.1 collective-permute-start.3
  18.9 3.6 %collective-permute-start.4 = (f32[16,128]{1,0:T(8,128)S(1)}, f32[16,128]{1,0:T(8,128)S(1)}, u32[]{:S(2)}, u32[]{:S(2)}) collective-permute-start(f32[16,128]{1,0:T(8,128)S(1)} %get-tuple-element.30), channel_id=1, source_target_pairs={{0,0},{1,2},{2,1},{3,4},{4,3},{5,6},{6,5},{7,8},{8,7},{9,10},{10,9... | collective-permute-start | bytes 24584 | tf_op jit(solution)/shard_map/ppermute | solution.py:673
  22.5 4.9 %inner_cells.1 = (f32[2,25,32,128]{3,2,1,0:T(8,128)S(1)}, f32[25,32,128]{2,1,0:T(8,128)S(1)}, f32[24,32,128]{2,1,0:T(8,128)S(1)}, f32[32,128]{1,0:T(8,128)S(1)}) custom-call(f32[2,25,32,128]{3,2,1,0:T(8,128)} %t_hbm.7, f32[25,32,128]{2,1,0:T(8,128)} %e_hbm.7, f32[25,32,128]{2,1,0:T(8,128)} %n_hbm.7, s32[32,128]{1,0:T(8,128)} %d_hbm.7, f32[24,32,128]{2,1,0:T(8,128)} %mix_hbm.1), custom_call_target="tpu_custom_call" | custom-call | bytes 300000 | tf_op jit(solution)/shard_map/inner_cells/pallas_call | solution.py:655
  27.4 3.0 %top_strip.1.strip = f32[2,25,8,128]{3,2,1,0:T(8,128)S(1)} custom-call(f32[2,25,32,128]{3,2,1,0:T(8,128)} %t_hbm.7, f32[25,32,128]{2,1,0:T(8,128)} %e_hbm.7, f32[25,32,128]{2,1,0:T(8,128)} %n_hbm.7, s32[32,128]{1,0:T(8,128)} %d_hbm.7, f32[25,16,128]{2,1,0:T(8,128)S(1)} %collective-permute-done.fold), custom_call_target="tpu_custom_call" | custom-call | bytes 300000 | tf_op jit(solution)/shard_map/top_strip/pallas_call | solution.py:675
  30.5 0.0 all-to-all-done.pieces
  30.5 0.0 collective-permute-done.1.core
  30.5 0.0 collective-permute-done.2.odd
  30.5 0.0 collective-permute-done.3.fold_core
  30.5 0.0 collective-permute-done.4.fold_odd
  30.5 2.3 %edges_and_columns.1 = f32[2,25,32,128]{3,2,1,0:T(8,128)} custom-call(f32[2,25,8,128]{3,2,1,0:T(8,128)S(1)} %top_strip.1.strip, f32[32,128]{1,0:T(8,128)S(1)} %get-tuple-element.19.wet, f32[2,25,32,128]{3,2,1,0:T(8,128)S(1)} %get-tuple-element.20.inner, f32[25,32,128]{2,1,0:T(8,128)S(1)} %get-tuple-element.21.inverse, ...), custom_call_target="tpu_custom_call" | custom-call | bytes 300000 | tf_op jit(solution)/shard_map/edges_and_columns/pallas_call | solution.py:684
Async XLA Ops:
  1.4 17.1 %collective-permute-start = (f32[25,16,128]{2,1,0:T(8,128)S(1)}, f32[25,16,128]{2,1,0:T(8,128)S(1)}, u32[]{:S(2)}, u32[]{:S(2)}) collective-permute-start(f32[25,16,128]{2,1,0:T(8,128)S(1)} %get-tuple-element.18), channel_id=1, source_target_pairs={{0,15},{1,14},{2,13},{3,12},{4,11},{5,10},{6,9},{7,8},{8,7},{9,6},... | collective-permute-start | bytes 614408 | tf_op jit(solution)/shard_map/ppermute | solution.py:623
  9.6 20.9 %collective-permute-start.1 = (f32[4,32,128]{2,1,0:T(8,128)S(1)}, f32[4,32,128]{2,1,0:T(8,128)S(1)}, u32[]{:S(2)}, u32[]{:S(2)}) collective-permute-start(f32[4,32,128]{2,1,0:T(8,128)S(1)} %get-tuple-element.24), channel_id=1, source_target_pairs={{0,1},{1,0},{2,3},{3,2},{4,5},{5,4},{6,7},{7,6},{8,9},{9,8},{10,11... | collective-permute-start | bytes 196616 | tf_op jit(solution)/shard_map/ppermute | solution.py:635
  9.6 20.8 %collective-permute-start.2 = (f32[4,32,128]{2,1,0:T(8,128)S(1)}, f32[4,32,128]{2,1,0:T(8,128)S(1)}, u32[]{:S(2)}, u32[]{:S(2)}) collective-permute-start(f32[4,32,128]{2,1,0:T(8,128)S(1)} %get-tuple-element.25), channel_id=1, source_target_pairs={{0,15},{1,2},{2,1},{3,4},{4,3},{5,6},{6,5},{7,8},{8,7},{9,10},{10,... | collective-permute-start | bytes 196616 | tf_op jit(solution)/shard_map/ppermute | solution.py:636
  12.9 17.5 %all-to-all-start = ((f32[16,4,128]{2,1,0:T(4,128)}), f32[16,4,128]{2,1,0:T(4,128)S(1)}, u32[]{:S(2)}, u32[]{:S(2)}) async-start(f32[16,4,128]{2,1,0:T(4,128)} %regrid.1), calls=%async_computation | async-start | bytes 65536 | tf_op jit(solution)/shard_map/all_to_all | solution.py:653
  18.8 11.7 %collective-permute-start.3 = (f32[16,128]{1,0:T(8,128)S(1)}, f32[16,128]{1,0:T(8,128)S(1)}, u32[]{:S(2)}, u32[]{:S(2)}) collective-permute-start(f32[16,128]{1,0:T(8,128)S(1)} %get-tuple-element.29), channel_id=1, source_target_pairs={{0,1},{1,0},{2,3},{3,2},{4,5},{5,4},{6,7},{7,6},{8,9},{9,8},{10,11... | collective-permute-start | bytes 24584 | tf_op jit(solution)/shard_map/ppermute | solution.py:671
  18.9 11.5 %collective-permute-start.4 = (f32[16,128]{1,0:T(8,128)S(1)}, f32[16,128]{1,0:T(8,128)S(1)}, u32[]{:S(2)}, u32[]{:S(2)}) collective-permute-start(f32[16,128]{1,0:T(8,128)S(1)} %get-tuple-element.30), channel_id=1, source_target_pairs={{0,0},{1,2},{2,1},{3,4},{4,3},{5,6},{6,5},{7,8},{8,7},{9,10},{10,9... | collective-permute-start | bytes 24584 | tf_op jit(solution)/shard_map/ppermute | solution.py:673

commit v2 on v1

v2 whole, which is shorter than its diff:
```python
import functools

import jax
import jax.numpy as jnp
from jax import lax
from jax.experimental import pallas as pl
from jax.experimental.pallas import tpu as pltpu
from jax.sharding import PartitionSpec as P

SUB = 4
DIFFUSION = 0.12
FLUX_GAIN = 0.5
GROUP = 5
PART = 13
F32 = jnp.float32
VMEM = pl.BlockSpec(memory_space=pltpu.VMEM)
SMEM = pl.BlockSpec(memory_space=pltpu.SMEM)
HBM = pl.BlockSpec(memory_space=pltpu.HBM)
VMEM_LIMIT = 16 * 1024 * 1024


def lane_index():
    return lax.broadcasted_iota(jnp.int32, (8, 128), 1)


def row_index():
    return lax.broadcasted_iota(jnp.int32, (8, 128), 0)


def lanes(tile, shift):
    shift = shift % 128
    return pltpu.roll(tile, shift, 1) if shift else tile


def rows(tile, shift):
    shift = shift % 8
    return pltpu.roll(tile, shift, 0) if shift else tile


def take(tile, index):
    return jnp.take_along_axis(tile, index, axis=1)


def spread_order():
    lane = lane_index()
    return 4 * (lane & 31) + (lane >> 5)


def gather_order():
    lane = lane_index()
    return 32 * (lane & 3) + (lane >> 2)


def call(body, out, in_specs, scratch=(), out_specs=None, cost=None, name=None):
    return pl.pallas_call(
        body,
        out_shape=out,
        in_specs=in_specs,
        out_specs=out_specs if out_specs is not None else [VMEM] * len(out),
        scratch_shapes=list(scratch),
        compiler_params=pltpu.CompilerParams(vmem_limit_bytes=VMEM_LIMIT),
        cost_estimate=cost,
        name=name,
    )


def cost(micros):
    return pl.CostEstimate(flops=0, bytes_accessed=int(micros * 3.0e6), transcendentals=0)


def shape(*dims):
    return pltpu.VMEM(dims, F32)


def in_hbm(*arrays):
    return [pltpu.with_memory_space_constraint(x, pltpu.HBM) for x in arrays]


def in_vmem(*arrays):
    return [pltpu.with_memory_space_constraint(x, pltpu.VMEM) for x in arrays]


def face(half, open_face):
    return jnp.where(open_face, half + DIFFUSION, 0.0), jnp.where(open_face, half - DIFFUSION, 0.0)


def stencil(east, north, west, south):
    a_e, b_e = east
    a_n, b_n = north
    a_w, b_w = west
    a_s, b_s = south
    return (((1.0 - a_e) + b_w) - a_n) + b_s, b_e, a_w, b_n, a_s


def advance(weights, cell, east, west, north, south):
    own, b_e, a_w, b_n, a_s = weights
    return (own * cell + (a_w * west - b_e * east)) + (a_s * south - b_n * north)


def north_of(tiles, beyond):
    row = row_index()
    turned = [rows(t, -1) for t in tiles]
    return [jnp.where(row == 7, n, t) for t, n in zip(turned, turned[1:] + [beyond])]


def south_of(tiles):
    row = row_index()
    turned = [rows(t, 1) for t in tiles]
    return [turned[0]] + [jnp.where(row == 0, p, t) for p, t in zip(turned, turned[1:])]


def northern_rows(t_hbm, e_hbm, n_hbm, d_hbm, t, e, n, d, sems):
    top = pl.ds(t_hbm.shape[2] - 8, 8)
    return [
        pltpu.make_async_copy(t_hbm.at[:, :, top], t, sems.at[0]),
        pltpu.make_async_copy(e_hbm.at[:, top], e, sems.at[1]),
        pltpu.make_async_copy(n_hbm.at[:, top], n, sems.at[2]),
        pltpu.make_async_copy(d_hbm.at[top], d, sems.at[3]),
    ]


def fold_kernel(depth, t_hbm, e_hbm, n_hbm, d_hbm, out, west, east, t, e, n, d, sems):
    copies = northern_rows(t_hbm, e_hbm, n_hbm, d_hbm, t, e, n, d, sems)
    for copy in copies:
        copy.start()
    for copy in copies:
        copy.wait()
    row = row_index()
    turn = 127 - lane_index()
    levels = d[...].astype(F32)
    for k in range(depth):
        cells = jnp.where(row < 4, rows(t[0, k], 4), t[1, k])
        flows = jnp.where(row < 4, rows(n[k], 4), e[k])
        if k < 4:
            flows = jnp.where(row == 4, rows(levels, -k), flows)
        out[k, 0:8] = take(cells, turn)
        out[k, 8:16] = take(flows, turn)
    spans, stacks = [], []
    for half in range(2):
        span = slice(8 * half, 8 * half + 8)
        spans.append(span)
        stacks.append(stack_of(out, depth, span))
    stacks[1].append(lambda: take(levels, turn))
    for span, found in zip(spans, edge_columns(stacks)):
        east[span], west[span] = found[0], found[3]


def edge_columns(stacks):
    lane = lane_index()
    outer = (lane < 8) | (lane >= 120)
    group = [((lane >> 2) & 3) == c for c in range(3)]
    sums = [[None] * 4 for _ in stacks]
    for k in range(max(len(x) for x in stacks)):
        for total, stack in zip(sums, stacks):
            if k < len(stack):
                tile = lanes(jnp.where(outer, stack[k](), 0.0), 4 * k)
                total[k % 4] = tile if total[k % 4] is None else total[k % 4] + tile
    offsets = (0, 1, -2, -1)
    found = []
    for offset in offsets:
        for total in sums:
            a, b, c, d = [total[(g - offset) % 4] for g in range(4)]
            tile = jnp.where(group[0], a, jnp.where(group[1], b, jnp.where(group[2], c, d)))
            found.append(lanes(tile, -4 * offset))
    order = spread_order()
    found = [take(x, order) for x in found]
    return [[found[b * len(stacks) + i] for b in range(4)] for i in range(len(stacks))]


def stack_of(ref, depth, *where):
    return [lambda k=k: ref[(k, *where)] for k in range(depth)]


def columns_kernel(depth, t_hbm, e_hbm, n_hbm, d_hbm, blocks, to_core, to_odd, t, e, n, d, sems):
    copies = [
        pltpu.make_async_copy(d_hbm, d, sems.at[4]),
        pltpu.make_async_copy(t_hbm.at[0], t.at[0], sems.at[0]),
        pltpu.make_async_copy(t_hbm.at[1], t.at[1], sems.at[1]),
        pltpu.make_async_copy(e_hbm, e, sems.at[2]),
        pltpu.make_async_copy(n_hbm, n, sems.at[3]),
    ]
    for copy in copies:
        copy.start()
    even = lax.rem(lax.axis_index("lon"), 2) == 0
    count = t.shape[2] // 8
    copies[0].wait()
    spans = [slice(8 * j, 8 * j + 8) for j in range(count)]
    fields = (t.at[0], t.at[1], e, n)
    for pair in ((0, 1), (2, 3)):
        for f in pair:
            copies[f + 1].wait()
        places = [(f, span) for f in pair for span in spans]
        stacks = [stack_of(fields[f], depth, span) for f, span in places]
        if 0 in pair:
            for stack, span in zip(stacks, spans):
                stack.append(lambda span=span: d[span].astype(F32))
        for (f, span), found in zip(places, edge_columns(stacks)):
            for b, tile in enumerate(found):
                blocks[b, f, span] = tile
            w1, e1 = found[0], found[3]
            to_core[f, span] = jnp.where(even, e1, w1)
            to_odd[f, span] = jnp.where(even, w1, e1)


def regrid_kernel(size, atm_hbm, w_hbm, src_hbm, out, wide, w, part, atm, src, sems, w_sems):
    first = [pltpu.make_async_copy(atm_hbm, atm, sems.at[0]), pltpu.make_async_copy(src_hbm, src, sems.at[1])]
    for copy in first:
        copy.start()
    parts = w_sems.shape[0]
    each = size // parts
    weights = [
        pltpu.make_async_copy(w_hbm.at[0, pl.ds(p * each, each)], w.at[pl.ds(p * each, each)], w_sems.at[p])
        for p in range(parts)
    ]
    for copy in weights:
        copy.start()
    for copy in first:
        copy.wait()
    flat = atm[...].reshape(atm.shape[0] * atm.shape[1], atm.shape[2])
    count = flat.shape[0]
    blocks = atm.shape[1]
    columns = jnp.transpose(jnp.concatenate([flat, jnp.zeros((128 - count, 128), F32)], axis=0))
    for c in range(count):
        wide[c] = jnp.broadcast_to(columns[:, c : c + 1], (128, 128))
    def owner(e, carry):
        for s in range(2):
            block = src[s, e]
            sums = [None, None]
            for i in range(16):
                span = slice(8 * i, 8 * i + 8)
                weight = w[e, s, span]
                for f in range(2):
                    term = weight * wide[f * blocks + block, span]
                    sums[f] = term if sums[f] is None else sums[f] + term
            for f in range(2):
                part[e, 2 * f + s] = sums[f]
        return carry

    for p in range(parts):
        weights[p].wait()
        lax.fori_loop(p * each, (p + 1) * each, owner, 0, unroll=4)

    def pair(e, carry):
        out[e] = totals([part[2 * e + i // 4, i % 4] for i in range(8)])
        return carry

    lax.fori_loop(0, size // 2, pair, 0, unroll=8)


def totals(tiles):
    row = row_index()
    for step in (4, 2, 1):
        low = (row & step) == 0
        half = len(tiles) // 2
        merged = []
        for a, b in zip(tiles[:half], tiles[half:]):
            kept, moved = jnp.where(low, a, b), jnp.where(low, b, a)
            if step == 4:
                turned = rows(moved, 4)
            else:
                turned = jnp.where(low, rows(moved, -step), rows(moved, step))
            merged.append(kept + turned)
        tiles = merged
    return tiles[0]


def inner_kernel(
    depth, t_hbm, e_hbm, n_hbm, d_hbm, mix_hbm, fold, out, surface_wet, columns,
    t, e, n, d, mix, weights, folded, over, sems, flow_sems, cell_sems,
):
    levels = pltpu.make_async_copy(d_hbm, d, sems.at[0])
    mixing = pltpu.make_async_copy(mix_hbm, mix, sems.at[1])
    parts = [pl.ds(k, min(PART, depth - k)) for k in range(0, depth, PART)]
    flows = [
        (
            pltpu.make_async_copy(e_hbm.at[p], e.at[p], flow_sems.at[0, i]),
            pltpu.make_async_copy(n_hbm.at[p], n.at[p], flow_sems.at[1, i]),
        )
        for i, p in enumerate(parts)
    ]
    cells = [pltpu.make_async_copy(t_hbm.at[:, p], t.at[:, p], cell_sems.at[i]) for i, p in enumerate(parts)]
    levels.start()
    for pair in flows:
        for copy in pair:
            copy.start()
    for copy in cells:
        copy.start()
    mixing.start()
    levels.wait()
    row = row_index()
    count = t.shape[2] // 8
    spans = [slice(8 * j, 8 * j + 8) for j in range(count)]
    deep = [d[s].astype(F32) for s in spans]
    fold_deep = fold_levels(fold)

    def plus(tiles):
        return [lanes(x, 1) for x in tiles]

    def minus(tiles):
        return [lanes(x, -1) for x in tiles]

    over_faces = fold_faces([fold_deep], [deep[-1]], plus, minus)
    east_faces = [jnp.minimum(x, y) for x, y in zip(deep, minus(deep))]
    faces = list(zip(east_faces, plus(east_faces), block_faces(deep, fold_deep)))

    def fold_coefficients(levels):
        found = fold_weights(
            [fold[k, 8:16] for k in levels], over_faces * len(levels), [float(k) for k in levels], minus
        )
        for k, tiles in zip(levels, found):
            for i, x in enumerate(tiles):
                over[i, k] = x

    def coefficients(k):
        e_half = [0.5 * e[k, s] for s in spans]
        n_half = [0.5 * n[k, s] for s in spans]
        for s, he, hw, hn, hs, (east, west, (north, south)) in zip(
            spans, e_half, plus(e_half), n_half, south_of(n_half), faces
        ):
            found = stencil(
                face(he, east > float(k)),
                face(hn, north > float(k)),
                face(hw, west > float(k)),
                face(hs, south > float(k)),
            )
            for i, x in enumerate(found):
                weights[i, k, s] = x

    def substep(k, step):
        source = out if step else t
        state = [[source[f, k, s] for s in spans] for f in range(2)]
        cells = folded[k] if step else fold[k, 0:8]
        beyond = (rows(cells, 4), cells)
        for f in range(2):
            up, down = north_of(state[f], beyond[f]), south_of(state[f])
            for s, c, u, v in zip(spans, state[f], up, down):
                w = [weights[i, k, s] for i in range(5)]
                out[f, k, s] = advance(w, c, lanes(c, -1), lanes(c, 1), u, v)
        if step < SUB - 1:
            up = fold_north(cells, state[0][-1], state[1][-1])
            w = [over[i, k] for i in range(5)]
            folded[k] = advance(w, cells, lanes(cells, 1), lanes(cells, -1), up, rows(cells, 1))

    zero = jnp.zeros((8, 128), F32)
    above, ratio = [zero] * count, [zero] * count

    def pivots(k):
        for j, s in enumerate(spans):
            link = jnp.where(deep[j] > float(k + 1), mix[k, s], 0.0) if k < depth - 1 else zero
            inv = 1.0 / (1.0 + above[j] + link + above[j] * ratio[j])
            columns[0, k, s] = inv
            columns[1, k, s] = link
            above[j], ratio[j] = link, -link * inv

    for s, x in zip(spans, deep):
        surface_wet[s] = jnp.where(x > 0.0, 1.0, 0.0)
    for k in range(0, depth, GROUP):
        fold_coefficients(range(k, min(k + GROUP, depth)))
    for k in range(depth):
        if k % PART == 0:
            for copy in flows[k // PART]:
                copy.wait()
        coefficients(k)
    for k in range(depth):
        if k % PART == 0:
            cells[k // PART].wait()
        substep(k, 0)
    mixing.wait()
    for step in range(1, SUB):
        for k in range(depth):
            substep(k, step)
            if step == 1:
                pivots(k)


def fold_faces(deep, own_deep, toward_east, toward_west):
    easts = [jnp.minimum(x, y) for x, y in zip(deep, toward_east(deep))]
    norths = [jnp.minimum(x, fold_north(x, y, y)) for x, y in zip(deep, own_deep)]
    return list(zip(easts, toward_west(easts), norths, [rows(x, 1) for x in norths]))


def fold_weights(flows, faces, levels, toward_west):
    row = row_index()
    turned = [rows(x, 4) for x in flows]
    e_half = [0.5 * jnp.where(row < 4, y, x) for x, y in zip(flows, turned)]
    n_half = [0.5 * jnp.where(row < 4, x, y) for x, y in zip(flows, turned)]
    w_half = toward_west(e_half)
    s_half = [rows(x, 1) for x in n_half]
    return [
        stencil(face(e, east > k), face(n, north > k), face(w, west > k), face(s, south > k))
        for e, n, w, s, (east, west, north, south), k in zip(e_half, n_half, w_half, s_half, faces, levels)
    ]


def block_faces(deep, beyond):
    norths = [jnp.minimum(x, y) for x, y in zip(deep, north_of(deep, beyond))]
    souths = south_of(norths)
    souths[0] = jnp.where(row_index() == 0, 0.0, souths[0])
    return list(zip(norths, souths))


def fold_north(fold, first, second):
    row = row_index()
    return jnp.where((row & 3) == 3, jnp.where(row < 4, rows(first, 4), second), rows(fold, -1))


def fold_levels(fold):
    row = row_index()
    deep = jnp.zeros((8, 128), F32)
    for r in range(4):
        deep = jnp.where((row & 3) == r, jnp.broadcast_to(fold[r, 12:13], (8, 128)), deep)
    return deep


def corners_kernel(depth, size, fold, west, east, blocks, to_core, to_odd):
    me = lax.axis_index("lon")
    even = lax.rem(me, 2) == 0
    spans = [slice(0, 8), slice(8, 16)]
    stacks = [stack_of(fold, depth, span) for span in spans]
    stacks[1].append(lambda: fold_levels(fold))
    for span, found in zip(spans, edge_columns(stacks)):
        for b, tile in enumerate(found):
            blocks[b, span] = tile
        w1, e1 = found[0], found[3]
        to_core[span] = jnp.where(even, e1, w1)
        odd = jnp.where(even, w1, e1)
        odd = jnp.where(me == 0, west[span], odd)
        to_odd[span] = jnp.where(me == size - 1, east[span], odd)


def edge_side(depth, rows_count, cells, flows, fold_cells, fold_flows):
    lane, row = lane_index(), row_index()
    level = (lane & 31).astype(F32)
    count = rows_count // 8

    def plus(tiles):
        turned = [lanes(x, 32) for x in tiles]
        return [turned[0]] + [jnp.where(lane < 32, p, x) for p, x in zip(turned, turned[1:])]

    def minus(tiles):
        turned = [lanes(x, -32) for x in tiles]
        return [jnp.where(lane >= 96, q, x) for x, q in zip(turned, turned[1:])] + [turned[2]]

    at_levels = (lane & 96) + depth
    deep = [[take(cells[b][0][j], at_levels) for j in range(count)] for b in range(3)]
    fold_deep = []
    for b in range(3):
        found = take(fold_flows[b], at_levels)
        fold_deep.append(jnp.where(row < 4, rows(found, 4), found))
    over_faces = fold_faces(fold_deep, [deep[b][-1] for b in range(3)], plus, minus)
    over = fold_weights(fold_flows, over_faces, [level] * 3, minus)

    weights = [[None] * count for _ in range(3)]
    meridional = [block_faces(deep[b], fold_deep[b]) for b in range(3)]
    halves = [[0.5 * x for x in flows[b][1]] for b in range(3)]
    southern = [south_of(x) for x in halves]
    for j in range(count):
        line = [deep[b][j] for b in range(3)]
        easts = [jnp.minimum(x, y) for x, y in zip(line, minus(line))]
        e_half = [0.5 * flows[b][0][j] for b in range(3)]
        for b, (east, west, he, hw) in enumerate(zip(easts, plus(easts), e_half, plus(e_half))):
            north, south = meridional[b][j]
            weights[b][j] = stencil(
                face(he, east > level),
                face(halves[b][j], north > level),
                face(hw, west > level),
                face(southern[b][j], south > level),
            )

    state = [[list(cells[b][f]) for f in range(2)] for b in range(3)]
    folded = list(fold_cells)
    for step in range(SUB):
        fold_east, fold_west = plus(folded), minus(folded)
        following = [[[None] * count for _ in range(2)] for _ in range(3)]
        for f in range(2):
            for j in range(count):
                line = [state[b][f][j] for b in range(3)]
                east, west = minus(line), plus(line)
                for b in range(3):
                    following[b][f][j] = (east[b], west[b])
        next_fold = []
        for b in range(3):
            up = fold_north(folded[b], state[b][0][-1], state[b][1][-1])
            next_fold.append(
                advance(over[b], folded[b], fold_east[b], fold_west[b], up, rows(folded[b], 1))
            )
        for b in range(3):
            beyond = (rows(folded[b], 4), folded[b])
            for f in range(2):
                tiles = state[b][f]
                up, down = north_of(tiles, beyond[f]), south_of(tiles)
                state[b][f] = [
                    advance(weights[b][j], tiles[j], *following[b][f][j], up[j], down[j]) for j in range(count)
                ]
        folded = next_fold
    return state[1]


def last_kernel(
    depth, wet, inner, blocks, core, odd, fold, fold_core, fold_odd, pieces, columns, target_hbm,
    out_hbm, merged, out, target, sems, other,
):
    targets = pltpu.make_async_copy(target_hbm, target, other.at[0])
    targets.start()
    lane, row = lane_index(), row_index()
    size = pieces.shape[0]
    rows_count = inner.shape[2]
    count = rows_count // 8
    spans = [slice(8 * j, 8 * j + 8) for j in range(count)]
    me = lax.axis_index("lon")
    even = lax.rem(me, 2) == 0

    def received(f, s, west):
        a, b = core[f, s], odd[f, s]
        return jnp.where(even, b, a) if west else jnp.where(even, a, b)

    def own(b, f, s):
        return blocks[b, f, s]

    sides = []
    for west in (True, False):
        near, far = (0, 1) if west else (3, 2)
        here = [[[own(b, f, s) for s in spans] for f in range(4)] for b in (near, far)]
        there = [[received(f, s, west) for s in spans] for f in range(4)]
        a, b = fold_core[...], fold_odd[...]
        letter = jnp.where(even, b, a) if west else jnp.where(even, a, b)
        line = [there, here[0], here[1]] if west else [here[1], here[0], there]
        cells_near = [fold[near, 0:8], fold[far, 0:8]]
        flows_near = [fold[near, 8:16], fold[far, 8:16]]
        if west:
            fold_cells = [letter[0:8]] + cells_near
            fold_flows = [letter[8:16]] + flows_near
        else:
            fold_cells = cells_near[::-1] + [letter[0:8]]
            fold_flows = flows_near[::-1] + [letter[8:16]]
        sides.append(
            edge_side(depth, rows_count, [x[0:2] for x in line], [x[2:4] for x in line], fold_cells, fold_flows)
        )

    order = gather_order()
    group_even = ((lane >> 2) & 1) == 0
    for f in range(2):
        for j, s in enumerate(spans):
            a = take(sides[0][f][j], order)
            b = lanes(take(sides[1][f][j], order), -4)
            merged[0, f, s] = jnp.where(group_even, a, b)
            merged[1, f, s] = jnp.where(group_even, b, a)

    surface = [[jnp.zeros((8, 128), F32) for _ in spans] for _ in range(2)]
    targets.wait()
    for a in range(size):
        for s in range(2):
            goal = target[s, a]
            hits = [row + 8 * j == goal for j in range(count)]
            for f in range(2):
                piece = jnp.broadcast_to(pieces[a, 2 * f + s : 2 * f + s + 1], (8, 128))
                surface[f] = [x + jnp.where(hit, piece, 0.0) for x, hit in zip(surface[f], hits)]

    outer = (lane < 4) | (lane >= 124)
    partial_value = [[None] * count for _ in range(2)]
    for k in range(depth):
        for f in range(2):
            for j, s in enumerate(spans):
                cell = inner[f, k, s]
                cell = jnp.where(outer, lanes(merged[k % 2, f, s], -4 * k), cell)
                if k == 0:
                    cell = cell + FLUX_GAIN * surface[f][j] * wet[s]
                else:
                    cell = cell + columns[1, k - 1, s] * partial_value[f][j]
                value = cell * columns[0, k, s]
                partial_value[f][j] = value
                out[f, k, s] = value
    copies = []
    for k in range(depth - 1, -1, -1):
        if k < depth - 1:
            for f in range(2):
                for j, s in enumerate(spans):
                    value = out[f, k, s] + columns[1, k, s] * columns[0, k, s] * partial_value[f][j]
                    partial_value[f][j] = value
                    out[f, k, s] = value
        if k % GROUP == 0:
            part = pl.ds(k, min(GROUP, depth - k))
            copy = pltpu.make_async_copy(out.at[:, part], out_hbm.at[:, part], sems.at[k // GROUP])
            copy.start()
            copies.append(copy)
    for copy in copies:
        copy.wait()


def on_device(
    tracers,
    east_flow,
    north_flow,
    mixing,
    depth_levels,
    atm_flux,
    source_blocks,
    target_rows,
    regrid_weights,
):
    size = lax.axis_size("lon")
    depth, lat = tracers.shape[1], tracers.shape[2]
    dma = pltpu.SemaphoreType.DMA
    band = [
        pltpu.VMEM((2, depth, 8, 128), F32),
        pltpu.VMEM((depth, 8, 128), F32),
        pltpu.VMEM((depth, 8, 128), F32),
        pltpu.VMEM((8, 128), jnp.int32),
    ]
    top, west_corner, east_corner = call(
        functools.partial(fold_kernel, depth),
        (shape(depth, 16, 128), shape(16, 128), shape(16, 128)),
        [HBM] * 4,
        [*band, dma((4,))],
        cost=cost(0.1),
        name="fold_rows",
    )(*in_hbm(tracers, east_flow, north_flow, depth_levels))
    fold = lax.ppermute(top, "lon", [(i, size - 1 - i) for i in range(size)])

    plane = shape(depth, lat, 128)
    block = [shape(2, depth, lat, 128), plane, plane, pltpu.VMEM((lat, 128), jnp.int32)]
    blocks, to_core, to_odd = call(
        functools.partial(columns_kernel, depth),
        (shape(4, 4, lat, 128), shape(4, lat, 128), shape(4, lat, 128)),
        [HBM] * 4,
        [*block, dma((5,))],
        cost=cost(0.1),
        name="edge_columns",
    )(*in_hbm(tracers, east_flow, north_flow, depth_levels))
    core = lax.ppermute(to_core, "lon", [(i, i ^ 1) for i in range(size)])
    odd = lax.ppermute(to_odd, "lon", [(i, (i + (1 if i % 2 else -1)) % size) for i in range(size)])

    (pieces,) = call(
        functools.partial(regrid_kernel, size),
        (shape(size // 2, 8, 128),),
        [HBM, HBM, HBM],
        [
            pltpu.VMEM((2 * atm_flux.shape[1], 128, 128), F32),
            pltpu.VMEM((size, 2, 128, 128), F32),
            pltpu.VMEM((size, 4, 8, 128), F32),
            pltpu.VMEM(atm_flux.shape, F32),
            pltpu.SMEM((2, size), jnp.int32),
            dma((2,)),
            dma((4,)),
        ],
        cost=cost(0.1),
        name="regrid",
    )(*in_hbm(atm_flux, regrid_weights, jnp.transpose(source_blocks[0])))
    pieces = pieces.reshape(size, 4, 128)
    received = lax.all_to_all(pieces, "lon", split_axis=0, concat_axis=0, tiled=True)

    fold_blocks, fold_core, fold_odd = call(
        functools.partial(corners_kernel, depth, size),
        (shape(4, 16, 128), shape(16, 128), shape(16, 128)),
        [VMEM] * 3,
        cost=cost(0.1),
        name="fold_corners",
    )(*in_vmem(fold, west_corner, east_corner))
    fold_core = lax.ppermute(fold_core, "lon", [(i, i ^ 1) for i in range(size)])
    near = [(i, i + (1 if i % 2 else -1)) for i in range(1, size - 1)]
    fold_odd = lax.ppermute(fold_odd, "lon", [(0, 0), *near, (size - 1, size - 1)])

    inner, wet, columns = call(
        functools.partial(inner_kernel, depth),
        (
            shape(2, depth, lat, 128), shape(lat, 128),
            shape(2, depth, lat, 128),
        ),
        [HBM] * 5 + [VMEM],
        [
            *block,
            shape(depth - 1, lat, 128),
            shape(5, depth, lat, 128),
            shape(depth, 8, 128),
            shape(5, depth, 8, 128),
            dma((2,)),
            dma((2, -(-depth // PART))),
            dma((-(-depth // PART),)),
        ],
        cost=cost(0.1),
        name="inner_cells",
    )(*in_hbm(tracers, east_flow, north_flow, depth_levels, mixing), *in_vmem(fold))

    (result,) = call(
        functools.partial(last_kernel, depth),
        (jax.ShapeDtypeStruct((2, depth, lat, 128), F32),),
        [VMEM] * 10 + [HBM],
        [
            pltpu.VMEM((2, 2, lat, 128), F32),
            pltpu.VMEM((2, depth, lat, 128), F32),
            pltpu.SMEM((2, size), jnp.int32),
            dma((-(-depth // GROUP),)),
            dma((1,)),
        ],
        out_specs=[HBM],
        cost=cost(0.1),
        name="edges_and_columns",
    )(
        *in_vmem(wet, inner, blocks, core, odd, fold_blocks, fold_core, fold_odd, received, columns),
        *in_hbm(jnp.transpose(target_rows[:, 0, :])),
    )
    return result


def solution(mesh):
    return jax.shard_map(
        on_device,
        mesh=mesh,
        in_specs=(
            P(None, "ens", None, "lon"),
            P("ens", None, "lon"),
            P("ens", None, "lon"),
            P("ens", None, "lon"),
            P(None, "lon"),
            P("ens", "lon", None),
            P("lon", None, None),
            P(None, "lon", None),
            P("lon", None, None, None, None),
        ),
        out_specs=P(None, "ens", None, "lon"),
        check_vma=False,
    )
```

time: 33.1 us -> 28.9 us (0.87)
  Pallas kernels: 17 us -> 12.7 us
    pallas_call x2 -> x1, Pallas kernels: 5.7 us -> 2.56 us  [on_device(): call(functools.partial(regrid_kernel, size), (shape(size // 2, 8, 128),),...]
    pallas_call x1, Pallas kernels: 4.88 us -> 3.87 us  [on_device(): call(functools.partial(inner_kernel, depth), (shape(2, depth, lat, 128),...]
    pallas_call x1, Pallas kernels: 2.4 us -> 2.06 us  [on_device(): call(functools.partial(columns_kernel, depth), (shape(4, 4, lat, 128), sh...]
  transfers between devices with their start and end apart: 6 -> 6, of which waited for: 0 -> 0; matrix products, arithmetic and copies ran while one was open for 0% -> 0% of each run, Pallas kernels for 40% -> 31%
where the time goes in v2:
time: 28.9 us; the launch traced here: 28.6 us
  starting transfers between devices  15.7 us (54%)
  Pallas kernels  12.7 us (44%)
    ppermute x1, starting transfers between devices, on_device(): fold = lax.ppermute(top, 'lon', [(i, size - 1 - i) for i in range(size)])  5.73 us
    all_to_all x1, starting transfers between devices, on_device(): lax.all_to_all(pieces, 'lon', split_axis=0, concat_axis=0, tiled=True)  5.63 us
    pallas_call x1, Pallas kernels, on_device(): call(functools.partial(inner_kernel, depth), (shape(2, depth, lat, 128),...  3.87 us
    ppermute x1, starting transfers between devices, on_device(): lax.ppermute(fold_odd, 'lon', [(0, 0), *near, (size - 1, size - 1)])  3.57 us
    pallas_call x1, Pallas kernels, on_device(): call(functools.partial(regrid_kernel, size), (shape(size // 2, 8, 128),),...  2.56 us
    pallas_call x1, Pallas kernels, on_device(): call(functools.partial(last_kernel, depth), (jax.ShapeDtypeStruct((2, dep...  2.56 us
    pallas_call x1, Pallas kernels, on_device(): call(functools.partial(columns_kernel, depth), (shape(4, 4, lat, 128), sh...  2.06 us
    pallas_call x1, Pallas kernels, on_device(): call(functools.partial(fold_kernel, depth), (shape(depth, 16, 128), shape...  1.42 us
  transfers between devices with their start and end apart: 6, of which 0 were waited for; matrix products, arithmetic and copies ran while one was open for 0% of the time, Pallas kernels for 31%

profile of v2, /device:TPU:1, one launch (start us, length us, event | category | flops | bytes accessed | tf_op | source)
XLA Modules:
  0.0 28.6 jit_solution(16974966576550556712)
XLA Ops:
  0.0 1.4 %fold_rows.1 = (f32[25,16,128]{2,1,0:T(8,128)S(1)}, f32[16,128]{1,0:T(8,128)S(1)}, f32[16,128]{1,0:T(8,128)S(1)}) custom-call(f32[2,25,32,128]{3,2,1,0:T(8,128)} %t_hbm.5, f32[25,32,128]{2,1,0:T(8,128)} %e_hbm.5, f32[25,32,128]{2,1,0:T(8,128)} %n_hbm.5, s32[32,128]{1,0:T(8,128)} %d_hbm.5), custom_call_target="tpu_custom_call" | custom-call | bytes 300000 | tf_op jit(solution)/shard_map/fold_rows/pallas_call | solution.py:610
  1.4 5.7 %collective-permute-start = (f32[25,16,128]{2,1,0:T(8,128)S(1)}, f32[25,16,128]{2,1,0:T(8,128)S(1)}, u32[]{:S(2)}, u32[]{:S(2)}) collective-permute-start(f32[25,16,128]{2,1,0:T(8,128)S(1)} %get-tuple-element.17), channel_id=1, source_target_pairs={{0,15},{1,14},{2,13},{3,12},{4,11},{5,10},{6,9},{7,8},{8,7},{9,6},... | collective-permute-start | bytes 614408 | tf_op jit(solution)/shard_map/ppermute | solution.py:618
  7.2 2.1 %edge_columns.1 = (f32[4,4,32,128]{3,2,1,0:T(8,128)S(1)}, f32[4,32,128]{2,1,0:T(8,128)S(1)}, f32[4,32,128]{2,1,0:T(8,128)S(1)}) custom-call(f32[2,25,32,128]{3,2,1,0:T(8,128)} %t_hbm.5, f32[25,32,128]{2,1,0:T(8,128)} %e_hbm.5, f32[25,32,128]{2,1,0:T(8,128)} %n_hbm.5, s32[32,128]{1,0:T(8,128)} %d_hbm.5), custom_call_target="tpu_custom_call" | custom-call | bytes 300000 | tf_op jit(solution)/shard_map/edge_columns/pallas_call | solution.py:622
  9.2 0.1 collective-permute-start.1
  9.3 0.6 %collective-permute-start.2 = (f32[4,32,128]{2,1,0:T(8,128)S(1)}, f32[4,32,128]{2,1,0:T(8,128)S(1)}, u32[]{:S(2)}, u32[]{:S(2)}) collective-permute-start(f32[4,32,128]{2,1,0:T(8,128)S(1)} %get-tuple-element.22), channel_id=1, source_target_pairs={{0,15},{1,2},{2,1},{3,4},{4,3},{5,6},{6,5},{7,8},{8,7},{9,10},{10,... | collective-permute-start | bytes 196616 | tf_op jit(solution)/shard_map/ppermute | solution.py:631
  9.9 2.6 %regrid.1 = f32[8,8,128]{2,1,0:T(8,128)} custom-call(f32[2,8,128]{2,1,0:T(8,128)} %atm_hbm.1, f32[1,16,2,128,128]{4,3,2,1,0:T(8,128)} %w_hbm.1, s32[2,16]{1,0:T(2,128)} %bitcast.7), custom_call_target="tpu_custom_call" | custom-call | bytes 300000 | tf_op jit(solution)/shard_map/regrid/pallas_call | solution.py:633
  12.5 5.6 %all-to-all-start = ((f32[16,4,128]{2,1,0:T(4,128)}), f32[16,4,128]{2,1,0:T(4,128)S(1)}, u32[]{:S(2)}, u32[]{:S(2)}) async-start(f32[16,4,128]{2,1,0:T(4,128)} %bitcast.2), calls=%async_computation | async-start | bytes 65536 | tf_op jit(solution)/shard_map/all_to_all | solution.py:650
  18.1 0.0 collective-permute-done.fold
  18.1 0.3 fold_corners.1
  18.4 0.1 collective-permute-start.3
  18.5 3.6 %collective-permute-start.4 = (f32[16,128]{1,0:T(8,128)S(1)}, f32[16,128]{1,0:T(8,128)S(1)}, u32[]{:S(2)}, u32[]{:S(2)}) collective-permute-start(f32[16,128]{1,0:T(8,128)S(1)} %get-tuple-element.27), channel_id=1, source_target_pairs={{0,0},{1,2},{2,1},{3,4},{4,3},{5,6},{6,5},{7,8},{8,7},{9,10},{10,9... | collective-permute-start | bytes 24584 | tf_op jit(solution)/shard_map/ppermute | solution.py:661
  22.1 3.9 %inner_cells.1 = (f32[2,25,32,128]{3,2,1,0:T(8,128)S(1)}, f32[32,128]{1,0:T(8,128)S(1)}, f32[2,25,32,128]{3,2,1,0:T(8,128)S(1)}) custom-call(f32[2,25,32,128]{3,2,1,0:T(8,128)} %t_hbm.5, f32[25,32,128]{2,1,0:T(8,128)} %e_hbm.5, f32[25,32,128]{2,1,0:T(8,128)} %n_hbm.5, s32[32,128]{1,0:T(8,128)} %d_hbm.5, f32[24,32,128]{2,1,0:T(8,128)} %mix_hbm.1, ...), custom_call_target="tpu_custom_call" | custom-call | bytes 300000 | tf_op jit(solution)/shard_map/inner_cells/pallas_call | solution.py:663
  26.0 0.0 all-to-all-done.pieces
  26.0 0.0 collective-permute-done.1.core
  26.0 0.0 collective-permute-done.2.odd
  26.0 0.0 collective-permute-done.3.fold_core
  26.0 0.0 collective-permute-done.4.fold_odd
  26.0 2.6 %edges_and_columns.1 = f32[2,25,32,128]{3,2,1,0:T(8,128)} custom-call(f32[32,128]{1,0:T(8,128)S(1)} %get-tuple-element.18.wet, f32[2,25,32,128]{3,2,1,0:T(8,128)S(1)} %get-tuple-element.19.inner, f32[4,4,32,128]{3,2,1,0:T(8,128)S(1)} %get-tuple-element.20.blocks, f32[4,32,128]{2,1,0:T(8,128)S(1)} %collective-permute-done.1.core, ...), custom_call_target="tpu_custom_call" | custom-call | bytes 300000 | tf_op jit(solution)/shard_map/edges_and_columns/pallas_call | solution.py:684
Async XLA Ops:
  1.4 16.7 %collective-permute-start = (f32[25,16,128]{2,1,0:T(8,128)S(1)}, f32[25,16,128]{2,1,0:T(8,128)S(1)}, u32[]{:S(2)}, u32[]{:S(2)}) collective-permute-start(f32[25,16,128]{2,1,0:T(8,128)S(1)} %get-tuple-element.17), channel_id=1, source_target_pairs={{0,15},{1,14},{2,13},{3,12},{4,11},{5,10},{6,9},{7,8},{8,7},{9,6},... | collective-permute-start | bytes 614408 | tf_op jit(solution)/shard_map/ppermute | solution.py:618
  9.2 16.7 %collective-permute-start.1 = (f32[4,32,128]{2,1,0:T(8,128)S(1)}, f32[4,32,128]{2,1,0:T(8,128)S(1)}, u32[]{:S(2)}, u32[]{:S(2)}) collective-permute-start(f32[4,32,128]{2,1,0:T(8,128)S(1)} %get-tuple-element.21), channel_id=1, source_target_pairs={{0,1},{1,0},{2,3},{3,2},{4,5},{5,4},{6,7},{7,6},{8,9},{9,8},{10,11... | collective-permute-start | bytes 196616 | tf_op jit(solution)/shard_map/ppermute | solution.py:630
  9.3 16.7 %collective-permute-start.2 = (f32[4,32,128]{2,1,0:T(8,128)S(1)}, f32[4,32,128]{2,1,0:T(8,128)S(1)}, u32[]{:S(2)}, u32[]{:S(2)}) collective-permute-start(f32[4,32,128]{2,1,0:T(8,128)S(1)} %get-tuple-element.22), channel_id=1, source_target_pairs={{0,15},{1,2},{2,1},{3,4},{4,3},{5,6},{6,5},{7,8},{8,7},{9,10},{10,... | collective-permute-start | bytes 196616 | tf_op jit(solution)/shard_map/ppermute | solution.py:631
  12.5 13.5 %all-to-all-start = ((f32[16,4,128]{2,1,0:T(4,128)}), f32[16,4,128]{2,1,0:T(4,128)S(1)}, u32[]{:S(2)}, u32[]{:S(2)}) async-start(f32[16,4,128]{2,1,0:T(4,128)} %bitcast.2), calls=%async_computation | async-start | bytes 65536 | tf_op jit(solution)/shard_map/all_to_all | solution.py:650
  18.4 7.6 %collective-permute-start.3 = (f32[16,128]{1,0:T(8,128)S(1)}, f32[16,128]{1,0:T(8,128)S(1)}, u32[]{:S(2)}, u32[]{:S(2)}) collective-permute-start(f32[16,128]{1,0:T(8,128)S(1)} %get-tuple-element.26), channel_id=1, source_target_pairs={{0,1},{1,0},{2,3},{3,2},{4,5},{5,4},{6,7},{7,6},{8,9},{9,8},{10,11... | collective-permute-start | bytes 24584 | tf_op jit(solution)/shard_map/ppermute | solution.py:659
  18.5 7.5 %collective-permute-start.4 = (f32[16,128]{1,0:T(8,128)S(1)}, f32[16,128]{1,0:T(8,128)S(1)}, u32[]{:S(2)}, u32[]{:S(2)}) collective-permute-start(f32[16,128]{1,0:T(8,128)S(1)} %get-tuple-element.27), channel_id=1, source_target_pairs={{0,0},{1,2},{2,1},{3,4},{4,3},{5,6},{6,5},{7,8},{8,7},{9,10},{10,9... | collective-permute-start | bytes 24584 | tf_op jit(solution)/shard_map/ppermute | solution.py:661

commit v3 on v2

--- a/solution.py
+++ b/solution.py
@@ -12,6 +12,7 @@
 FLUX_GAIN = 0.5
 GROUP = 5
 PART = 13
+PIECE_ROW = ((0, 4), (8, 12))
 F32 = jnp.float32
 VMEM = pl.BlockSpec(memory_space=pltpu.VMEM)
 SMEM = pl.BlockSpec(memory_space=pltpu.SMEM)
@@ -117,32 +118,6 @@
         pltpu.make_async_copy(n_hbm.at[:, top], n, sems.at[2]),
         pltpu.make_async_copy(d_hbm.at[top], d, sems.at[3]),
     ]
-
-
-def fold_kernel(depth, t_hbm, e_hbm, n_hbm, d_hbm, out, west, east, t, e, n, d, sems):
-    copies = northern_rows(t_hbm, e_hbm, n_hbm, d_hbm, t, e, n, d, sems)
-    for copy in copies:
-        copy.start()
-    for copy in copies:
-        copy.wait()
-    row = row_index()
-    turn = 127 - lane_index()
-    levels = d[...].astype(F32)
-    for k in range(depth):
-        cells = jnp.where(row < 4, rows(t[0, k], 4), t[1, k])
-        flows = jnp.where(row < 4, rows(n[k], 4), e[k])
-        if k < 4:
-            flows = jnp.where(row == 4, rows(levels, -k), flows)
-        out[k, 0:8] = take(cells, turn)
-        out[k, 8:16] = take(flows, turn)
-    spans, stacks = [], []
-    for half in range(2):
-        span = slice(8 * half, 8 * half + 8)
-        spans.append(span)
-        stacks.append(stack_of(out, depth, span))
-    stacks[1].append(lambda: take(levels, turn))
-    for span, found in zip(spans, edge_columns(stacks)):
-        east[span], west[span] = found[0], found[3]
 
 
 def edge_columns(stacks):
@@ -171,38 +146,62 @@
     return [lambda k=k: ref[(k, *where)] for k in range(depth)]
 
 
-def columns_kernel(depth, t_hbm, e_hbm, n_hbm, d_hbm, blocks, to_core, to_odd, t, e, n, d, sems):
+def pack_kernel(
+    depth, t_hbm, e_hbm, n_hbm, d_hbm, out, west, east, blocks, to_core, to_odd, t, e, n, d, sems
+):
     copies = [
-        pltpu.make_async_copy(d_hbm, d, sems.at[4]),
-        pltpu.make_async_copy(t_hbm.at[0], t.at[0], sems.at[0]),
-        pltpu.make_async_copy(t_hbm.at[1], t.at[1], sems.at[1]),
+        pltpu.make_async_copy(d_hbm, d, sems.at[0]),
+        pltpu.make_async_copy(t_hbm, t, sems.at[1]),
         pltpu.make_async_copy(e_hbm, e, sems.at[2]),
         pltpu.make_async_copy(n_hbm, n, sems.at[3]),
     ]
     for copy in copies:
         copy.start()
-    even = lax.rem(lax.axis_index("lon"), 2) == 0
+    me = lax.axis_index("lon")
+    even = lax.rem(me, 2) == 0
+    row = row_index()
+    turn = 127 - lane_index()
     count = t.shape[2] // 8
-    copies[0].wait()
     spans = [slice(8 * j, 8 * j + 8) for j in range(count)]
     fields = (t.at[0], t.at[1], e, n)
-    for pair in ((0, 1), (2, 3)):
-        for f in pair:
-            copies[f + 1].wait()
-        places = [(f, span) for f in pair for span in spans]
-        stacks = [stack_of(fields[f], depth, span) for f, span in places]
-        if 0 in pair:
+
+    def columns(chosen):
+        places = [(f, j) for f in chosen for j in range(count)]
+        stacks = [stack_of(fields[f], depth, spans[j]) for f, j in places]
+        if 0 in chosen:
             for stack, span in zip(stacks, spans):
                 stack.append(lambda span=span: d[span].astype(F32))
-        for (f, span), found in zip(places, edge_columns(stacks)):
+        for (f, j), found in zip(places, edge_columns(stacks)):
             for b, tile in enumerate(found):
-                blocks[b, f, span] = tile
+                blocks[b, f, spans[j]] = tile
             w1, e1 = found[0], found[3]
-            to_core[f, span] = jnp.where(even, e1, w1)
-            to_odd[f, span] = jnp.where(even, w1, e1)
-
-
-def regrid_kernel(size, atm_hbm, w_hbm, src_hbm, out, wide, w, part, atm, src, sems, w_sems):
+            to_core[f, spans[j]] = jnp.where(even, e1, w1)
+            to_odd[f, spans[j]] = jnp.where(even, w1, e1)
+            place = f * count + j
+            out[depth + place // 2, 8 * (place % 2) : 8 * (place % 2) + 8] = jnp.where(me == 0, w1, e1)
+
+    copies[0].wait()
+    copies[1].wait()
+    columns((0, 1))
+    copies[2].wait()
+    copies[3].wait()
+    levels = d[spans[-1]].astype(F32)
+    for k in range(depth):
+        cells = jnp.where(row < 4, rows(t[0, k, spans[-1]], 4), t[1, k, spans[-1]])
+        flows = jnp.where(row < 4, rows(n[k, spans[-1]], 4), e[k, spans[-1]])
+        if k < 4:
+            flows = jnp.where(row == 4, rows(levels, -k), flows)
+        out[k, 0:8] = take(cells, turn)
+        out[k, 8:16] = take(flows, turn)
+    columns((2, 3))
+    halves = [slice(0, 8), slice(8, 16)]
+    stacks = [stack_of(out, depth, span) for span in halves]
+    stacks[1].append(lambda: take(levels, turn))
+    for span, found in zip(halves, edge_columns(stacks)):
+        east[span], west[span] = found[0], found[3]
+
+
+def regrid_kernel(size, atm_hbm, w_hbm, src_hbm, west, east, out, wide, w, part, atm, src, sems, w_sems):
     first = [pltpu.make_async_copy(atm_hbm, atm, sems.at[0]), pltpu.make_async_copy(src_hbm, src, sems.at[1])]
     for copy in first:
         copy.start()
@@ -222,6 +221,17 @@
     columns = jnp.transpose(jnp.concatenate([flat, jnp.zeros((128 - count, 128), F32)], axis=0))
     for c in range(count):
         wide[c] = jnp.broadcast_to(columns[:, c : c + 1], (128, 128))
+    row = row_index()
+    me = lax.axis_index("lon")
+    message = west[...]
+
+    def fill(e, carry):
+        out[e] = message
+        return carry
+
+    lax.fori_loop(0, size, fill, 0, unroll=8)
+    out[lax.rem(2 * size - 2 - me, size)] = east[...]
+
     def owner(e, carry):
         for s in range(2):
             block = src[s, e]
@@ -236,37 +246,25 @@
                 part[e, 2 * f + s] = sums[f]
         return carry
 
+    def letter(e, carry):
+        for f in range(2):
+            a, b = part[e, 2 * f], part[e, 2 * f + 1]
+            tile = jnp.where(row < 4, a, b) + rows(jnp.where(row < 4, b, a), 4)
+            tile = tile + rows(tile, -1)
+            tile = tile + rows(tile, -2)
+            span = slice(8 * f, 8 * f + 8)
+            out[e, span] = jnp.where((row & 3) == 0, tile, out[e, span])
+        return carry
+
     for p in range(parts):
         weights[p].wait()
         lax.fori_loop(p * each, (p + 1) * each, owner, 0, unroll=4)
-
-    def pair(e, carry):
-        out[e] = totals([part[2 * e + i // 4, i % 4] for i in range(8)])
-        return carry
-
-    lax.fori_loop(0, size // 2, pair, 0, unroll=8)
-
-
-def totals(tiles):
-    row = row_index()
-    for step in (4, 2, 1):
-        low = (row & step) == 0
-        half = len(tiles) // 2
-        merged = []
-        for a, b in zip(tiles[:half], tiles[half:]):
-            kept, moved = jnp.where(low, a, b), jnp.where(low, b, a)
-            if step == 4:
-                turned = rows(moved, 4)
-            else:
-                turned = jnp.where(low, rows(moved, -step), rows(moved, step))
-            merged.append(kept + turned)
-        tiles = merged
-    return tiles[0]
+        lax.fori_loop(p * each, (p + 1) * each, letter, 0, unroll=8)
 
 
 def inner_kernel(
-    depth, t_hbm, e_hbm, n_hbm, d_hbm, mix_hbm, fold, out, surface_wet, columns,
-    t, e, n, d, mix, weights, folded, over, sems, flow_sems, cell_sems,
+    depth, t_hbm, e_hbm, n_hbm, d_hbm, mix_hbm, out, surface_wet, columns,
+    t, e, n, d, mix, weights, sems, flow_sems, cell_sems,
 ):
     levels = pltpu.make_async_copy(d_hbm, d, sems.at[0])
     mixing = pltpu.make_async_copy(mix_hbm, mix, sems.at[1])
@@ -291,7 +289,6 @@
     count = t.shape[2] // 8
     spans = [slice(8 * j, 8 * j + 8) for j in range(count)]
     deep = [d[s].astype(F32) for s in spans]
-    fold_deep = fold_levels(fold)
 
     def plus(tiles):
         return [lanes(x, 1) for x in tiles]
@@ -299,17 +296,8 @@
     def minus(tiles):
         return [lanes(x, -1) for x in tiles]
 
-    over_faces = fold_faces([fold_deep], [deep[-1]], plus, minus)
     east_faces = [jnp.minimum(x, y) for x, y in zip(deep, minus(deep))]
-    faces = list(zip(east_faces, plus(east_faces), block_faces(deep, fold_deep)))
-
-    def fold_coefficients(levels):
-        found = fold_weights(
-            [fold[k, 8:16] for k in levels], over_faces * len(levels), [float(k) for k in levels], minus
-        )
-        for k, tiles in zip(levels, found):
-            for i, x in enumerate(tiles):
-                over[i, k] = x
+    faces = list(zip(east_faces, plus(east_faces), block_faces(deep, deep[-1])))
 
     def coefficients(k):
         e_half = [0.5 * e[k, s] for s in spans]
@@ -328,18 +316,12 @@
 
     def substep(k, step):
         source = out if step else t
-        state = [[source[f, k, s] for s in spans] for f in range(2)]
-        cells = folded[k] if step else fold[k, 0:8]
-        beyond = (rows(cells, 4), cells)
         for f in range(2):
-            up, down = north_of(state[f], beyond[f]), south_of(state[f])
-            for s, c, u, v in zip(spans, state[f], up, down):
+            state = [source[f, k, s] for s in spans]
+            up, down = north_of(state, state[-1]), south_of(state)
+            for s, c, u, v in zip(spans, state, up, down):
                 w = [weights[i, k, s] for i in range(5)]
                 out[f, k, s] = advance(w, c, lanes(c, -1), lanes(c, 1), u, v)
-        if step < SUB - 1:
-            up = fold_north(cells, state[0][-1], state[1][-1])
-            w = [over[i, k] for i in range(5)]
-            folded[k] = advance(w, cells, lanes(cells, 1), lanes(cells, -1), up, rows(cells, 1))
 
     zero = jnp.zeros((8, 128), F32)
     above, ratio = [zero] * count, [zero] * count
@@ -354,8 +336,6 @@
 
     for s, x in zip(spans, deep):
         surface_wet[s] = jnp.where(x > 0.0, 1.0, 0.0)
-    for k in range(0, depth, GROUP):
-        fold_coefficients(range(k, min(k + GROUP, depth)))
     for k in range(depth):
         if k % PART == 0:
             for copy in flows[k // PART]:
@@ -412,20 +392,56 @@
     return deep
 
 
-def corners_kernel(depth, size, fold, west, east, blocks, to_core, to_odd):
-    me = lax.axis_index("lon")
-    even = lax.rem(me, 2) == 0
-    spans = [slice(0, 8), slice(8, 16)]
-    stacks = [stack_of(fold, depth, span) for span in spans]
-    stacks[1].append(lambda: fold_levels(fold))
-    for span, found in zip(spans, edge_columns(stacks)):
-        for b, tile in enumerate(found):
-            blocks[b, span] = tile
-        w1, e1 = found[0], found[3]
-        to_core[span] = jnp.where(even, e1, w1)
-        odd = jnp.where(even, w1, e1)
-        odd = jnp.where(me == 0, west[span], odd)
-        to_odd[span] = jnp.where(me == size - 1, east[span], odd)
+def top_strip(depth, t, e, n, d, fold, strip, folded, weights, over):
+    row = row_index()
+    deep = d[...].astype(F32)
+    fold_deep = fold_levels(fold)
+
+    def plus(tiles):
+        return [lanes(x, 1) for x in tiles]
+
+    def minus(tiles):
+        return [lanes(x, -1) for x in tiles]
+
+    over_faces = fold_faces([fold_deep], [deep], plus, minus)
+    east = jnp.minimum(deep, lanes(deep, -1))
+    west = lanes(east, 1)
+    north = jnp.minimum(deep, jnp.where(row == 7, fold_deep, rows(deep, -1)))
+    south = rows(north, 1)
+    for k in range(0, depth, GROUP):
+        levels = range(k, min(k + GROUP, depth))
+        found = fold_weights(
+            [fold[k, 8:16] for k in levels], over_faces * len(levels), [float(k) for k in levels], minus
+        )
+        for k, tiles in zip(levels, found):
+            for i, x in enumerate(tiles):
+                over[i, k] = x
+    for k in range(depth):
+        he, hn = 0.5 * e[k], 0.5 * n[k]
+        level = float(k)
+        found = stencil(
+            face(he, east > level),
+            face(hn, north > level),
+            face(lanes(he, 1), west > level),
+            face(rows(hn, 1), south > level),
+        )
+        for i, x in enumerate(found):
+            weights[i, k] = x
+    for step in range(SUB):
+        for k in range(depth):
+            if step:
+                one, two, cells = strip[0, k], strip[1, k], folded[k]
+            else:
+                one, two, cells = t[0, k], t[1, k], fold[k, 0:8]
+            up_one = jnp.where(row == 7, rows(cells, 4), rows(one, -1))
+            up_two = jnp.where(row == 7, cells, rows(two, -1))
+            if step < SUB - 1:
+                up = fold_north(cells, one, two)
+                w = [over[i, k] for i in range(5)]
+                folded[k] = advance(w, cells, lanes(cells, 1), lanes(cells, -1), up, rows(cells, 1))
+            w = [weights[i, k] for i in range(5)]
+            strip[0, k] = advance(w, one, lanes(one, -1), lanes(one, 1), up_one, rows(one, 1))
+            strip[1, k] = advance(w, two, lanes(two, -1), lanes(two, 1), up_two, rows(two, 1))
 
 
 def edge_side(depth, rows_count, cells, flows, fold_cells, fold_flows):
@@ -455,6 +471,7 @@
     halves = [[0.5 * x for x in flows[b][1]] for b in range(3)]
     southern = [south_of(x) for x in halves]
     for j in range(count):
+        yield
         line = [deep[b][j] for b in range(3)]
         easts = [jnp.minimum(x, y) for x, y in zip(line, minus(line))]
         e_half = [0.5 * flows[b][0][j] for b in range(3)]
@@ -470,48 +487,75 @@
     state = [[list(cells[b][f]) for f in range(2)] for b in range(3)]
     folded = list(fold_cells)
     for step in range(SUB):
-        fold_east, fold_west = plus(folded), minus(folded)
-        following = [[[None] * count for _ in range(2)] for _ in range(3)]
+        yield
+        beyond = [(rows(x, 4), x) for x in folded]
+        if step < SUB - 1:
+            fold_east, fold_west = plus(folded), minus(folded)
+            ups = [fold_north(folded[b], state[b][0][-1], state[b][1][-1]) for b in range(3)]
+            folded = [
+                advance(over[b], folded[b], fold_east[b], fold_west[b], ups[b], rows(folded[b], 1)) for b in range(3)
+            ]
         for f in range(2):
+            yield
+            east, west = [], []
             for j in range(count):
                 line = [state[b][f][j] for b in range(3)]
-                east, west = minus(line), plus(line)
-                for b in range(3):
-                    following[b][f][j] = (east[b], west[b])
-        next_fold = []
-        for b in range(3):
-            up = fold_north(folded[b], state[b][0][-1], state[b][1][-1])
-            next_fold.append(
-                advance(over[b], folded[b], fold_east[b], fold_west[b], up, rows(folded[b], 1))
-            )
-        for b in range(3):
-            beyond = (rows(folded[b], 4), folded[b])
-            for f in range(2):
+                east.append(minus(line))
+                west.append(plus(line))
+            yield
+            for b in range(3):
                 tiles = state[b][f]
-                up, down = north_of(tiles, beyond[f]), south_of(tiles)
+                up, down = north_of(tiles, beyond[b][f]), south_of(tiles)
                 state[b][f] = [
-                    advance(weights[b][j], tiles[j], *following[b][f][j], up[j], down[j]) for j in range(count)
+                    advance(weights[b][j], tiles[j], east[j][b], west[j][b], up[j], down[j]) for j in range(count)
                 ]
-        folded = next_fold
     return state[1]
 
 
+def side_by_side(stages):
+    results = [None] * len(stages)
+    running = list(enumerate(stages))
+    while running:
+        left = []
+        for i, stage in running:
+            try:
+                next(stage)
+                left.append((i, stage))
+            except StopIteration as end:
+                results[i] = end.value
+        running = left
+    return results
+
+
 def last_kernel(
-    depth, wet, inner, blocks, core, odd, fold, fold_core, fold_odd, pieces, columns, target_hbm,
-    out_hbm, merged, out, target, sems, other,
+    depth, t_hbm, e_hbm, n_hbm, d_hbm, wet, inner, blocks, core, odd, fold, mail, columns, target_hbm,
+    out_hbm, t, e, n, d, strip, folded, top_weights, over, merged, out, target, sems, other,
 ):
-    targets = pltpu.make_async_copy(target_hbm, target, other.at[0])
+    targets = pltpu.make_async_copy(target_hbm, target, other.at[4])
+    band = northern_rows(t_hbm, e_hbm, n_hbm, d_hbm, t, e, n, d, other)
+    for copy in band:
+        copy.start()
     targets.start()
     lane, row = lane_index(), row_index()
-    size = pieces.shape[0]
+    size = mail.shape[0]
     rows_count = inner.shape[2]
     count = rows_count // 8
     spans = [slice(8 * j, 8 * j + 8) for j in range(count)]
     me = lax.axis_index("lon")
     even = lax.rem(me, 2) == 0
 
-    def received(f, s, west):
-        a, b = core[f, s], odd[f, s]
+    halves = [slice(0, 8), slice(8, 16)]
+    stacks = [stack_of(fold, depth, span) for span in halves]
+    stacks[1].append(lambda: fold_levels(fold))
+    folds = edge_columns(stacks)
+    west_mail = mail[lax.rem(size - me, size)]
+    east_mail = mail[lax.rem(2 * size - 2 - me, size)]
+    at_wrap = (me == 0) | (me == size - 1)
+
+    def received(f, j, west):
+        place = f * count + j
+        wrapped = fold[depth + place // 2, 8 * (place % 2) : 8 * (place % 2) + 8]
+        a, b = core[f, spans[j]], jnp.where(at_wrap, wrapped, odd[f, spans[j]])
         return jnp.where(even, b, a) if west else jnp.where(even, a, b)
 
     def own(b, f, s):
@@ -521,12 +565,11 @@
     for west in (True, False):
         near, far = (0, 1) if west else (3, 2)
         here = [[[own(b, f, s) for s in spans] for f in range(4)] for b in (near, far)]
-        there = [[received(f, s, west) for s in spans] for f in range(4)]
-        a, b = fold_core[...], fold_odd[...]
-        letter = jnp.where(even, b, a) if west else jnp.where(even, a, b)
+        there = [[received(f, j, west) for j in range(count)] for f in range(4)]
+        letter = west_mail if west else east_mail
         line = [there, here[0], here[1]] if west else [here[1], here[0], there]
-        cells_near = [fold[near, 0:8], fold[far, 0:8]]
-        flows_near = [fold[near, 8:16], fold[far, 8:16]]
+        cells_near = [folds[0][near], folds[0][far]]
+        flows_near = [folds[1][near], folds[1][far]]
         if west:
             fold_cells = [letter[0:8]] + cells_near
             fold_flows = [letter[8:16]] + flows_near
@@ -537,6 +580,10 @@
             edge_side(depth, rows_count, [x[0:2] for x in line], [x[2:4] for x in line], fold_cells, fold_flows)
         )
 
+    sides = side_by_side(sides)
+    for copy in band:
+        copy.wait()
+    top_strip(depth, t, e, n, d, fold, strip, folded, top_weights, over)
     order = gather_order()
     group_even = ((lane >> 2) & 1) == 0
     for f in range(2):
@@ -553,16 +600,22 @@
             goal = target[s, a]
             hits = [row + 8 * j == goal for j in range(count)]
             for f in range(2):
-                piece = jnp.broadcast_to(pieces[a, 2 * f + s : 2 * f + s + 1], (8, 128))
+                piece = jnp.broadcast_to(mail[a, PIECE_ROW[f][s] : PIECE_ROW[f][s] + 1], (8, 128))
                 surface[f] = [x + jnp.where(hit, piece, 0.0) for x, hit in zip(surface[f], hits)]
 
     outer = (lane < 4) | (lane >= 124)
+    for k in range(depth):
+        for f in range(2):
+            for j, s in enumerate(spans):
+                cell = inner[f, k, s]
+                if j == count - 1:
+                    cell = jnp.where(row >= 4, strip[f, k], cell)
+                out[f, k, s] = jnp.where(outer, lanes(merged[k % 2, f, s], -4 * k), cell)
     partial_value = [[None] * count for _ in range(2)]
     for k in range(depth):
         for f in range(2):
             for j, s in enumerate(spans):
-                cell = inner[f, k, s]
-                cell = jnp.where(outer, lanes(merged[k % 2, f, s], -4 * k), cell)
+                cell = out[f, k, s]
                 if k == 0:
                     cell = cell + FLUX_GAIN * surface[f][j] * wet[s]
                 else:
@@ -601,39 +654,34 @@
     size = lax.axis_size("lon")
     depth, lat = tracers.shape[1], tracers.shape[2]
     dma = pltpu.SemaphoreType.DMA
+    near = [(i, i + (1 if i % 2 else -1)) for i in range(1, size - 1)]
     band = [
-        pltpu.VMEM((2, depth, 8, 128), F32),
-        pltpu.VMEM((depth, 8, 128), F32),
-        pltpu.VMEM((depth, 8, 128), F32),
+        shape(2, depth, 8, 128),
+        shape(depth, 8, 128),
+        shape(depth, 8, 128),
         pltpu.VMEM((8, 128), jnp.int32),
     ]
-    top, west_corner, east_corner = call(
-        functools.partial(fold_kernel, depth),
-        (shape(depth, 16, 128), shape(16, 128), shape(16, 128)),
-        [HBM] * 4,
-        [*band, dma((4,))],
-        cost=cost(0.1),
-        name="fold_rows",
-    )(*in_hbm(tracers, east_flow, north_flow, depth_levels))
-    fold = lax.ppermute(top, "lon", [(i, size - 1 - i) for i in range(size)])
-
     plane = shape(depth, lat, 128)
     block = [shape(2, depth, lat, 128), plane, plane, pltpu.VMEM((lat, 128), jnp.int32)]
-    blocks, to_core, to_odd = call(
-        functools.partial(columns_kernel, depth),
-        (shape(4, 4, lat, 128), shape(4, lat, 128), shape(4, lat, 128)),
+    strips = shape(4, lat, 128)
+    fields = in_hbm(tracers, east_flow, north_flow, depth_levels)
+
+    message, west_corner, east_corner, blocks, to_core, to_odd = call(
+        functools.partial(pack_kernel, depth),
+        (shape(depth + lat // 4, 16, 128), shape(16, 128), shape(16, 128), shape(4, 4, lat, 128), strips, strips),
         [HBM] * 4,
-        [*block, dma((5,))],
+        [*block, dma((4,))],
         cost=cost(0.1),
-        name="edge_columns",
-    )(*in_hbm(tracers, east_flow, north_flow, depth_levels))
+        name="fold_rows_and_columns",
+    )(*fields)
+    fold = lax.ppermute(message, "lon", [(i, size - 1 - i) for i in range(size)])
     core = lax.ppermute(to_core, "lon", [(i, i ^ 1) for i in range(size)])
-    odd = lax.ppermute(to_odd, "lon", [(i, (i + (1 if i % 2 else -1)) % size) for i in range(size)])
-
-    (pieces,) = call(
+    odd = lax.ppermute(to_odd, "lon", [(0, 0), *near, (size - 1, size - 1)])
+
+    (letters,) = call(
         functools.partial(regrid_kernel, size),
-        (shape(size // 2, 8, 128),),
-        [HBM, HBM, HBM],
+        (shape(size, 16, 128),),
+        [HBM, HBM, HBM, VMEM, VMEM],
         [
             pltpu.VMEM((2 * atm_flux.shape[1], 128, 128), F32),
             pltpu.VMEM((size, 2, 128, 128), F32),
@@ -641,62 +689,54 @@
             pltpu.VMEM(atm_flux.shape, F32),
             pltpu.SMEM((2, size), jnp.int32),
             dma((2,)),
-            dma((4,)),
+            dma((2,)),
         ],
         cost=cost(0.1),
         name="regrid",
-    )(*in_hbm(atm_flux, regrid_weights, jnp.transpose(source_blocks[0])))
-    pieces = pieces.reshape(size, 4, 128)
-    received = lax.all_to_all(pieces, "lon", split_axis=0, concat_axis=0, tiled=True)
-
-    fold_blocks, fold_core, fold_odd = call(
-        functools.partial(corners_kernel, depth, size),
-        (shape(4, 16, 128), shape(16, 128), shape(16, 128)),
-        [VMEM] * 3,
-        cost=cost(0.1),
-        name="fold_corners",
-    )(*in_vmem(fold, west_corner, east_corner))
-    fold_core = lax.ppermute(fold_core, "lon", [(i, i ^ 1) for i in range(size)])
-    near = [(i, i + (1 if i % 2 else -1)) for i in range(1, size - 1)]
-    fold_odd = lax.ppermute(fold_odd, "lon", [(0, 0), *near, (size - 1, size - 1)])
+    )(
+        *in_hbm(atm_flux, regrid_weights, jnp.transpose(source_blocks[0])),
+        *in_vmem(west_corner, east_corner),
+    )
+    mail = lax.all_to_all(letters, "lon", split_axis=0, concat_axis=0, tiled=True)
 
     inner, wet, columns = call(
         functools.partial(inner_kernel, depth),
-        (
-            shape(2, depth, lat, 128), shape(lat, 128),
-            shape(2, depth, lat, 128),
-        ),
-        [HBM] * 5 + [VMEM],
+        (shape(2, depth, lat, 128), shape(lat, 128), shape(2, depth, lat, 128)),
+        [HBM] * 5,
         [
             *block,
             shape(depth - 1, lat, 128),
             shape(5, depth, lat, 128),
-            shape(depth, 8, 128),
-            shape(5, depth, 8, 128),
             dma((2,)),
             dma((2, -(-depth // PART))),
             dma((-(-depth // PART),)),
         ],
         cost=cost(0.1),
         name="inner_cells",
-    )(*in_hbm(tracers, east_flow, north_flow, depth_levels, mixing), *in_vmem(fold))
+    )(*fields, *in_hbm(mixing))
 
     (result,) = call(
         functools.partial(last_kernel, depth),
         (jax.ShapeDtypeStruct((2, depth, lat, 128), F32),),
-        [VMEM] * 10 + [HBM],
+        [HBM] * 4 + [VMEM] * 8 + [HBM],
         [
+            *band,
+            shape(2, depth, 8, 128),
+            shape(depth, 8, 128),
+            shape(5, depth, 8, 128),
+            shape(5, depth, 8, 128),
             pltpu.VMEM((2, 2, lat, 128), F32),
             pltpu.VMEM((2, depth, lat, 128), F32),
             pltpu.SMEM((2, size), jnp.int32),
             dma((-(-depth // GROUP),)),
-            dma((1,)),
+            dma((5,)),
         ],
         out_specs=[HBM],
         cost=cost(0.1),
         name="edges_and_columns",
     )(
-        *in_vmem(wet, inner, blocks, core, odd, fold_blocks, fold_core, fold_odd, received, columns),
+        *fields,
+        *in_vmem(wet, inner, blocks, core, odd, fold, mail, columns),
         *in_hbm(jnp.transpose(target_rows[:, 0, :])),
     )
     return result

time: 28.9 us -> 27 us (0.934)
  the two profiles are of different devices: /device:TPU:1 before, /device:TPU:0 now
where the time goes in v3:
time: 27 us; the launch traced here: 26.6 us
  Pallas kernels  12.1 us (45%)
  starting transfers between devices  10.3 us (38%)
  waiting for transfers between devices  4.14 us (15%)
    ppermute x1, starting transfers between devices, on_device(): lax.ppermute(message, 'lon', [(i, size - 1 - i) for i in range(size)])  5.51 us
    all_to_all x1, waiting for transfers between devices, on_device(): lax.all_to_all(letters, 'lon', split_axis=0, concat_axis=0, tiled=True)  4.13 us
    pallas_call x1, Pallas kernels, on_device(): call(functools.partial(last_kernel, depth), (jax.ShapeDtypeStruct((2, dep...  3.74 us
    pallas_call x1, Pallas kernels, on_device(): call(functools.partial(inner_kernel, depth), (shape(2, depth, lat, 128),...  3.6 us
    all_to_all x1, starting transfers between devices, on_device(): lax.all_to_all(letters, 'lon', split_axis=0, concat_axis=0, tiled=True)  3.52 us
    pallas_call x1, Pallas kernels, on_device(): call(functools.partial(regrid_kernel, size), (shape(size, 16, 128),), [HB...  2.43 us
    pallas_call x1, Pallas kernels, on_device(): call(functools.partial(pack_kernel, depth), (shape(depth + lat // 4, 16,...  2.29 us
    ppermute x1, starting transfers between devices, on_device(): odd = lax.ppermute(to_odd, 'lon', [(0, 0), *near, (size - 1, size - 1)])  0.65 us
  transfers between devices with their start and end apart: 4, of which 1 were waited for; matrix products, arithmetic and copies ran while one was open for 0% of the time, Pallas kernels for 23%

profile of v3, /device:TPU:0, one launch (start us, length us, event | category | flops | bytes accessed | tf_op | source)
XLA Modules:
  0.0 26.6 jit_solution(297533664011634068)
XLA Ops:
  0.0 2.3 %fold_rows_and_columns.1 = (f32[33,16,128]{2,1,0:T(8,128)S(1)}, f32[16,128]{1,0:T(8,128)S(1)}, f32[16,128]{1,0:T(8,128)S(1)}, f32[4,4,32,128]{3,2,1,0:T(8,128)S(...) custom-call(f32[2,25,32,128]{3,2,1,0:T(8,128)} %t_hbm.5, f32[25,32,128]{2,1,0:T(8,128)} %e_hbm.5, ...), custom_call_target="tpu_custom_call" | custom-call | bytes 300000 | tf_op jit(solution)/shard_map/fold_rows_and_columns/pallas_call | solution.py:669
  2.3 5.5 %collective-permute-start.2 = (f32[33,16,128]{2,1,0:T(8,128)S(1)}, f32[33,16,128]{2,1,0:T(8,128)S(1)}, u32[]{:S(2)}, u32[]{:S(2)}) collective-permute-start(f32[33,16,128]{2,1,0:T(8,128)S(1)} %get-tuple-element.19), channel_id=1, source_target_pairs={{0,15},{1,14},{2,13},{3,12},{4,11},{5,10},{6,9},{7,8},{8,7},{9,6},... | collective-permute-start | bytes 811016 | tf_op jit(solution)/shard_map/ppermute | solution.py:677
  7.8 2.4 %regrid.1 = f32[16,16,128]{2,1,0:T(8,128)} custom-call(f32[2,8,128]{2,1,0:T(8,128)} %atm_hbm.1, f32[1,16,2,128,128]{4,3,2,1,0:T(8,128)} %w_hbm.1, s32[2,16]{1,0:T(2,128)} %bitcast.6, f32[16,128]{1,0:T(8,128)S(1)} %get-tuple-element.20.west, f32[16,128]{1,0:T(8,128)S(1)} %get-tuple-element.21.east), custom_call_target="tpu_custom_call" | custom-call | bytes 300000 | tf_op jit(solution)/shard_map/regrid/pallas_call | solution.py:681
  10.2 3.5 %all-to-all-start = ((f32[16,16,128]{2,1,0:T(8,128)}), f32[16,16,128]{2,1,0:T(8,128)S(1)}, u32[]{:S(2)}, u32[]{:S(2)}) async-start(f32[16,16,128]{2,1,0:T(8,128)} %regrid.1), calls=%async_computation | async-start | bytes 262144 | tf_op jit(solution)/shard_map/all_to_all | solution.py:700
  13.8 0.6 %collective-permute-start = (f32[4,32,128]{2,1,0:T(8,128)S(1)}, f32[4,32,128]{2,1,0:T(8,128)S(1)}, u32[]{:S(2)}, u32[]{:S(2)}) collective-permute-start(f32[4,32,128]{2,1,0:T(8,128)S(1)} %get-tuple-element.17), channel_id=1, source_target_pairs={{0,1},{1,0},{2,3},{3,2},{4,5},{5,4},{6,7},{7,6},{8,9},{9,8},{10,11... | collective-permute-start | bytes 196616 | tf_op jit(solution)/shard_map/ppermute | solution.py:678
  14.4 0.7 %collective-permute-start.1 = (f32[4,32,128]{2,1,0:T(8,128)S(1)}, f32[4,32,128]{2,1,0:T(8,128)S(1)}, u32[]{:S(2)}, u32[]{:S(2)}) collective-permute-start(f32[4,32,128]{2,1,0:T(8,128)S(1)} %get-tuple-element.18), channel_id=1, source_target_pairs={{0,0},{1,2},{2,1},{3,4},{4,3},{5,6},{6,5},{7,8},{8,7},{9,10},{10,9... | collective-permute-start | bytes 196616 | tf_op jit(solution)/shard_map/ppermute | solution.py:679
  15.1 3.6 %inner_cells.1 = (f32[2,25,32,128]{3,2,1,0:T(8,128)S(1)}, f32[32,128]{1,0:T(8,128)S(1)}, f32[2,25,32,128]{3,2,1,0:T(8,128)S(1)}) custom-call(f32[2,25,32,128]{3,2,1,0:T(8,128)} %t_hbm.5, f32[25,32,128]{2,1,0:T(8,128)} %e_hbm.5, f32[25,32,128]{2,1,0:T(8,128)} %n_hbm.5, s32[32,128]{1,0:T(8,128)} %d_hbm.5, f32[24,32,128]{2,1,0:T(8,128)} %mix_hbm.1), custom_call_target="tpu_custom_call" | custom-call | bytes 300000 | tf_op jit(solution)/shard_map/inner_cells/pallas_call | solution.py:702
  18.7 0.0 collective-permute-done.core
  18.7 0.0 collective-permute-done.1.odd
  18.7 4.1 %all-to-all-done.mail = f32[16,16,128]{2,1,0:T(8,128)S(1)} async-done(((f32[16,16,128]{2,1,0:T(8,128)}), f32[16,16,128]{2,1,0:T(8,128)S(1)}, u32[]{:S(2)}, u32[]{:S(2)}) %all-to-all-start) | async-done | bytes 131104 | tf_op jit(solution)/shard_map/all_to_all | solution.py:700
  22.8 0.0 collective-permute-done.2.fold
  22.8 3.7 %edges_and_columns.1 = f32[2,25,32,128]{3,2,1,0:T(8,128)} custom-call(f32[2,25,32,128]{3,2,1,0:T(8,128)} %t_hbm.5, f32[25,32,128]{2,1,0:T(8,128)} %e_hbm.5, f32[25,32,128]{2,1,0:T(8,128)} %n_hbm.5, s32[32,128]{1,0:T(8,128)} %d_hbm.5, f32[32,128]{1,0:T(8,128)S(1)} %get-tuple-element.14.wet, f32[2,25,32,128]{3,2,1,0:T(8,128)S(1)} %get-tuple-element.15.inner, ...), custom_call_target="tpu_custom_call" | custom-call | bytes 300000 | tf_op jit(solution)/shard_map/edges_and_columns/pallas_call | solution.py:718
Async XLA Ops:
  2.3 20.5 %collective-permute-start.2 = (f32[33,16,128]{2,1,0:T(8,128)S(1)}, f32[33,16,128]{2,1,0:T(8,128)S(1)}, u32[]{:S(2)}, u32[]{:S(2)}) collective-permute-start(f32[33,16,128]{2,1,0:T(8,128)S(1)} %get-tuple-element.19), channel_id=1, source_target_pairs={{0,15},{1,14},{2,13},{3,12},{4,11},{5,10},{6,9},{7,8},{8,7},{9,6},... | collective-permute-start | bytes 811016 | tf_op jit(solution)/shard_map/ppermute | solution.py:677
  10.2 12.6 %all-to-all-start = ((f32[16,16,128]{2,1,0:T(8,128)}), f32[16,16,128]{2,1,0:T(8,128)S(1)}, u32[]{:S(2)}, u32[]{:S(2)}) async-start(f32[16,16,128]{2,1,0:T(8,128)} %regrid.1), calls=%async_computation | async-start | bytes 262144 | tf_op jit(solution)/shard_map/all_to_all | solution.py:700
  13.8 4.9 %collective-permute-start = (f32[4,32,128]{2,1,0:T(8,128)S(1)}, f32[4,32,128]{2,1,0:T(8,128)S(1)}, u32[]{:S(2)}, u32[]{:S(2)}) collective-permute-start(f32[4,32,128]{2,1,0:T(8,128)S(1)} %get-tuple-element.17), channel_id=1, source_target_pairs={{0,1},{1,0},{2,3},{3,2},{4,5},{5,4},{6,7},{7,6},{8,9},{9,8},{10,11... | collective-permute-start | bytes 196616 | tf_op jit(solution)/shard_map/ppermute | solution.py:678
  14.4 4.3 %collective-permute-start.1 = (f32[4,32,128]{2,1,0:T(8,128)S(1)}, f32[4,32,128]{2,1,0:T(8,128)S(1)}, u32[]{:S(2)}, u32[]{:S(2)}) collective-permute-start(f32[4,32,128]{2,1,0:T(8,128)S(1)} %get-tuple-element.18), channel_id=1, source_target_pairs={{0,0},{1,2},{2,1},{3,4},{4,3},{5,6},{6,5},{7,8},{8,7},{9,10},{10,9... | collective-permute-start | bytes 196616 | tf_op jit(solution)/shard_map/ppermute | solution.py:679

commit v4 on v3

--- a/solution.py
+++ b/solution.py
@@ -147,13 +147,16 @@
 
 
 def pack_kernel(
-    depth, t_hbm, e_hbm, n_hbm, d_hbm, out, west, east, blocks, to_core, to_odd, t, e, n, d, sems
+    depth, t_hbm, e_hbm, n_hbm, d_hbm, w_hbm, atm_hbm, out, west, east, blocks, to_core, to_odd, w, atm,
+    t, e, n, d, sems,
 ):
     copies = [
         pltpu.make_async_copy(d_hbm, d, sems.at[0]),
         pltpu.make_async_copy(t_hbm, t, sems.at[1]),
         pltpu.make_async_copy(e_hbm, e, sems.at[2]),
         pltpu.make_async_copy(n_hbm, n, sems.at[3]),
+        pltpu.make_async_copy(atm_hbm, atm, sems.at[4]),
+        pltpu.make_async_copy(w_hbm.at[0], w, sems.at[5]),
     ]
     for copy in copies:
         copy.start()
@@ -199,22 +202,13 @@
     stacks[1].append(lambda: take(levels, turn))
     for span, found in zip(halves, edge_columns(stacks)):
         east[span], west[span] = found[0], found[3]
-
-
-def regrid_kernel(size, atm_hbm, w_hbm, src_hbm, west, east, out, wide, w, part, atm, src, sems, w_sems):
-    first = [pltpu.make_async_copy(atm_hbm, atm, sems.at[0]), pltpu.make_async_copy(src_hbm, src, sems.at[1])]
-    for copy in first:
-        copy.start()
-    parts = w_sems.shape[0]
-    each = size // parts
-    weights = [
-        pltpu.make_async_copy(w_hbm.at[0, pl.ds(p * each, each)], w.at[pl.ds(p * each, each)], w_sems.at[p])
-        for p in range(parts)
-    ]
-    for copy in weights:
-        copy.start()
-    for copy in first:
-        copy.wait()
+    copies[4].wait()
+    copies[5].wait()
+
+
+def regrid_kernel(size, atm, w, src_hbm, west, east, out, wide, part, src, sems):
+    blocks_read = pltpu.make_async_copy(src_hbm, src, sems.at[0])
+    blocks_read.start()
     flat = atm[...].reshape(atm.shape[0] * atm.shape[1], atm.shape[2])
     count = flat.shape[0]
     blocks = atm.shape[1]
@@ -256,10 +250,9 @@
             out[e, span] = jnp.where((row & 3) == 0, tile, out[e, span])
         return carry
 
-    for p in range(parts):
-        weights[p].wait()
-        lax.fori_loop(p * each, (p + 1) * each, owner, 0, unroll=4)
-        lax.fori_loop(p * each, (p + 1) * each, letter, 0, unroll=8)
+    blocks_read.wait()
+    lax.fori_loop(0, size, owner, 0, unroll=4)
+    lax.fori_loop(0, size, letter, 0, unroll=8)
 
 
 def inner_kernel(
@@ -392,7 +385,18 @@
     return deep
 
 
-def top_strip(depth, t, e, n, d, fold, strip, folded, weights, over):
+def strip_kernel(depth, t_hbm, e_hbm, n_hbm, d_hbm, fold, strip, blocks, t, e, n, d, folded, weights, over, sems):
+    band = northern_rows(t_hbm, e_hbm, n_hbm, d_hbm, t, e, n, d, sems)
+    for copy in band:
+        copy.start()
+    halves = [slice(0, 8), slice(8, 16)]
+    stacks = [stack_of(fold, depth, span) for span in halves]
+    stacks[1].append(lambda: fold_levels(fold))
+    for span, found in zip(halves, edge_columns(stacks)):
+        for b, tile in enumerate(found):
+            blocks[b, span] = tile
+    for copy in band:
+        copy.wait()
     row = row_index()
     deep = d[...].astype(F32)
     fold_deep = fold_levels(fold)
@@ -528,13 +532,10 @@
 
 
 def last_kernel(
-    depth, t_hbm, e_hbm, n_hbm, d_hbm, wet, inner, blocks, core, odd, fold, mail, columns, target_hbm,
-    out_hbm, t, e, n, d, strip, folded, top_weights, over, merged, out, target, sems, other,
+    depth, strip, folds, wet, inner, blocks, core, odd, fold, mail, columns, target_hbm,
+    out_hbm, merged, out, target, sems, other,
 ):
-    targets = pltpu.make_async_copy(target_hbm, target, other.at[4])
-    band = northern_rows(t_hbm, e_hbm, n_hbm, d_hbm, t, e, n, d, other)
-    for copy in band:
-        copy.start()
+    targets = pltpu.make_async_copy(target_hbm, target, other.at[0])
     targets.start()
     lane, row = lane_index(), row_index()
     size = mail.shape[0]
@@ -544,10 +545,6 @@
     me = lax.axis_index("lon")
     even = lax.rem(me, 2) == 0
 
-    halves = [slice(0, 8), slice(8, 16)]
-    stacks = [stack_of(fold, depth, span) for span in halves]
-    stacks[1].append(lambda: fold_levels(fold))
-    folds = edge_columns(stacks)
     west_mail = mail[lax.rem(size - me, size)]
     east_mail = mail[lax.rem(2 * size - 2 - me, size)]
     at_wrap = (me == 0) | (me == size - 1)
@@ -568,8 +565,8 @@
         there = [[received(f, j, west) for j in range(count)] for f in range(4)]
         letter = west_mail if west else east_mail
         line = [there, here[0], here[1]] if west else [here[1], here[0], there]
-        cells_near = [folds[0][near], folds[0][far]]
-        flows_near = [folds[1][near], folds[1][far]]
+        cells_near = [folds[near, 0:8], folds[far, 0:8]]
+        flows_near = [folds[near, 8:16], folds[far, 8:16]]
         if west:
             fold_cells = [letter[0:8]] + cells_near
             fold_flows = [letter[8:16]] + flows_near
@@ -581,9 +578,6 @@
         )
 
     sides = side_by_side(sides)
-    for copy in band:
-        copy.wait()
-    top_strip(depth, t, e, n, d, fold, strip, folded, top_weights, over)
     order = gather_order()
     group_even = ((lane >> 2) & 1) == 0
     for f in range(2):
@@ -666,14 +660,17 @@
     strips = shape(4, lat, 128)
     fields = in_hbm(tracers, east_flow, north_flow, depth_levels)
 
-    message, west_corner, east_corner, blocks, to_core, to_odd = call(
+    message, west_corner, east_corner, blocks, to_core, to_odd, weights, flux = call(
         functools.partial(pack_kernel, depth),
-        (shape(depth + lat // 4, 16, 128), shape(16, 128), shape(16, 128), shape(4, 4, lat, 128), strips, strips),
-        [HBM] * 4,
-        [*block, dma((4,))],
+        (
+            shape(depth + lat // 4, 16, 128), shape(16, 128), shape(16, 128), shape(4, 4, lat, 128), strips, strips,
+            shape(*regrid_weights.shape[1:]), shape(*atm_flux.shape),
+        ),
+        [HBM] * 6,
+        [*block, dma((6,))],
         cost=cost(0.1),
         name="fold_rows_and_columns",
-    )(*fields)
+    )(*fields, *in_hbm(regrid_weights, atm_flux))
     fold = lax.ppermute(message, "lon", [(i, size - 1 - i) for i in range(size)])
     core = lax.ppermute(to_core, "lon", [(i, i ^ 1) for i in range(size)])
     odd = lax.ppermute(to_odd, "lon", [(0, 0), *near, (size - 1, size - 1)])
@@ -681,20 +678,18 @@
     (letters,) = call(
         functools.partial(regrid_kernel, size),
         (shape(size, 16, 128),),
-        [HBM, HBM, HBM, VMEM, VMEM],
+        [VMEM, VMEM, HBM, VMEM, VMEM],
         [
             pltpu.VMEM((2 * atm_flux.shape[1], 128, 128), F32),
-            pltpu.VMEM((size, 2, 128, 128), F32),
             pltpu.VMEM((size, 4, 8, 128), F32),
-            pltpu.VMEM(atm_flux.shape, F32),
             pltpu.SMEM((2, size), jnp.int32),
-            dma((2,)),
-            dma((2,)),
+            dma((1,)),
         ],
         cost=cost(0.1),
         name="regrid",
     )(
-        *in_hbm(atm_flux, regrid_weights, jnp.transpose(source_blocks[0])),
+        *in_vmem(flux, weights),
+        *in_hbm(jnp.transpose(source_blocks[0])),
         *in_vmem(west_corner, east_corner),
     )
     mail = lax.all_to_all(letters, "lon", split_axis=0, concat_axis=0, tiled=True)
@@ -715,28 +710,31 @@
         name="inner_cells",
     )(*fields, *in_hbm(mixing))
 
+    strip, folds = call(
+        functools.partial(strip_kernel, depth),
+        (shape(2, depth, 8, 128), shape(4, 16, 128)),
+        [HBM] * 4 + [VMEM],
+        [*band, shape(depth, 8, 128), shape(5, depth, 8, 128), shape(5, depth, 8, 128), dma((4,))],
+        cost=cost(0.1),
+        name="top_strip",
+    )(*fields, *in_vmem(fold))
+
     (result,) = call(
         functools.partial(last_kernel, depth),
         (jax.ShapeDtypeStruct((2, depth, lat, 128), F32),),
-        [HBM] * 4 + [VMEM] * 8 + [HBM],
+        [VMEM] * 10 + [HBM],
         [
-            *band,
-            shape(2, depth, 8, 128),
-            shape(depth, 8, 128),
-            shape(5, depth, 8, 128),
-            shape(5, depth, 8, 128),
             pltpu.VMEM((2, 2, lat, 128), F32),
             pltpu.VMEM((2, depth, lat, 128), F32),
             pltpu.SMEM((2, size), jnp.int32),
             dma((-(-depth // GROUP),)),
-            dma((5,)),
+            dma((1,)),
         ],
         out_specs=[HBM],
         cost=cost(0.1),
         name="edges_and_columns",
     )(
-        *fields,
-        *in_vmem(wet, inner, blocks, core, odd, fold, mail, columns),
+        *in_vmem(strip, folds, wet, inner, blocks, core, odd, fold, mail, columns),
         *in_hbm(jnp.transpose(target_rows[:, 0, :])),
     )
     return result

time: 27 us -> 25.4 us (0.941)
  waiting for transfers between devices: 4.14 us -> 2.68 us
    all_to_all x1, waiting for transfers between devices: 4.13 us -> 2.67 us  [on_device(): lax.all_to_all(letters, 'lon', split_axis=0, concat_axis=0, tiled=True)]
    pallas_call x1, Pallas kernels: 3.74 us -> 2.34 us  [on_device(): call(functools.partial(last_kernel, depth), (jax.ShapeDtypeStruct((2, dep...]
    pallas_call x1 -> x2, Pallas kernels: 2.43 us -> 3.65 us  [the longest x1 1.93 us: on_device(): call(functools.partial(strip_kernel, depth), (shape(2, depth, 8, 128), sh...]
  transfers between devices with their start and end apart: 4 -> 4, of which waited for: 1 -> 1; matrix products, arithmetic and copies ran while one was open for 0% -> 0% of each run, Pallas kernels for 23% -> 29%
where the time goes in v4:
time: 25.4 us; the launch traced here: 25.1 us
  Pallas kernels  12 us (47%)
  starting transfers between devices  10.3 us (41%)
  waiting for transfers between devices  2.68 us (11%)
    ppermute x1, starting transfers between devices, on_device(): lax.ppermute(message, 'lon', [(i, size - 1 - i) for i in range(size)])  5.51 us
    pallas_call x1, Pallas kernels, on_device(): call(functools.partial(inner_kernel, depth), (shape(2, depth, lat, 128),...  3.71 us
    all_to_all x1, starting transfers between devices, on_device(): lax.all_to_all(letters, 'lon', split_axis=0, concat_axis=0, tiled=True)  3.52 us
    all_to_all x1, waiting for transfers between devices, on_device(): lax.all_to_all(letters, 'lon', split_axis=0, concat_axis=0, tiled=True)  2.67 us
    pallas_call x1, Pallas kernels, on_device(): call(functools.partial(last_kernel, depth), (jax.ShapeDtypeStruct((2, dep...  2.34 us
    pallas_call x1, Pallas kernels, on_device(): call(functools.partial(pack_kernel, depth), (shape(depth + lat // 4, 16,...  2.31 us
    pallas_call x1, Pallas kernels, on_device(): call(functools.partial(strip_kernel, depth), (shape(2, depth, 8, 128), sh...  1.93 us
    pallas_call x1, Pallas kernels, on_device(): call(functools.partial(regrid_kernel, size), (shape(size, 16, 128),), [VM...  1.72 us
  transfers between devices with their start and end apart: 4, of which 1 were waited for; matrix products, arithmetic and copies ran while one was open for 0% of the time, Pallas kernels for 29%

profile of v4, /device:TPU:0, one launch (start us, length us, event | category | flops | bytes accessed | tf_op | source)
XLA Modules:
  0.0 25.1 jit_solution(6608926545117039613)
XLA Ops:
  0.0 2.3 %fold_rows_and_columns.1 = (f32[33,16,128]{2,1,0:T(8,128)S(1)}, f32[16,128]{1,0:T(8,128)S(1)}, f32[16,128]{1,0:T(8,128)S(1)}, f32[4,4,32,128]{3,2,1,0:T(8,128)S(...) custom-call(f32[2,25,32,128]{3,2,1,0:T(8,128)} %t_hbm.5, ...), custom_call_target="tpu_custom_call" | custom-call | bytes 300000 | tf_op jit(solution)/shard_map/fold_rows_and_columns/pallas_call | solution.py:663
  2.3 5.5 %collective-permute-start = (f32[33,16,128]{2,1,0:T(8,128)S(1)}, f32[33,16,128]{2,1,0:T(8,128)S(1)}, u32[]{:S(2)}, u32[]{:S(2)}) collective-permute-start(f32[33,16,128]{2,1,0:T(8,128)S(1)} %get-tuple-element.18), channel_id=1, source_target_pairs={{0,15},{1,14},{2,13},{3,12},{4,11},{5,10},{6,9},{7,8},{8,7},{9,6},... | collective-permute-start | bytes 811016 | tf_op jit(solution)/shard_map/ppermute | solution.py:674
  7.8 1.7 %regrid.1 = f32[16,16,128]{2,1,0:T(8,128)} custom-call(f32[2,8,128]{2,1,0:T(8,128)S(1)} %get-tuple-element.26.atm, f32[16,2,128,128]{3,2,1,0:T(8,128)S(1)} %get-tuple-element.27.w, s32[2,16]{1,0:T(2,128)} %bitcast.7, f32[16,128]{1,0:T(8,128)S(1)} %get-tuple-element.28.west, f32[16,128]{1,0:T(8,128)S(1)} %get-tuple-element.29.east), custom_call_target="tpu_custom_call" | custom-call | bytes 300000 | tf_op jit(solution)/shard_map/regrid/pallas_call | solution.py:678
  9.6 3.5 %all-to-all-start = ((f32[16,16,128]{2,1,0:T(8,128)}), f32[16,16,128]{2,1,0:T(8,128)S(1)}, u32[]{:S(2)}, u32[]{:S(2)}) async-start(f32[16,16,128]{2,1,0:T(8,128)} %regrid.1), calls=%async_computation | async-start | bytes 262144 | tf_op jit(solution)/shard_map/all_to_all | solution.py:695
  13.1 0.6 %collective-permute-start.1 = (f32[4,32,128]{2,1,0:T(8,128)S(1)}, f32[4,32,128]{2,1,0:T(8,128)S(1)}, u32[]{:S(2)}, u32[]{:S(2)}) collective-permute-start(f32[4,32,128]{2,1,0:T(8,128)S(1)} %get-tuple-element.24), channel_id=1, source_target_pairs={{0,1},{1,0},{2,3},{3,2},{4,5},{5,4},{6,7},{7,6},{8,9},{9,8},{10,11... | collective-permute-start | bytes 196616 | tf_op jit(solution)/shard_map/ppermute | solution.py:675
  13.7 0.7 %collective-permute-start.2 = (f32[4,32,128]{2,1,0:T(8,128)S(1)}, f32[4,32,128]{2,1,0:T(8,128)S(1)}, u32[]{:S(2)}, u32[]{:S(2)}) collective-permute-start(f32[4,32,128]{2,1,0:T(8,128)S(1)} %get-tuple-element.25), channel_id=1, source_target_pairs={{0,0},{1,2},{2,1},{3,4},{4,3},{5,6},{6,5},{7,8},{8,7},{9,10},{10,9... | collective-permute-start | bytes 196616 | tf_op jit(solution)/shard_map/ppermute | solution.py:676
  14.4 3.7 %inner_cells.1 = (f32[2,25,32,128]{3,2,1,0:T(8,128)S(1)}, f32[32,128]{1,0:T(8,128)S(1)}, f32[2,25,32,128]{3,2,1,0:T(8,128)S(1)}) custom-call(f32[2,25,32,128]{3,2,1,0:T(8,128)} %t_hbm.5, f32[25,32,128]{2,1,0:T(8,128)} %e_hbm.5, f32[25,32,128]{2,1,0:T(8,128)} %n_hbm.5, s32[32,128]{1,0:T(8,128)} %d_hbm.5, f32[24,32,128]{2,1,0:T(8,128)} %mix_hbm.1), custom_call_target="tpu_custom_call" | custom-call | bytes 300000 | tf_op jit(solution)/shard_map/inner_cells/pallas_call | solution.py:697
  18.1 0.0 collective-permute-done.fold
  18.1 1.9 %top_strip.1 = (f32[2,25,8,128]{3,2,1,0:T(8,128)S(1)}, f32[4,16,128]{2,1,0:T(8,128)S(1)}) custom-call(f32[2,25,32,128]{3,2,1,0:T(8,128)} %t_hbm.5, f32[25,32,128]{2,1,0:T(8,128)} %e_hbm.5, f32[25,32,128]{2,1,0:T(8,128)} %n_hbm.5, s32[32,128]{1,0:T(8,128)} %d_hbm.5, f32[33,16,128]{2,1,0:T(8,128)S(1)} %collective-permute-done.fold), custom_call_target="tpu_custom_call" | custom-call | bytes 300000 | tf_op jit(solution)/shard_map/top_strip/pallas_call | solution.py:713
  20.1 0.0 collective-permute-done.1.core
  20.1 0.0 collective-permute-done.2.odd
  20.1 2.7 %all-to-all-done.mail = f32[16,16,128]{2,1,0:T(8,128)S(1)} async-done(((f32[16,16,128]{2,1,0:T(8,128)}), f32[16,16,128]{2,1,0:T(8,128)S(1)}, u32[]{:S(2)}, u32[]{:S(2)}) %all-to-all-start) | async-done | bytes 131104 | tf_op jit(solution)/shard_map/all_to_all | solution.py:695
  22.7 2.3 %edges_and_columns.1 = f32[2,25,32,128]{3,2,1,0:T(8,128)} custom-call(f32[2,25,8,128]{3,2,1,0:T(8,128)S(1)} %get-tuple-element.19.strip, f32[4,16,128]{2,1,0:T(8,128)S(1)} %get-tuple-element.20.folds, f32[32,128]{1,0:T(8,128)S(1)} %get-tuple-element.21.wet, f32[2,25,32,128]{3,2,1,0:T(8,128)S(1)} %get-tuple-element.22.inner, ...), custom_call_target="tpu_custom_call" | custom-call | bytes 300000 | tf_op jit(solution)/shard_map/edges_and_columns/pallas_call | solution.py:722
Async XLA Ops:
  2.3 15.8 %collective-permute-start = (f32[33,16,128]{2,1,0:T(8,128)S(1)}, f32[33,16,128]{2,1,0:T(8,128)S(1)}, u32[]{:S(2)}, u32[]{:S(2)}) collective-permute-start(f32[33,16,128]{2,1,0:T(8,128)S(1)} %get-tuple-element.18), channel_id=1, source_target_pairs={{0,15},{1,14},{2,13},{3,12},{4,11},{5,10},{6,9},{7,8},{8,7},{9,6},... | collective-permute-start | bytes 811016 | tf_op jit(solution)/shard_map/ppermute | solution.py:674
  9.6 13.2 %all-to-all-start = ((f32[16,16,128]{2,1,0:T(8,128)}), f32[16,16,128]{2,1,0:T(8,128)S(1)}, u32[]{:S(2)}, u32[]{:S(2)}) async-start(f32[16,16,128]{2,1,0:T(8,128)} %regrid.1), calls=%async_computation | async-start | bytes 262144 | tf_op jit(solution)/shard_map/all_to_all | solution.py:695
  13.1 7.0 %collective-permute-start.1 = (f32[4,32,128]{2,1,0:T(8,128)S(1)}, f32[4,32,128]{2,1,0:T(8,128)S(1)}, u32[]{:S(2)}, u32[]{:S(2)}) collective-permute-start(f32[4,32,128]{2,1,0:T(8,128)S(1)} %get-tuple-element.24), channel_id=1, source_target_pairs={{0,1},{1,0},{2,3},{3,2},{4,5},{5,4},{6,7},{7,6},{8,9},{9,8},{10,11... | collective-permute-start | bytes 196616 | tf_op jit(solution)/shard_map/ppermute | solution.py:675
  13.7 6.3 %collective-permute-start.2 = (f32[4,32,128]{2,1,0:T(8,128)S(1)}, f32[4,32,128]{2,1,0:T(8,128)S(1)}, u32[]{:S(2)}, u32[]{:S(2)}) collective-permute-start(f32[4,32,128]{2,1,0:T(8,128)S(1)} %get-tuple-element.25), channel_id=1, source_target_pairs={{0,0},{1,2},{2,1},{3,4},{4,3},{5,6},{6,5},{7,8},{8,7},{9,10},{10,9... | collective-permute-start | bytes 196616 | tf_op jit(solution)/shard_map/ppermute | solution.py:676

commit v5 on v4

--- a/solution.py
+++ b/solution.py
@@ -12,7 +12,6 @@
 FLUX_GAIN = 0.5
 GROUP = 5
 PART = 13
-PIECE_ROW = ((0, 4), (8, 12))
 F32 = jnp.float32
 VMEM = pl.BlockSpec(memory_space=pltpu.VMEM)
 SMEM = pl.BlockSpec(memory_space=pltpu.SMEM)
@@ -110,14 +109,18 @@
     return [turned[0]] + [jnp.where(row == 0, p, t) for p, t in zip(turned, turned[1:])]
 
 
-def northern_rows(t_hbm, e_hbm, n_hbm, d_hbm, t, e, n, d, sems):
-    top = pl.ds(t_hbm.shape[2] - 8, 8)
-    return [
-        pltpu.make_async_copy(t_hbm.at[:, :, top], t, sems.at[0]),
-        pltpu.make_async_copy(e_hbm.at[:, top], e, sems.at[1]),
-        pltpu.make_async_copy(n_hbm.at[:, top], n, sems.at[2]),
-        pltpu.make_async_copy(d_hbm.at[top], d, sems.at[3]),
-    ]
+def shut_corner(cells, flows, west):
+    lane, row = lane_index(), row_index()
+    turn, far = (32, lane < 32) if west else (96, lane >= 96)
+    first = (row & 3) == 3
+    both = [jnp.where(first & far, rows(lanes(x, turn), 2), x) for x in (cells, flows)]
+    return jnp.where((row & 2) != 0, both[0], rows(both[1], -2))
+
+
+def open_corner(tile, west):
+    third = (row_index() & 3) == 1
+    turn = 96 if west else 32
+    return [jnp.where(third, rows(lanes(x, turn), -2), x) for x in (tile, rows(tile, 2))]
 
 
 def edge_columns(stacks):
@@ -200,8 +203,9 @@
     halves = [slice(0, 8), slice(8, 16)]
     stacks = [stack_of(out, depth, span) for span in halves]
     stacks[1].append(lambda: take(levels, turn))
-    for span, found in zip(halves, edge_columns(stacks)):
-        east[span], west[span] = found[0], found[3]
+    cells, flows = edge_columns(stacks)
+    east[...] = shut_corner(cells[0], flows[0], False)
+    west[...] = shut_corner(cells[3], flows[3], True)
     copies[4].wait()
     copies[5].wait()
 
@@ -215,16 +219,18 @@
     columns = jnp.transpose(jnp.concatenate([flat, jnp.zeros((128 - count, 128), F32)], axis=0))
     for c in range(count):
         wide[c] = jnp.broadcast_to(columns[:, c : c + 1], (128, 128))
-    row = row_index()
     me = lax.axis_index("lon")
-    message = west[...]
+
+    def send(e, tile):
+        out[3 * e + 1] = tile[0:4]
+        out[3 * e + 2] = tile[4:8]
 
     def fill(e, carry):
-        out[e] = message
+        send(e, west[...])
         return carry
 
     lax.fori_loop(0, size, fill, 0, unroll=8)
-    out[lax.rem(2 * size - 2 - me, size)] = east[...]
+    send(lax.rem(2 * size - 2 - me, size), east[...])
 
     def owner(e, carry):
         for s in range(2):
@@ -240,23 +246,36 @@
                 part[e, 2 * f + s] = sums[f]
         return carry
 
-    def letter(e, carry):
-        for f in range(2):
-            a, b = part[e, 2 * f], part[e, 2 * f + 1]
-            tile = jnp.where(row < 4, a, b) + rows(jnp.where(row < 4, b, a), 4)
-            tile = tile + rows(tile, -1)
-            tile = tile + rows(tile, -2)
-            span = slice(8 * f, 8 * f + 8)
-            out[e, span] = jnp.where((row & 3) == 0, tile, out[e, span])
+    def pair(e, carry):
+        tile = totals([part[2 * e + i // 4, i % 4] for i in range(8)])
+        out[6 * e] = tile[0:4]
+        out[6 * e + 3] = tile[4:8]
         return carry
 
     blocks_read.wait()
     lax.fori_loop(0, size, owner, 0, unroll=4)
-    lax.fori_loop(0, size, letter, 0, unroll=8)
+    lax.fori_loop(0, size // 2, pair, 0, unroll=8)
+
+
+def totals(tiles):
+    row = row_index()
+    for step in (4, 2, 1):
+        low = (row & step) == 0
+        half = len(tiles) // 2
+        merged = []
+        for a, b in zip(tiles[:half], tiles[half:]):
+            kept, moved = jnp.where(low, a, b), jnp.where(low, b, a)
+            if step == 4:
+                turned = rows(moved, 4)
+            else:
+                turned = jnp.where(low, rows(moved, -step), rows(moved, step))
+            merged.append(kept + turned)
+        tiles = merged
+    return tiles[0]
 
 
 def inner_kernel(
-    depth, t_hbm, e_hbm, n_hbm, d_hbm, mix_hbm, out, surface_wet, columns,
+    depth, t_hbm, e_hbm, n_hbm, d_hbm, mix_hbm, out, surface_wet, columns, top_t, top_e, top_n, top_d,
     t, e, n, d, mix, weights, sems, flow_sems, cell_sems,
 ):
     levels = pltpu.make_async_copy(d_hbm, d, sems.at[0])
@@ -327,6 +346,7 @@
             columns[1, k, s] = link
             above[j], ratio[j] = link, -link * inv
 
+    top_d[...] = deep[-1]
     for s, x in zip(spans, deep):
         surface_wet[s] = jnp.where(x > 0.0, 1.0, 0.0)
     for k in range(depth):
@@ -334,10 +354,14 @@
             for copy in flows[k // PART]:
                 copy.wait()
         coefficients(k)
+        top_e[k] = e[k, spans[-1]]
+        top_n[k] = n[k, spans[-1]]
     for k in range(depth):
         if k % PART == 0:
             cells[k // PART].wait()
         substep(k, 0)
+        for f in range(2):
+            top_t[f, k] = t[f, k, spans[-1]]
     mixing.wait()
     for step in range(1, SUB):
         for k in range(depth):
@@ -385,20 +409,15 @@
     return deep
 
 
-def strip_kernel(depth, t_hbm, e_hbm, n_hbm, d_hbm, fold, strip, blocks, t, e, n, d, folded, weights, over, sems):
-    band = northern_rows(t_hbm, e_hbm, n_hbm, d_hbm, t, e, n, d, sems)
-    for copy in band:
-        copy.start()
+def strip_kernel(depth, t, e, n, d, fold, strip, blocks, folded, weights, over):
     halves = [slice(0, 8), slice(8, 16)]
     stacks = [stack_of(fold, depth, span) for span in halves]
     stacks[1].append(lambda: fold_levels(fold))
     for span, found in zip(halves, edge_columns(stacks)):
         for b, tile in enumerate(found):
             blocks[b, span] = tile
-    for copy in band:
-        copy.wait()
-    row = row_index()
-    deep = d[...].astype(F32)
+    row = row_index()
+    deep = d[...]
     fold_deep = fold_levels(fold)
 
     def plus(tiles):
@@ -538,15 +557,18 @@
     targets = pltpu.make_async_copy(target_hbm, target, other.at[0])
     targets.start()
     lane, row = lane_index(), row_index()
-    size = mail.shape[0]
+    size = mail.shape[0] // 3
     rows_count = inner.shape[2]
     count = rows_count // 8
     spans = [slice(8 * j, 8 * j + 8) for j in range(count)]
     me = lax.axis_index("lon")
     even = lax.rem(me, 2) == 0
 
-    west_mail = mail[lax.rem(size - me, size)]
-    east_mail = mail[lax.rem(2 * size - 2 - me, size)]
+    def corner(sender, west):
+        place = 3 * lax.rem(sender, size)
+        return open_corner(jnp.concatenate([mail[place + 1], mail[place + 2]], axis=0), west)
+
+    west_mail, east_mail = corner(size - me, True), corner(2 * size - 2 - me, False)
     at_wrap = (me == 0) | (me == size - 1)
 
     def received(f, j, west):
@@ -568,11 +590,11 @@
         cells_near = [folds[near, 0:8], folds[far, 0:8]]
         flows_near = [folds[near, 8:16], folds[far, 8:16]]
         if west:
-            fold_cells = [letter[0:8]] + cells_near
-            fold_flows = [letter[8:16]] + flows_near
+            fold_cells = [letter[0]] + cells_near
+            fold_flows = [letter[1]] + flows_near
         else:
-            fold_cells = cells_near[::-1] + [letter[0:8]]
-            fold_flows = flows_near[::-1] + [letter[8:16]]
+            fold_cells = cells_near[::-1] + [letter[0]]
+            fold_flows = flows_near[::-1] + [letter[1]]
         sides.append(
             edge_side(depth, rows_count, [x[0:2] for x in line], [x[2:4] for x in line], fold_cells, fold_flows)
         )
@@ -594,7 +616,7 @@
             goal = target[s, a]
             hits = [row + 8 * j == goal for j in range(count)]
             for f in range(2):
-                piece = jnp.broadcast_to(mail[a, PIECE_ROW[f][s] : PIECE_ROW[f][s] + 1], (8, 128))
+                piece = jnp.broadcast_to(mail[3 * a, 2 * f + s : 2 * f + s + 1], (8, 128))
                 surface[f] = [x + jnp.where(hit, piece, 0.0) for x, hit in zip(surface[f], hits)]
 
     outer = (lane < 4) | (lane >= 124)
@@ -649,12 +671,6 @@
     depth, lat = tracers.shape[1], tracers.shape[2]
     dma = pltpu.SemaphoreType.DMA
     near = [(i, i + (1 if i % 2 else -1)) for i in range(1, size - 1)]
-    band = [
-        shape(2, depth, 8, 128),
-        shape(depth, 8, 128),
-        shape(depth, 8, 128),
-        pltpu.VMEM((8, 128), jnp.int32),
-    ]
     plane = shape(depth, lat, 128)
     block = [shape(2, depth, lat, 128), plane, plane, pltpu.VMEM((lat, 128), jnp.int32)]
     strips = shape(4, lat, 128)
@@ -663,7 +679,7 @@
     message, west_corner, east_corner, blocks, to_core, to_odd, weights, flux = call(
         functools.partial(pack_kernel, depth),
         (
-            shape(depth + lat // 4, 16, 128), shape(16, 128), shape(16, 128), shape(4, 4, lat, 128), strips, strips,
+            shape(depth + lat // 4, 16, 128), shape(8, 128), shape(8, 128), shape(4, 4, lat, 128), strips, strips,
             shape(*regrid_weights.shape[1:]), shape(*atm_flux.shape),
         ),
         [HBM] * 6,
@@ -677,7 +693,7 @@
 
     (letters,) = call(
         functools.partial(regrid_kernel, size),
-        (shape(size, 16, 128),),
+        (shape(3 * size, 4, 128),),
         [VMEM, VMEM, HBM, VMEM, VMEM],
         [
             pltpu.VMEM((2 * atm_flux.shape[1], 128, 128), F32),
@@ -694,9 +710,12 @@
     )
     mail = lax.all_to_all(letters, "lon", split_axis=0, concat_axis=0, tiled=True)
 
-    inner, wet, columns = call(
+    inner, wet, columns, *band = call(
         functools.partial(inner_kernel, depth),
-        (shape(2, depth, lat, 128), shape(lat, 128), shape(2, depth, lat, 128)),
+        (
+            shape(2, depth, lat, 128), shape(lat, 128), shape(2, depth, lat, 128),
+            shape(2, depth, 8, 128), shape(depth, 8, 128), shape(depth, 8, 128), shape(8, 128),
+        ),
         [HBM] * 5,
         [
             *block,
@@ -713,11 +732,11 @@
     strip, folds = call(
         functools.partial(strip_kernel, depth),
         (shape(2, depth, 8, 128), shape(4, 16, 128)),
-        [HBM] * 4 + [VMEM],
-        [*band, shape(depth, 8, 128), shape(5, depth, 8, 128), shape(5, depth, 8, 128), dma((4,))],
+        [VMEM] * 5,
+        [shape(depth, 8, 128), shape(5, depth, 8, 128), shape(5, depth, 8, 128)],
         cost=cost(0.1),
         name="top_strip",
-    )(*fields, *in_vmem(fold))
+    )(*in_vmem(*band, fold))
 
     (result,) = call(
         functools.partial(last_kernel, depth),

time: 25.4 us -> 24.9 us (0.980)
  Pallas kernels: 12 us -> 11.1 us
  waiting for transfers between devices: 2.68 us -> 3.06 us
    pallas_call x1, Pallas kernels: 1.93 us -> 0.93 us  [on_device(): call(functools.partial(strip_kernel, depth), (shape(2, depth, 8, 128), sh...]
    all_to_all x1, waiting for transfers between devices: 2.67 us -> 3.05 us  [on_device(): lax.all_to_all(letters, 'lon', split_axis=0, concat_axis=0, tiled=True)]
  transfers between devices with their start and end apart: 4 -> 4, of which waited for: 1 -> 1; matrix products, arithmetic and copies ran while one was open for 0% -> 0% of each run, Pallas kernels for 29% -> 26%
where the time goes in v5:
time: 24.9 us; the launch traced here: 24.5 us
  Pallas kernels  11.1 us (45%)
  starting transfers between devices  10.3 us (41%)
  waiting for transfers between devices  3.06 us (12%)
    ppermute x1, starting transfers between devices, on_device(): lax.ppermute(message, 'lon', [(i, size - 1 - i) for i in range(size)])  5.51 us
    pallas_call x1, Pallas kernels, on_device(): call(functools.partial(inner_kernel, depth), (shape(2, depth, lat, 128),...  3.71 us
    all_to_all x1, starting transfers between devices, on_device(): lax.all_to_all(letters, 'lon', split_axis=0, concat_axis=0, tiled=True)  3.52 us
    all_to_all x1, waiting for transfers between devices, on_device(): lax.all_to_all(letters, 'lon', split_axis=0, concat_axis=0, tiled=True)  3.05 us
    pallas_call x1, Pallas kernels, on_device(): call(functools.partial(pack_kernel, depth), (shape(depth + lat // 4, 16,...  2.34 us
    pallas_call x1, Pallas kernels, on_device(): call(functools.partial(last_kernel, depth), (jax.ShapeDtypeStruct((2, dep...  2.28 us
    pallas_call x1, Pallas kernels, on_device(): call(functools.partial(regrid_kernel, size), (shape(3 * size, 4, 128),),...  1.83 us
    pallas_call x1, Pallas kernels, on_device(): call(functools.partial(strip_kernel, depth), (shape(2, depth, 8, 128), sh...  0.93 us
  transfers between devices with their start and end apart: 4, of which 1 were waited for; matrix products, arithmetic and copies ran while one was open for 0% of the time, Pallas kernels for 26%

profile of v5, /device:TPU:0, one launch (start us, length us, event | category | flops | bytes accessed | tf_op | source)
XLA Modules:
  0.0 24.5 jit_solution(10655207229392753198)
XLA Ops:
  0.0 2.3 %fold_rows_and_columns.1 = (f32[33,16,128]{2,1,0:T(8,128)S(1)}, f32[8,128]{1,0:T(8,128)S(1)}, f32[8,128]{1,0:T(8,128)S(1)}, f32[4,4,32,128]{3,2,1,0:T(8,128)S(1)...) custom-call(f32[2,25,32,128]{3,2,1,0:T(8,128)} %t_hbm.3, ...), custom_call_target="tpu_custom_call" | custom-call | bytes 300000 | tf_op jit(solution)/shard_map/fold_rows_and_columns/pallas_call | solution.py:679
  2.3 5.5 %collective-permute-start = (f32[33,16,128]{2,1,0:T(8,128)S(1)}, f32[33,16,128]{2,1,0:T(8,128)S(1)}, u32[]{:S(2)}, u32[]{:S(2)}) collective-permute-start(f32[33,16,128]{2,1,0:T(8,128)S(1)} %get-tuple-element.26), channel_id=1, source_target_pairs={{0,15},{1,14},{2,13},{3,12},{4,11},{5,10},{6,9},{7,8},{8,7},{9,6},... | collective-permute-start | bytes 811016 | tf_op jit(solution)/shard_map/ppermute | solution.py:690
  7.9 1.8 %regrid.1 = f32[48,4,128]{2,1,0:T(4,128)} custom-call(f32[2,8,128]{2,1,0:T(8,128)S(1)} %get-tuple-element.34.atm, f32[16,2,128,128]{3,2,1,0:T(8,128)S(1)} %get-tuple-element.35.w, s32[2,16]{1,0:T(2,128)} %bitcast.7, f32[8,128]{1,0:T(8,128)S(1)} %get-tuple-element.36.west, f32[8,128]{1,0:T(8,128)S(1)} %get-tuple-element.37.east), custom_call_target="tpu_custom_call" | custom-call | bytes 300000 | tf_op jit(solution)/shard_map/regrid/pallas_call | solution.py:694
  9.7 3.5 %all-to-all-start = ((f32[48,4,128]{2,1,0:T(4,128)}), f32[48,4,128]{2,1,0:T(4,128)S(1)}, u32[]{:S(2)}, u32[]{:S(2)}) async-start(f32[48,4,128]{2,1,0:T(4,128)} %regrid.1), calls=%async_computation | async-start | bytes 196608 | tf_op jit(solution)/shard_map/all_to_all | solution.py:711
  13.2 0.6 %collective-permute-start.1 = (f32[4,32,128]{2,1,0:T(8,128)S(1)}, f32[4,32,128]{2,1,0:T(8,128)S(1)}, u32[]{:S(2)}, u32[]{:S(2)}) collective-permute-start(f32[4,32,128]{2,1,0:T(8,128)S(1)} %get-tuple-element.32), channel_id=1, source_target_pairs={{0,1},{1,0},{2,3},{3,2},{4,5},{5,4},{6,7},{7,6},{8,9},{9,8},{10,11... | collective-permute-start | bytes 196616 | tf_op jit(solution)/shard_map/ppermute | solution.py:691
  13.9 0.7 %collective-permute-start.2 = (f32[4,32,128]{2,1,0:T(8,128)S(1)}, f32[4,32,128]{2,1,0:T(8,128)S(1)}, u32[]{:S(2)}, u32[]{:S(2)}) collective-permute-start(f32[4,32,128]{2,1,0:T(8,128)S(1)} %get-tuple-element.33), channel_id=1, source_target_pairs={{0,0},{1,2},{2,1},{3,4},{4,3},{5,6},{6,5},{7,8},{8,7},{9,10},{10,9... | collective-permute-start | bytes 196616 | tf_op jit(solution)/shard_map/ppermute | solution.py:692
  14.5 3.7 %inner_cells.1 = (f32[2,25,32,128]{3,2,1,0:T(8,128)S(1)}, f32[32,128]{1,0:T(8,128)S(1)}, f32[2,25,32,128]{3,2,1,0:T(8,128)S(1)}, f32[2,25,8,128]{3,2,1,0:T(8,128...) custom-call(f32[2,25,32,128]{3,2,1,0:T(8,128)} %t_hbm.3, f32[25,32,128]{2,1,0:T(8,128)} %e_hbm.3, ...), custom_call_target="tpu_custom_call" | custom-call | bytes 300000 | tf_op jit(solution)/shard_map/inner_cells/pallas_call | solution.py:713
  18.2 0.0 collective-permute-done.fold
  18.3 0.9 %top_strip.1 = (f32[2,25,8,128]{3,2,1,0:T(8,128)S(1)}, f32[4,16,128]{2,1,0:T(8,128)S(1)}) custom-call(f32[2,25,8,128]{3,2,1,0:T(8,128)S(1)} %get-tuple-element.22.t, f32[25,8,128]{2,1,0:T(8,128)S(1)} %get-tuple-element.23.e, f32[25,8,128]{2,1,0:T(8,128)S(1)} %get-tuple-element.24.n, f32[8,128]{1,0:T(8,128)S(1)} %get-tuple-element.25.d, ...), custom_call_target="tpu_custom_call" | custom-call | bytes 300000 | tf_op jit(solution)/shard_map/top_strip/pallas_call | solution.py:732
  19.2 0.0 collective-permute-done.1.core
  19.2 0.0 collective-permute-done.2.odd
  19.2 3.1 %all-to-all-done.mail = f32[48,4,128]{2,1,0:T(4,128)S(1)} async-done(((f32[48,4,128]{2,1,0:T(4,128)}), f32[48,4,128]{2,1,0:T(4,128)S(1)}, u32[]{:S(2)}, u32[]{:S(2)}) %all-to-all-start) | async-done | bytes 98336 | tf_op jit(solution)/shard_map/all_to_all | solution.py:711
  22.3 2.3 %edges_and_columns.1 = f32[2,25,32,128]{3,2,1,0:T(8,128)} custom-call(f32[2,25,8,128]{3,2,1,0:T(8,128)S(1)} %get-tuple-element.27.strip, f32[4,16,128]{2,1,0:T(8,128)S(1)} %get-tuple-element.28.folds, f32[32,128]{1,0:T(8,128)S(1)} %get-tuple-element.29.wet, f32[2,25,32,128]{3,2,1,0:T(8,128)S(1)} %get-tuple-element.30.inner, ...), custom_call_target="tpu_custom_call" | custom-call | bytes 300000 | tf_op jit(solution)/shard_map/edges_and_columns/pallas_call | solution.py:741
Async XLA Ops:
  2.3 15.9 %collective-permute-start = (f32[33,16,128]{2,1,0:T(8,128)S(1)}, f32[33,16,128]{2,1,0:T(8,128)S(1)}, u32[]{:S(2)}, u32[]{:S(2)}) collective-permute-start(f32[33,16,128]{2,1,0:T(8,128)S(1)} %get-tuple-element.26), channel_id=1, source_target_pairs={{0,15},{1,14},{2,13},{3,12},{4,11},{5,10},{6,9},{7,8},{8,7},{9,6},... | collective-permute-start | bytes 811016 | tf_op jit(solution)/shard_map/ppermute | solution.py:690
  9.7 12.6 %all-to-all-start = ((f32[48,4,128]{2,1,0:T(4,128)}), f32[48,4,128]{2,1,0:T(4,128)S(1)}, u32[]{:S(2)}, u32[]{:S(2)}) async-start(f32[48,4,128]{2,1,0:T(4,128)} %regrid.1), calls=%async_computation | async-start | bytes 196608 | tf_op jit(solution)/shard_map/all_to_all | solution.py:711
  13.2 6.0 %collective-permute-start.1 = (f32[4,32,128]{2,1,0:T(8,128)S(1)}, f32[4,32,128]{2,1,0:T(8,128)S(1)}, u32[]{:S(2)}, u32[]{:S(2)}) collective-permute-start(f32[4,32,128]{2,1,0:T(8,128)S(1)} %get-tuple-element.32), channel_id=1, source_target_pairs={{0,1},{1,0},{2,3},{3,2},{4,5},{5,4},{6,7},{7,6},{8,9},{9,8},{10,11... | collective-permute-start | bytes 196616 | tf_op jit(solution)/shard_map/ppermute | solution.py:691
  13.9 5.3 %collective-permute-start.2 = (f32[4,32,128]{2,1,0:T(8,128)S(1)}, f32[4,32,128]{2,1,0:T(8,128)S(1)}, u32[]{:S(2)}, u32[]{:S(2)}) collective-permute-start(f32[4,32,128]{2,1,0:T(8,128)S(1)} %get-tuple-element.33), channel_id=1, source_target_pairs={{0,0},{1,2},{2,1},{3,4},{4,3},{5,6},{6,5},{7,8},{8,7},{9,10},{10,9... | collective-permute-start | bytes 196616 | tf_op jit(solution)/shard_map/ppermute | solution.py:692

commit v6 on v5

--- a/solution.py
+++ b/solution.py
@@ -11,7 +11,7 @@
 DIFFUSION = 0.12
 FLUX_GAIN = 0.5
 GROUP = 5
-PART = 13
+PART = 25
 F32 = jnp.float32
 VMEM = pl.BlockSpec(memory_space=pltpu.VMEM)
 SMEM = pl.BlockSpec(memory_space=pltpu.SMEM)
@@ -183,8 +183,13 @@
             w1, e1 = found[0], found[3]
             to_core[f, spans[j]] = jnp.where(even, e1, w1)
             to_odd[f, spans[j]] = jnp.where(even, w1, e1)
+            wrapped = jnp.where(me == 0, w1, e1)
             place = f * count + j
-            out[depth + place // 2, 8 * (place % 2) : 8 * (place % 2) + 8] = jnp.where(me == 0, w1, e1)
+            if place < 4 * count - 2:
+                out[depth + place // 2, 8 * (place % 2) : 8 * (place % 2) + 8] = wrapped
+            else:
+                for r in range(8):
+                    out[4 + 8 * (place - 4 * count + 2) + r, 12:13] = wrapped[r : r + 1]
 
     copies[0].wait()
     copies[1].wait()
@@ -573,7 +578,13 @@
 
     def received(f, j, west):
         place = f * count + j
-        wrapped = fold[depth + place // 2, 8 * (place % 2) : 8 * (place % 2) + 8]
+        if place < 4 * count - 2:
+            wrapped = fold[depth + place // 2, 8 * (place % 2) : 8 * (place % 2) + 8]
+        else:
+            wrapped = jnp.zeros((8, 128), F32)
+            for r in range(8):
+                line = fold[4 + 8 * (place - 4 * count + 2) + r, 12:13]
+                wrapped = jnp.where(row == r, jnp.broadcast_to(line, (8, 128)), wrapped)
         a, b = core[f, spans[j]], jnp.where(at_wrap, wrapped, odd[f, spans[j]])
         return jnp.where(even, b, a) if west else jnp.where(even, a, b)
 
@@ -679,7 +690,7 @@
     message, west_corner, east_corner, blocks, to_core, to_odd, weights, flux = call(
         functools.partial(pack_kernel, depth),
         (
-            shape(depth + lat // 4, 16, 128), shape(8, 128), shape(8, 128), shape(4, 4, lat, 128), strips, strips,
+            shape(depth + lat // 4 - 1, 16, 128), shape(8, 128), shape(8, 128), shape(4, 4, lat, 128), strips, strips,
             shape(*regrid_weights.shape[1:]), shape(*atm_flux.shape),
         ),
         [HBM] * 6,

time: 24.9 us -> 24.6 us (0.988)
  Pallas kernels: 11.1 us -> 10.7 us
  transfers between devices with their start and end apart: 4 -> 4, of which waited for: 1 -> 1; matrix products, arithmetic and copies ran while one was open for 0% -> 0% of each run, Pallas kernels for 26% -> 25%
where the time goes in v6:
time: 24.6 us; the launch traced here: 24.2 us
  Pallas kernels  10.7 us (43%)
  starting transfers between devices  10.3 us (42%)
  waiting for transfers between devices  3.09 us (13%)
    ppermute x1, starting transfers between devices, on_device(): lax.ppermute(message, 'lon', [(i, size - 1 - i) for i in range(size)])  5.51 us
    all_to_all x1, starting transfers between devices, on_device(): lax.all_to_all(letters, 'lon', split_axis=0, concat_axis=0, tiled=True)  3.52 us
    pallas_call x1, Pallas kernels, on_device(): call(functools.partial(inner_kernel, depth), (shape(2, depth, lat, 128),...  3.5 us
    all_to_all x1, waiting for transfers between devices, on_device(): lax.all_to_all(letters, 'lon', split_axis=0, concat_axis=0, tiled=True)  3.08 us
    pallas_call x1, Pallas kernels, on_device(): call(functools.partial(pack_kernel, depth), (shape(depth + lat // 4 - 1,...  2.42 us
    pallas_call x1, Pallas kernels, on_device(): call(functools.partial(last_kernel, depth), (jax.ShapeDtypeStruct((2, dep...  2.22 us
    pallas_call x1, Pallas kernels, on_device(): call(functools.partial(regrid_kernel, size), (shape(3 * size, 4, 128),),...  1.7 us
    pallas_call x1, Pallas kernels, on_device(): call(functools.partial(strip_kernel, depth), (shape(2, depth, 8, 128), sh...  0.9 us
  transfers between devices with their start and end apart: 4, of which 1 were waited for; matrix products, arithmetic and copies ran while one was open for 0% of the time, Pallas kernels for 25%

profile of v6, /device:TPU:0, one launch (start us, length us, event | category | flops | bytes accessed | tf_op | source)
XLA Modules:
  0.0 24.2 jit_solution(14472422294499929096)
XLA Ops:
  0.0 2.4 %fold_rows_and_columns.1 = (f32[32,16,128]{2,1,0:T(8,128)S(1)}, f32[8,128]{1,0:T(8,128)S(1)}, f32[8,128]{1,0:T(8,128)S(1)}, f32[4,4,32,128]{3,2,1,0:T(8,128)S(1)...) custom-call(f32[2,25,32,128]{3,2,1,0:T(8,128)} %t_hbm.3, ...), custom_call_target="tpu_custom_call" | custom-call | bytes 300000 | tf_op jit(solution)/shard_map/fold_rows_and_columns/pallas_call | solution.py:690
  2.4 5.5 %collective-permute-start = (f32[32,16,128]{2,1,0:T(8,128)S(1)}, f32[32,16,128]{2,1,0:T(8,128)S(1)}, u32[]{:S(2)}, u32[]{:S(2)}) collective-permute-start(f32[32,16,128]{2,1,0:T(8,128)S(1)} %get-tuple-element.26), channel_id=1, source_target_pairs={{0,15},{1,14},{2,13},{3,12},{4,11},{5,10},{6,9},{7,8},{8,7},{9,6},... | collective-permute-start | bytes 786440 | tf_op jit(solution)/shard_map/ppermute | solution.py:701
  7.9 1.7 %regrid.1 = f32[48,4,128]{2,1,0:T(4,128)} custom-call(f32[2,8,128]{2,1,0:T(8,128)S(1)} %get-tuple-element.34.atm, f32[16,2,128,128]{3,2,1,0:T(8,128)S(1)} %get-tuple-element.35.w, s32[2,16]{1,0:T(2,128)} %bitcast.7, f32[8,128]{1,0:T(8,128)S(1)} %get-tuple-element.36.west, f32[8,128]{1,0:T(8,128)S(1)} %get-tuple-element.37.east), custom_call_target="tpu_custom_call" | custom-call | bytes 300000 | tf_op jit(solution)/shard_map/regrid/pallas_call | solution.py:705
  9.6 3.5 %all-to-all-start = ((f32[48,4,128]{2,1,0:T(4,128)}), f32[48,4,128]{2,1,0:T(4,128)S(1)}, u32[]{:S(2)}, u32[]{:S(2)}) async-start(f32[48,4,128]{2,1,0:T(4,128)} %regrid.1), calls=%async_computation | async-start | bytes 196608 | tf_op jit(solution)/shard_map/all_to_all | solution.py:722
  13.2 0.6 %collective-permute-start.1 = (f32[4,32,128]{2,1,0:T(8,128)S(1)}, f32[4,32,128]{2,1,0:T(8,128)S(1)}, u32[]{:S(2)}, u32[]{:S(2)}) collective-permute-start(f32[4,32,128]{2,1,0:T(8,128)S(1)} %get-tuple-element.32), channel_id=1, source_target_pairs={{0,1},{1,0},{2,3},{3,2},{4,5},{5,4},{6,7},{7,6},{8,9},{9,8},{10,11... | collective-permute-start | bytes 196616 | tf_op jit(solution)/shard_map/ppermute | solution.py:702
  13.8 0.7 %collective-permute-start.2 = (f32[4,32,128]{2,1,0:T(8,128)S(1)}, f32[4,32,128]{2,1,0:T(8,128)S(1)}, u32[]{:S(2)}, u32[]{:S(2)}) collective-permute-start(f32[4,32,128]{2,1,0:T(8,128)S(1)} %get-tuple-element.33), channel_id=1, source_target_pairs={{0,0},{1,2},{2,1},{3,4},{4,3},{5,6},{6,5},{7,8},{8,7},{9,10},{10,9... | collective-permute-start | bytes 196616 | tf_op jit(solution)/shard_map/ppermute | solution.py:703
  14.5 3.5 %inner_cells.1 = (f32[2,25,32,128]{3,2,1,0:T(8,128)S(1)}, f32[32,128]{1,0:T(8,128)S(1)}, f32[2,25,32,128]{3,2,1,0:T(8,128)S(1)}, f32[2,25,8,128]{3,2,1,0:T(8,128...) custom-call(f32[2,25,32,128]{3,2,1,0:T(8,128)} %t_hbm.3, f32[25,32,128]{2,1,0:T(8,128)} %e_hbm.3, ...), custom_call_target="tpu_custom_call" | custom-call | bytes 300000 | tf_op jit(solution)/shard_map/inner_cells/pallas_call | solution.py:724
  18.0 0.0 collective-permute-done.fold
  18.0 0.9 %top_strip.1 = (f32[2,25,8,128]{3,2,1,0:T(8,128)S(1)}, f32[4,16,128]{2,1,0:T(8,128)S(1)}) custom-call(f32[2,25,8,128]{3,2,1,0:T(8,128)S(1)} %get-tuple-element.22.t, f32[25,8,128]{2,1,0:T(8,128)S(1)} %get-tuple-element.23.e, f32[25,8,128]{2,1,0:T(8,128)S(1)} %get-tuple-element.24.n, f32[8,128]{1,0:T(8,128)S(1)} %get-tuple-element.25.d, ...), custom_call_target="tpu_custom_call" | custom-call | bytes 300000 | tf_op jit(solution)/shard_map/top_strip/pallas_call | solution.py:743
  18.9 0.0 collective-permute-done.1.core
  18.9 0.0 collective-permute-done.2.odd
  18.9 3.1 %all-to-all-done.mail = f32[48,4,128]{2,1,0:T(4,128)S(1)} async-done(((f32[48,4,128]{2,1,0:T(4,128)}), f32[48,4,128]{2,1,0:T(4,128)S(1)}, u32[]{:S(2)}, u32[]{:S(2)}) %all-to-all-start) | async-done | bytes 98336 | tf_op jit(solution)/shard_map/all_to_all | solution.py:722
  22.0 2.2 %edges_and_columns.1 = f32[2,25,32,128]{3,2,1,0:T(8,128)} custom-call(f32[2,25,8,128]{3,2,1,0:T(8,128)S(1)} %get-tuple-element.27.strip, f32[4,16,128]{2,1,0:T(8,128)S(1)} %get-tuple-element.28.folds, f32[32,128]{1,0:T(8,128)S(1)} %get-tuple-element.29.wet, f32[2,25,32,128]{3,2,1,0:T(8,128)S(1)} %get-tuple-element.30.inner, ...), custom_call_target="tpu_custom_call" | custom-call | bytes 300000 | tf_op jit(solution)/shard_map/edges_and_columns/pallas_call | solution.py:752
Async XLA Ops:
  2.4 15.6 %collective-permute-start = (f32[32,16,128]{2,1,0:T(8,128)S(1)}, f32[32,16,128]{2,1,0:T(8,128)S(1)}, u32[]{:S(2)}, u32[]{:S(2)}) collective-permute-start(f32[32,16,128]{2,1,0:T(8,128)S(1)} %get-tuple-element.26), channel_id=1, source_target_pairs={{0,15},{1,14},{2,13},{3,12},{4,11},{5,10},{6,9},{7,8},{8,7},{9,6},... | collective-permute-start | bytes 786440 | tf_op jit(solution)/shard_map/ppermute | solution.py:701
  9.6 12.4 %all-to-all-start = ((f32[48,4,128]{2,1,0:T(4,128)}), f32[48,4,128]{2,1,0:T(4,128)S(1)}, u32[]{:S(2)}, u32[]{:S(2)}) async-start(f32[48,4,128]{2,1,0:T(4,128)} %regrid.1), calls=%async_computation | async-start | bytes 196608 | tf_op jit(solution)/shard_map/all_to_all | solution.py:722
  13.2 5.7 %collective-permute-start.1 = (f32[4,32,128]{2,1,0:T(8,128)S(1)}, f32[4,32,128]{2,1,0:T(8,128)S(1)}, u32[]{:S(2)}, u32[]{:S(2)}) collective-permute-start(f32[4,32,128]{2,1,0:T(8,128)S(1)} %get-tuple-element.32), channel_id=1, source_target_pairs={{0,1},{1,0},{2,3},{3,2},{4,5},{5,4},{6,7},{7,6},{8,9},{9,8},{10,11... | collective-permute-start | bytes 196616 | tf_op jit(solution)/shard_map/ppermute | solution.py:702
  13.8 5.1 %collective-permute-start.2 = (f32[4,32,128]{2,1,0:T(8,128)S(1)}, f32[4,32,128]{2,1,0:T(8,128)S(1)}, u32[]{:S(2)}, u32[]{:S(2)}) collective-permute-start(f32[4,32,128]{2,1,0:T(8,128)S(1)} %get-tuple-element.33), channel_id=1, source_target_pairs={{0,0},{1,2},{2,1},{3,4},{4,3},{5,6},{6,5},{7,8},{8,7},{9,10},{10,9... | collective-permute-start | bytes 196616 | tf_op jit(solution)/shard_map/ppermute | solution.py:703

commit v7 on v6

--- a/solution.py
+++ b/solution.py
@@ -150,7 +150,7 @@
 
 
 def pack_kernel(
-    depth, t_hbm, e_hbm, n_hbm, d_hbm, w_hbm, atm_hbm, out, west, east, blocks, to_core, to_odd, w, atm,
+    depth, t_hbm, e_hbm, n_hbm, d_hbm, w_hbm, atm_hbm, out, blocks, to_core, to_odd, w, atm,
     t, e, n, d, sems,
 ):
     copies = [
@@ -205,17 +205,11 @@
         out[k, 0:8] = take(cells, turn)
         out[k, 8:16] = take(flows, turn)
     columns((2, 3))
-    halves = [slice(0, 8), slice(8, 16)]
-    stacks = [stack_of(out, depth, span) for span in halves]
-    stacks[1].append(lambda: take(levels, turn))
-    cells, flows = edge_columns(stacks)
-    east[...] = shut_corner(cells[0], flows[0], False)
-    west[...] = shut_corner(cells[3], flows[3], True)
     copies[4].wait()
     copies[5].wait()
 
 
-def regrid_kernel(size, atm, w, src_hbm, west, east, out, wide, part, src, sems):
+def regrid_kernel(depth, size, atm, w, src_hbm, fold, out, wide, part, src, sems):
     blocks_read = pltpu.make_async_copy(src_hbm, src, sems.at[0])
     blocks_read.start()
     flat = atm[...].reshape(atm.shape[0] * atm.shape[1], atm.shape[2])
@@ -226,16 +220,23 @@
         wide[c] = jnp.broadcast_to(columns[:, c : c + 1], (128, 128))
     me = lax.axis_index("lon")
 
+    halves = [slice(0, 8), slice(8, 16)]
+    stacks = [stack_of(fold, depth, span) for span in halves]
+    stacks[1].append(lambda: fold_levels(fold))
+    cells, flows = edge_columns(stacks)
+    east = shut_corner(cells[0], flows[0], False)
+    west = shut_corner(cells[3], flows[3], True)
+
     def send(e, tile):
         out[3 * e + 1] = tile[0:4]
         out[3 * e + 2] = tile[4:8]
 
     def fill(e, carry):
-        send(e, west[...])
+        send(e, west)
         return carry
 
     lax.fori_loop(0, size, fill, 0, unroll=8)
-    send(lax.rem(2 * size - 2 - me, size), east[...])
+    send(lax.rem(2 * size - 2 - me, size), east)
 
     def owner(e, carry):
         for s in range(2):
@@ -687,10 +688,10 @@
     strips = shape(4, lat, 128)
     fields = in_hbm(tracers, east_flow, north_flow, depth_levels)
 
-    message, west_corner, east_corner, blocks, to_core, to_odd, weights, flux = call(
+    message, blocks, to_core, to_odd, weights, flux = call(
         functools.partial(pack_kernel, depth),
         (
-            shape(depth + lat // 4 - 1, 16, 128), shape(8, 128), shape(8, 128), shape(4, 4, lat, 128), strips, strips,
+            shape(depth + lat // 4 - 1, 16, 128), shape(4, 4, lat, 128), strips, strips,
             shape(*regrid_weights.shape[1:]), shape(*atm_flux.shape),
         ),
         [HBM] * 6,
@@ -703,9 +704,9 @@
     odd = lax.ppermute(to_odd, "lon", [(0, 0), *near, (size - 1, size - 1)])
 
     (letters,) = call(
-        functools.partial(regrid_kernel, size),
+        functools.partial(regrid_kernel, depth, size),
         (shape(3 * size, 4, 128),),
-        [VMEM, VMEM, HBM, VMEM, VMEM],
+        [VMEM, VMEM, HBM, VMEM],
         [
             pltpu.VMEM((2 * atm_flux.shape[1], 128, 128), F32),
             pltpu.VMEM((size, 4, 8, 128), F32),
@@ -717,7 +718,7 @@
     )(
         *in_vmem(flux, weights),
         *in_hbm(jnp.transpose(source_blocks[0])),
-        *in_vmem(west_corner, east_corner),
+        *in_vmem(message),
     )
     mail = lax.all_to_all(letters, "lon", split_axis=0, concat_axis=0, tiled=True)
 

time: 24.6 us -> 24.4 us (level)
  waiting for transfers between devices: 3.09 us -> 2.56 us
  Pallas kernels: 10.7 us -> 11 us
    all_to_all x1, waiting for transfers between devices: 3.08 us -> 2.55 us  [on_device(): lax.all_to_all(letters, 'lon', split_axis=0, concat_axis=0, tiled=True)]
    pallas_call x1, Pallas kernels: 1.7 us -> 2.23 us  [on_device(): call(functools.partial(regrid_kernel, depth, size), (shape(3 * size, 4, 1...]
  transfers between devices with their start and end apart: 4 -> 4, of which waited for: 1 -> 1; matrix products, arithmetic and copies ran while one was open for 0% -> 0% of each run, Pallas kernels for 25% -> 28%
where the time goes in v7:
time: 24.4 us; the launch traced here: 24 us
  Pallas kernels  11 us (45%)
  starting transfers between devices  10.3 us (42%)
  waiting for transfers between devices  2.56 us (10%)
    ppermute x1, starting transfers between devices, on_device(): lax.ppermute(message, 'lon', [(i, size - 1 - i) for i in range(size)])  5.51 us
    all_to_all x1, starting transfers between devices, on_device(): lax.all_to_all(letters, 'lon', split_axis=0, concat_axis=0, tiled=True)  3.52 us
    pallas_call x1, Pallas kernels, on_device(): call(functools.partial(inner_kernel, depth), (shape(2, depth, lat, 128),...  3.5 us
    all_to_all x1, waiting for transfers between devices, on_device(): lax.all_to_all(letters, 'lon', split_axis=0, concat_axis=0, tiled=True)  2.55 us
    pallas_call x1, Pallas kernels, on_device(): call(functools.partial(regrid_kernel, depth, size), (shape(3 * size, 4, 1...  2.23 us
    pallas_call x1, Pallas kernels, on_device(): call(functools.partial(last_kernel, depth), (jax.ShapeDtypeStruct((2, dep...  2.22 us
    pallas_call x1, Pallas kernels, on_device(): call(functools.partial(pack_kernel, depth), (shape(depth + lat // 4 - 1,...  2.18 us
    pallas_call x1, Pallas kernels, on_device(): call(functools.partial(strip_kernel, depth), (shape(2, depth, 8, 128), sh...  0.9 us
  transfers between devices with their start and end apart: 4, of which 1 were waited for; matrix products, arithmetic and copies ran while one was open for 0% of the time, Pallas kernels for 28%

profile of v7, /device:TPU:0, one launch (start us, length us, event | category | flops | bytes accessed | tf_op | source)
XLA Modules:
  0.0 24.0 jit_solution(6339999363155146494)
XLA Ops:
  0.0 2.2 %fold_rows_and_columns.1 = (f32[32,16,128]{2,1,0:T(8,128)S(1)}, f32[4,4,32,128]{3,2,1,0:T(8,128)S(1)}, f32[4,32,128]{2,1,0:T(8,128)S(1)}, f32[4,32,128]{2,1,0:T(...) custom-call(f32[2,25,32,128]{3,2,1,0:T(8,128)} %t_hbm.3, f32[25,32,128]{2,1,0:T(8,128)} %e_hbm.3, ...), custom_call_target="tpu_custom_call" | custom-call | bytes 300000 | tf_op jit(solution)/shard_map/fold_rows_and_columns/pallas_call | solution.py:691
  2.2 5.5 %collective-permute-start = (f32[32,16,128]{2,1,0:T(8,128)S(1)}, f32[32,16,128]{2,1,0:T(8,128)S(1)}, u32[]{:S(2)}, u32[]{:S(2)}) collective-permute-start(f32[32,16,128]{2,1,0:T(8,128)S(1)} %get-tuple-element.24.fold), channel_id=1, source_target_pairs={{0,15},{1,14},{2,13},{3,12},{4,11},{5,10},{6,9},{7,8},{8,7},{9,6},... | collective-permute-start | bytes 786440 | tf_op jit(solution)/shard_map/ppermute | solution.py:702
  7.7 2.2 %regrid.1 = f32[48,4,128]{2,1,0:T(4,128)} custom-call(f32[2,8,128]{2,1,0:T(8,128)S(1)} %get-tuple-element.32.atm, f32[16,2,128,128]{3,2,1,0:T(8,128)S(1)} %get-tuple-element.33.w, s32[2,16]{1,0:T(2,128)} %bitcast.7, f32[32,16,128]{2,1,0:T(8,128)S(1)} %get-tuple-element.24.fold), custom_call_target="tpu_custom_call" | custom-call | bytes 300000 | tf_op jit(solution)/shard_map/regrid/pallas_call | solution.py:706
  9.9 3.5 %all-to-all-start = ((f32[48,4,128]{2,1,0:T(4,128)}), f32[48,4,128]{2,1,0:T(4,128)S(1)}, u32[]{:S(2)}, u32[]{:S(2)}) async-start(f32[48,4,128]{2,1,0:T(4,128)} %regrid.1), calls=%async_computation | async-start | bytes 196608 | tf_op jit(solution)/shard_map/all_to_all | solution.py:723
  13.5 0.6 %collective-permute-start.1 = (f32[4,32,128]{2,1,0:T(8,128)S(1)}, f32[4,32,128]{2,1,0:T(8,128)S(1)}, u32[]{:S(2)}, u32[]{:S(2)}) collective-permute-start(f32[4,32,128]{2,1,0:T(8,128)S(1)} %get-tuple-element.30), channel_id=1, source_target_pairs={{0,1},{1,0},{2,3},{3,2},{4,5},{5,4},{6,7},{7,6},{8,9},{9,8},{10,11... | collective-permute-start | bytes 196616 | tf_op jit(solution)/shard_map/ppermute | solution.py:703
  14.1 0.7 %collective-permute-start.2 = (f32[4,32,128]{2,1,0:T(8,128)S(1)}, f32[4,32,128]{2,1,0:T(8,128)S(1)}, u32[]{:S(2)}, u32[]{:S(2)}) collective-permute-start(f32[4,32,128]{2,1,0:T(8,128)S(1)} %get-tuple-element.31), channel_id=1, source_target_pairs={{0,0},{1,2},{2,1},{3,4},{4,3},{5,6},{6,5},{7,8},{8,7},{9,10},{10,9... | collective-permute-start | bytes 196616 | tf_op jit(solution)/shard_map/ppermute | solution.py:704
  14.8 3.5 %inner_cells.1 = (f32[2,25,32,128]{3,2,1,0:T(8,128)S(1)}, f32[32,128]{1,0:T(8,128)S(1)}, f32[2,25,32,128]{3,2,1,0:T(8,128)S(1)}, f32[2,25,8,128]{3,2,1,0:T(8,128...) custom-call(f32[2,25,32,128]{3,2,1,0:T(8,128)} %t_hbm.3, f32[25,32,128]{2,1,0:T(8,128)} %e_hbm.3, ...), custom_call_target="tpu_custom_call" | custom-call | bytes 300000 | tf_op jit(solution)/shard_map/inner_cells/pallas_call | solution.py:725
  18.3 0.0 collective-permute-done.fold
  18.3 0.9 %top_strip.1 = (f32[2,25,8,128]{3,2,1,0:T(8,128)S(1)}, f32[4,16,128]{2,1,0:T(8,128)S(1)}) custom-call(f32[2,25,8,128]{3,2,1,0:T(8,128)S(1)} %get-tuple-element.20.t, f32[25,8,128]{2,1,0:T(8,128)S(1)} %get-tuple-element.21.e, f32[25,8,128]{2,1,0:T(8,128)S(1)} %get-tuple-element.22.n, f32[8,128]{1,0:T(8,128)S(1)} %get-tuple-element.23.d, ...), custom_call_target="tpu_custom_call" | custom-call | bytes 300000 | tf_op jit(solution)/shard_map/top_strip/pallas_call | solution.py:744
  19.2 0.0 collective-permute-done.1.core
  19.2 0.0 collective-permute-done.2.odd
  19.2 2.5 %all-to-all-done.mail = f32[48,4,128]{2,1,0:T(4,128)S(1)} async-done(((f32[48,4,128]{2,1,0:T(4,128)}), f32[48,4,128]{2,1,0:T(4,128)S(1)}, u32[]{:S(2)}, u32[]{:S(2)}) %all-to-all-start) | async-done | bytes 98336 | tf_op jit(solution)/shard_map/all_to_all | solution.py:723
  21.8 2.2 %edges_and_columns.1 = f32[2,25,32,128]{3,2,1,0:T(8,128)} custom-call(f32[2,25,8,128]{3,2,1,0:T(8,128)S(1)} %get-tuple-element.25.strip, f32[4,16,128]{2,1,0:T(8,128)S(1)} %get-tuple-element.26.folds, f32[32,128]{1,0:T(8,128)S(1)} %get-tuple-element.27.wet, f32[2,25,32,128]{3,2,1,0:T(8,128)S(1)} %get-tuple-element.28.inner, ...), custom_call_target="tpu_custom_call" | custom-call | bytes 300000 | tf_op jit(solution)/shard_map/edges_and_columns/pallas_call | solution.py:753
Async XLA Ops:
  2.2 16.1 %collective-permute-start = (f32[32,16,128]{2,1,0:T(8,128)S(1)}, f32[32,16,128]{2,1,0:T(8,128)S(1)}, u32[]{:S(2)}, u32[]{:S(2)}) collective-permute-start(f32[32,16,128]{2,1,0:T(8,128)S(1)} %get-tuple-element.24.fold), channel_id=1, source_target_pairs={{0,15},{1,14},{2,13},{3,12},{4,11},{5,10},{6,9},{7,8},{8,7},{9,6},... | collective-permute-start | bytes 786440 | tf_op jit(solution)/shard_map/ppermute | solution.py:702
  9.9 11.8 %all-to-all-start = ((f32[48,4,128]{2,1,0:T(4,128)}), f32[48,4,128]{2,1,0:T(4,128)S(1)}, u32[]{:S(2)}, u32[]{:S(2)}) async-start(f32[48,4,128]{2,1,0:T(4,128)} %regrid.1), calls=%async_computation | async-start | bytes 196608 | tf_op jit(solution)/shard_map/all_to_all | solution.py:723
  13.5 5.7 %collective-permute-start.1 = (f32[4,32,128]{2,1,0:T(8,128)S(1)}, f32[4,32,128]{2,1,0:T(8,128)S(1)}, u32[]{:S(2)}, u32[]{:S(2)}) collective-permute-start(f32[4,32,128]{2,1,0:T(8,128)S(1)} %get-tuple-element.30), channel_id=1, source_target_pairs={{0,1},{1,0},{2,3},{3,2},{4,5},{5,4},{6,7},{7,6},{8,9},{9,8},{10,11... | collective-permute-start | bytes 196616 | tf_op jit(solution)/shard_map/ppermute | solution.py:703
  14.1 5.1 %collective-permute-start.2 = (f32[4,32,128]{2,1,0:T(8,128)S(1)}, f32[4,32,128]{2,1,0:T(8,128)S(1)}, u32[]{:S(2)}, u32[]{:S(2)}) collective-permute-start(f32[4,32,128]{2,1,0:T(8,128)S(1)} %get-tuple-element.31), channel_id=1, source_target_pairs={{0,0},{1,2},{2,1},{3,4},{4,3},{5,6},{6,5},{7,8},{8,7},{9,10},{10,9... | collective-permute-start | bytes 196616 | tf_op jit(solution)/shard_map/ppermute | solution.py:704
